TPU v7x, 512 devices: a whole 4x8x8 slice. The times are simulated.
512 devices in a mesh: gx: 16 (over y, z_lo), gy: 32 (over x, z_hi, core).
Axes of the slice: x: 4, y: 8, z: 8 (z_hi: 4, z_lo: 2; z = z_hi * 2 + z_lo), core: 2. Of those that a mesh axis runs over, the one named last changes fastest.
Arguments:
- features: float32 [32, 64, 128, 512], P('gx', 'gy'), may hold values from -6 to 6
- tile_filter: float32 [32, 64, 9, 128, 128], P('gx', 'gy'), may hold values from -0.17677669 to 0.17677669
- positions: float32 [3, 32, 64, 128], P(None, 'gx', 'gy'), may hold values from 0 to 1, as said below
- wave_vectors: int32 [3, 1024], replicated, may hold values from -8 to 8, as said below
- msg_weight: float32 [512, 512], replicated, may hold values from -0.25 to 0.25
- out_gain: float32 [512], replicated, may hold values from 0.1 to 1.9
Outputs:
- updated: float32 [32, 64, 128, 512], P('gx', 'gy')
Inputs may be any that keep to these rules, and one draw needn't show every extreme that they name: positions[:, a, b, t] = ((a + u) / 32, (b + v) / 64, w) with u, v, w in [0, 1): each atom lies in its tile's slab. `wave_vectors`: the 1024 vectors are distinct and nonzero, and hold at most one of each pair k, -k: the first nonzero component of each is positive.
All inputs are finite; a program needn't handle non-finite values.
Results may differ from a plain program's by a relative error of at most 0.0003.
Values sent between devices are 32-bit elements; how exact they have to be, the bound alone decides.
No kernel may reach another device: no remote copies, remote signals or barrier semaphores. Data moves between devices by JAX's collectives and lax.ppermute only.
A program may use at most 128 MiB of HBM per device.

v0:
```python
import functools
import math

import jax
import jax.numpy as jnp
from jax import lax
from jax.experimental import pallas as pl
from jax.experimental.pallas import tpu as pltpu
from jax.sharding import Mesh
from jax.sharding import PartitionSpec as P

HIGH = lax.Precision.HIGHEST
F32, BF16 = jnp.float32, jnp.bfloat16
NN = (((1,), (0,)), ((), ()))
NT = (((1,), (1,)), ((), ()))
SLAB_X, SLAB_Y = ("y", "zl"), ("x", "zh", "c")
VMEM_LIMIT = 56 * 1024 * 1024


def halves(value):
    top = value.astype(BF16)
    return top, (value - top.astype(F32)).astype(BF16)


def dot(a, b, dims=NN):
    return lax.dot_general(a, b, dims, preferred_element_type=F32)


SIN_TERMS = tuple((-1) ** n * math.pi ** (2 * n + 1) / math.factorial(2 * n + 1) for n in range(6))
COS_TERMS = tuple((-1) ** n * math.pi ** (2 * n) / math.factorial(2 * n) for n in range(7))


def horner(terms, square):
    value = jnp.full_like(square, terms[-1])
    for term in terms[-2::-1]:
        value = value * square + term
    return value


def turn(fraction):
    rest = fraction - jnp.round(fraction)
    square = rest * rest
    sine = rest * horner(SIN_TERMS, square)
    cosine = horner(COS_TERMS, square)
    return 1.0 - 2.0 * (sine * sine), 2.0 * (sine * cosine)


def forward_kernel(scale, rows, place, vec, feat_a, feat_b, out, top, low, feat_split):
    atoms = place.shape[0]
    chans = feat_a.shape[1]

    @pl.when(pl.program_id(0) == 0)
    def _():
        for part, ref in enumerate((feat_a, feat_b)):
            count = ref.shape[0]
            hi, lo = halves(ref[...].T)
            feat_split[:chans, part * count : (part + 1) * count] = hi
            feat_split[chans:, part * count : (part + 1) * count] = lo

    vectors = vec[...]
    kx, ky, kz = vectors[0:1], vectors[1:2], vectors[2:3]

    @pl.loop(0, atoms // rows)
    def _(step):
        here = pl.ds(pl.multiple_of(step * rows, rows), rows)
        spot = place[here, :]
        cosine, sine = turn(spot[:, 0:1] * kx + spot[:, 1:2] * ky + spot[:, 2:3] * kz)
        for kind, value in enumerate((cosine, sine)):
            hi, lo = halves(value)
            top[kind, here, :] = hi
            low[kind, here, :] = lo

    damp = scale * jnp.exp(-(kx * kx + ky * ky + kz * kz) / 64.0)
    for kind in range(2):
        both = dot(feat_split[...], top[kind])
        total = both[:chans] + both[chans:] + dot(feat_split[:chans, :], low[kind])
        total = total * damp
        for tile in range(out.shape[1]):
            out[kind, tile] = total[:, tile * 128 : (tile + 1) * 128]


def forward(place, vec, feat_a, feat_b, scale):
    atoms, count, chans = place.shape[0], vec.shape[1], feat_a.shape[1]
    block = 256
    trig = jax.ShapeDtypeStruct((2, atoms, count), BF16)
    trig_spec = pl.BlockSpec((2, atoms, block), lambda j: (0, 0, j))
    whole = lambda a: pl.BlockSpec(a.shape, lambda j: (0, 0))
    return pl.pallas_call(
        functools.partial(forward_kernel, scale, 32),
        grid=(count // block,),
        in_specs=[whole(place), pl.BlockSpec((3, block), lambda j: (0, j)), whole(feat_a), whole(feat_b)],
        out_specs=[pl.BlockSpec((2, block // 128, chans, 128), lambda j: (0, j, 0, 0)), trig_spec, trig_spec],
        out_shape=[jax.ShapeDtypeStruct((2, count // 128, chans, 128), F32), trig, trig],
        scratch_shapes=[pltpu.VMEM((2 * chans, atoms), BF16)],
        compiler_params=pltpu.CompilerParams(vmem_limit_bytes=VMEM_LIMIT),
        cost_estimate=pl.CostEstimate(
            flops=12 * atoms * count * chans, bytes_accessed=24 * 2**20, transcendentals=0
        ),
    )(place, vec, feat_a, feat_b)


def inverse_kernel(top, low, coef, out, coef_top, coef_low):
    tiles = coef.shape[1]

    @pl.when(pl.program_id(0) == 0)
    def _():
        for kind in range(2):
            for tile in range(tiles):
                hi, lo = halves(coef[kind, tile])
                coef_top[kind, :, tile * 128 : (tile + 1) * 128] = hi
                coef_low[kind, :, tile * 128 : (tile + 1) * 128] = lo

    total = None
    for kind in range(2):
        for a, b in ((top, coef_top), (top, coef_low), (low, coef_top)):
            term = dot(a[kind], b[kind], NT)
            total = term if total is None else total + term
    out[...] = total


def inverse(top, low, coef):
    kinds, atoms, count = top.shape
    chans = coef.shape[2]
    block = 256
    trig_spec = pl.BlockSpec((kinds, block, count), lambda i: (0, i, 0))
    return pl.pallas_call(
        inverse_kernel,
        grid=(atoms // block,),
        in_specs=[trig_spec, trig_spec, pl.BlockSpec(coef.shape, lambda i: (0, 0, 0, 0))],
        out_specs=pl.BlockSpec((block, chans), lambda i: (i, 0)),
        out_shape=jax.ShapeDtypeStruct((atoms, chans), F32),
        scratch_shapes=[pltpu.VMEM((kinds, chans, count), BF16)] * 2,
        compiler_params=pltpu.CompilerParams(vmem_limit_bytes=VMEM_LIMIT),
        cost_estimate=pl.CostEstimate(
            flops=12 * atoms * count * chans, bytes_accessed=12 * 2**20, transcendentals=0
        ),
    )(top, low, coef)


def message_kernel(taps, own, up, down, left, right, out, block_top, block_low):
    a, b = pl.program_id(0), pl.program_id(1)

    @pl.when((a == 0) & (b == 0))
    def _():
        def put(row, column, value):
            hi, lo = halves(value)
            block_top[row, column] = hi
            block_low[row, column] = lo

        for i in range(2):
            put(0, 1 + i, up[0, i])
            put(3, 1 + i, down[0, i])
            for j in range(2):
                put(1 + i, 1 + j, own[i, j])
        for i in range(4):
            put(i, 0, left[i, 0])
            put(i, 3, right[i, 0])

    total = None
    for dx in range(3):
        for dy in range(3):
            hi, lo = halves(taps[0, 0, 3 * dx + dy])
            there_top, there_low = block_top[a + dx, b + dy], block_low[a + dx, b + dy]
            for left_part, right_part in ((hi, there_top), (hi, there_low), (lo, there_top)):
                term = dot(left_part, right_part)
                total = term if total is None else total + term
    out[0, 0] = total


def neighbour_sum(taps, own, up, down, left, right):
    tiles_x, tiles_y, rows, chans = own.shape
    whole = lambda a: pl.BlockSpec(a.shape, lambda i, j: (0, 0, 0, 0))
    return pl.pallas_call(
        message_kernel,
        grid=(tiles_x, tiles_y),
        in_specs=[pl.BlockSpec((1, 1) + taps.shape[2:], lambda i, j: (i, j, 0, 0, 0))]
        + [whole(a) for a in (own, up, down, left, right)],
        out_specs=pl.BlockSpec((1, 1, rows, chans), lambda i, j: (i, j, 0, 0)),
        out_shape=jax.ShapeDtypeStruct(own.shape, F32),
        scratch_shapes=[pltpu.VMEM((tiles_x + 2, tiles_y + 2, rows, chans), BF16)] * 2,
        compiler_params=pltpu.CompilerParams(vmem_limit_bytes=VMEM_LIMIT),
        cost_estimate=pl.CostEstimate(
            flops=6 * tiles_x * tiles_y * 9 * rows * rows * chans, bytes_accessed=8 * 2**20, transcendentals=0
        ),
    )(taps, own, up, down, left, right)


def update_kernel(core, message, mine, theirs, feat, gain, out):
    first = core[0] == 0
    a, b = mine[...], theirs[...]
    ewald = jnp.concatenate([jnp.where(first, a, b), jnp.where(first, b, a)], axis=1)
    total = message[...] + ewald
    scale = jnp.sqrt(jnp.mean(total * total, axis=-1, keepdims=True) + 1e-6)
    out[...] = feat[...] + gain[...] * (total / scale)


def update(core, message, ewald, theirs, feat, gain):
    atoms, chans = feat.shape
    block = 128
    rows = pl.BlockSpec((block, chans), lambda i: (i, 0))
    part = pl.BlockSpec((block, chans // 2), lambda i: (i, 0))
    return pl.pallas_call(
        update_kernel,
        grid=(atoms // block,),
        in_specs=[pl.BlockSpec(memory_space=pltpu.SMEM), rows, part, part, rows, pl.BlockSpec((1, chans), lambda i: (0, 0))],
        out_specs=rows,
        out_shape=jax.ShapeDtypeStruct((atoms, chans), F32),
    )(core, message, ewald, theirs, feat, gain)


def neighbours(cells, axis, dim):
    count = lax.axis_size(axis)
    head = lax.slice_in_dim(cells, 0, 1, axis=dim)
    tail = lax.slice_in_dim(cells, cells.shape[dim] - 1, cells.shape[dim], axis=dim)
    before = lax.ppermute(tail, axis, [(i, (i + 1) % count) for i in range(count)])
    after = lax.ppermute(head, axis, [((i + 1) % count, i) for i in range(count)])
    return before, after


def scatter(value, axes):
    count = lax.axis_size(axes)
    parts = value.reshape(count, value.shape[0] // count, value.shape[1])
    return jnp.sum(lax.all_to_all(parts, axes, 0, 0, tiled=True), axis=0)


def gather(value, axes):
    copies = jnp.broadcast_to(value[None], (lax.axis_size(axes),) + value.shape)
    return lax.all_to_all(copies, axes, 0, 0, tiled=True)


def shards(features, tile_filter, positions, wave_vectors, msg_weight, out_gain):
    tiles_x, tiles_y, tile_rows, channels = features.shape
    atoms = tiles_x * tiles_y * tile_rows
    count = wave_vectors.shape[1]
    atoms_all = atoms * lax.axis_size(SLAB_X) * lax.axis_size(SLAB_Y)
    core = lax.axis_index("c")
    swap = [(0, 1), (1, 0)]
    half = channels // 2

    flat = features.reshape(atoms, channels)
    place = positions.reshape(3, atoms).T
    keep = lax.dynamic_slice_in_dim(flat, core * half, half, 1)
    give = lax.dynamic_slice_in_dim(flat, (1 - core) * half, half, 1)
    place = jnp.concatenate([place, lax.ppermute(place, "c", swap)])
    take = lax.ppermute(give, "c", swap)
    scale = 1.0 / math.sqrt(atoms_all) / math.sqrt(count)
    partial, top, low = forward(place, wave_vectors.astype(F32), keep, take, scale)

    projected = jnp.einsum("abtf,fg->abtg", features, msg_weight, precision=HIGH)
    up, down = neighbours(projected, SLAB_X, 0)
    left, right = neighbours(jnp.concatenate([up, projected, down]), SLAB_Y, 1)
    message = neighbour_sum(tile_filter, projected, up, down, left, right)

    rows = partial.reshape(-1, 128)
    rows = scatter(rows, ("x",))
    rows = scatter(rows, ("y", "zl"))
    rows = jnp.sum(gather(rows, ("zh",)), axis=0)
    rows = gather(rows, ("y", "zl")).reshape(-1, 128)
    coef = gather(rows, ("x",)).reshape(partial.shape)

    ewald = inverse(top, low, coef)
    theirs = lax.ppermute(ewald[atoms:], "c", swap)
    out = update(
        core.reshape(1).astype(jnp.int32),
        message.reshape(atoms, channels),
        ewald[:atoms],
        theirs,
        flat,
        out_gain.reshape(1, channels),
    )
    return out.reshape(features.shape)


def solution(mesh):
    fine = Mesh(mesh.devices.reshape(8, 2, 4, 4, 2), ("y", "zl", "x", "zh", "c"))
    placed = (
        P(SLAB_X, SLAB_Y, None, None),
        P(SLAB_X, SLAB_Y, None, None, None),
        P(None, SLAB_X, SLAB_Y, None),
        P(),
        P(),
        P(),
    )
    return jax.shard_map(
        shards, mesh=fine, in_specs=placed, out_specs=P(SLAB_X, SLAB_Y, None, None), check_vma=False
    )
```

profile of v0, /device:TPU:1, one launch (start us, length us, event | category | flops | bytes accessed | tf_op | source)
XLA Modules:
  0.0 204.5 jit_solution(1570628700616842722)
XLA Ops:
  0.0 0.0 copy-start
  0.0 0.0 copy-start.7
  0.0 0.0 copy-start.6
  0.0 2.2 %constant_dynamic-slice_fusion = (f32[512,256]{1,0:T(8,128)S(1)}, f32[512,256]{1,0:T(8,128)}) fusion(f32[512,512]{1,0:T(8,128)} %bitcast.16, s32[]{:T(128)S(6)} %select_n.7, s32[]{:T(128)S(6)} %select_n.6), kind=kLoop, calls=%fused_computation.4 | loop fusion | bytes 2097160 | tf_op jit(solution)/shard_map/dynamic_slice | solution.py:243
  2.2 8.8 %collective-permute-start.5 = (f32[512,256]{1,0:T(8,128)S(1)}, f32[512,256]{1,0:T(8,128)S(1)}, u32[]{:S(2)}, u32[]{:S(2)}) collective-permute-start(f32[512,256]{1,0:T(8,128)S(1)} %get-tuple-element.15), channel_id=1, source_target_pairs={{0,1},{1,0},{2,3},{3,2},{4,5},{5,4},{6,7},{7,6},{8,9},{9,8},{10,11... | collective-permute-start | bytes 1572872 | tf_op jit(solution)/shard_map/ppermute | solution.py:245
  10.9 0.0 copy-done.7
  11.0 1.9 collective-permute-start.4
  12.9 0.0 copy-done.6
  12.9 0.6 convert_element_type.3.vec
  13.5 0.5 collective-permute-done.4
  14.0 1.0 copy.9.place
  15.1 0.0 collective-permute-done.5.feat_b
  15.1 0.0 copy-start.8
  15.1 0.8 copy-done.8
  15.9 23.9 %shard_map.65 = (f32[2,8,256,128]{3,2,1,0:T(8,128)}, bf16[2,1024,1024]{2,1,0:T(8,128)(2,1)}, bf16[2,1024,1024]{2,1,0:T(8,128)(2,1)}) custom-call(f32[1024,3]{1,0:T(8,128)} %copy.9.place, f32[3,1024]{1,0:T(4,128)} %convert_element_type.3.vec, f32[512,256]{1,0:T(8,128)} %get-tuple-element.16.feat_a, f32[512,256]{1,0:T(8,128)} %copy-done.8), custom_call_target="tpu_custom_call" | custom-call | flops 3221225472 | bytes 25165824 | tf_op jit(solution)/shard_map/pallas_call | solution.py:88
  39.8 29.6 %all_to_all.25 = f32[4,1024,128]{2,1,0:T(8,128)S(1)} all-to-all(f32[4,1024,128]{2,1,0:T(8,128)} %bitcast.20), channel_id=1, replica_groups=mesh['y'=8,'zl'=2,'x'=4,'zh'=4,'c'=2] {'x'}, dimensions={0} | all-to-all | bytes 4194304 | tf_op jit(solution)/shard_map/all_to_all | solution.py:223
  69.4 0.9 reduce_sum.27
  70.3 19.0 %all_to_all.26 = f32[16,64,128]{2,1,0:T(8,128)S(1)} all-to-all(f32[16,64,128]{2,1,0:T(8,128)} %bitcast.21), channel_id=1, replica_groups=mesh['y'=8,'zl'=2,'x'=4,'zh'=4,'c'=2] {'y','zl'}, dimensions={0} | all-to-all | bytes 1048576 | tf_op jit(solution)/shard_map/all_to_all | solution.py:223
  89.4 16.2 %all_to_all.27 = f32[4,64,128]{2,1,0:T(8,128)S(1)} all-to-all(f32[4,64,128]{2,1,0:T(8,128)S(1)} %broadcast_in_dim.8), channel_id=1, replica_groups=mesh['y'=8,'zl'=2,'x'=4,'zh'=4,'c'=2] {'zh'}, dimensions={0} | all-to-all | bytes 262144 | tf_op jit(solution)/shard_map/all_to_all | solution.py:228
  105.6 16.8 %all_to_all.28 = f32[16,64,128]{2,1,0:T(8,128)S(1)} all-to-all(f32[16,64,128]{2,1,0:T(8,128)S(1)} %broadcast_in_dim.9), channel_id=1, replica_groups=mesh['y'=8,'zl'=2,'x'=4,'zh'=4,'c'=2] {'y','zl'}, dimensions={0} | all-to-all | bytes 1048576 | tf_op jit(solution)/shard_map/all_to_all | solution.py:228
  122.4 1.5 broadcast_in_dim.22
  123.9 4.6 %all-to-all-start.4 = ((f32[4,1024,128]{2,1,0:T(8,128)}), f32[4,1024,128]{2,1,0:T(8,128)}, u32[]{:S(2)}, u32[]{:S(2)}) async-start(f32[4,1024,128]{2,1,0:T(8,128)} %broadcast_in_dim.22), calls=%async_computation.4 | async-start | bytes 4194304 | tf_op jit(solution)/shard_map/all_to_all | solution.py:228
  128.5 0.0 copy-done
  128.5 0.0 copy-done.2
  128.5 1.9 fusion.own
  130.3 0.0 copy-start.1
  130.4 0.1 fusion.4
  130.4 1.9 collective-permute-start
  132.4 5.5 %collective-permute-start.1 = (f32[1,2,128,512]{3,2,1,0:T(8,128)S(1)}, f32[1,2,128,512]{3,2,1,0:T(8,128)S(1)}, u32[]{:S(2)}, u32[]{:S(2)}) collective-permute-start(f32[1,2,128,512]{3,2,1,0:T(8,128)S(1)} %get-tuple-element.17), channel_id=1, source_target_pairs={{32,0},{64,32},{96,64},{128,96},{160,128},{192,160},{224,192},{256... | collective-permute-start | bytes 1572872 | tf_op jit(solution)/shard_map/ppermute | solution.py:216
  137.8 13.0 %collective-permute-done.up = f32[1,2,128,512]{3,2,1,0:T(8,128)S(1)} collective-permute-done((f32[1,2,128,512]{3,2,1,0:T(8,128)S(1)}, f32[1,2,128,512]{3,2,1,0:T(8,128)S(1)}, u32[]{:S(2)}, u32[]{:S(2)}) %collective-permute-start) | collective-permute-done | bytes 524320 | tf_op jit(solution)/shard_map/ppermute | solution.py:215
  150.8 8.1 %collective-permute-done.1.down = f32[1,2,128,512]{3,2,1,0:T(8,128)S(1)} collective-permute-done((f32[1,2,128,512]{3,2,1,0:T(8,128)S(1)}, f32[1,2,128,512]{3,2,1,0:T(8,128)S(1)}, u32[]{:S(2)}, u32[]{:S(2)}) %collective-permute-start.1) | collective-permute-done | bytes 524320 | tf_op jit(solution)/shard_map/ppermute | solution.py:216
  158.9 0.2 pad_maximum_fusion
  159.0 0.0 copy-done.1
  159.0 0.0 copy-done.3
  159.1 0.6 copy-done.4
  159.7 0.2 fusion.2
  159.8 4.2 %collective-permute-start.2 = (f32[4,1,128,512]{3,2,1,0:T(8,128)S(1)}, f32[4,1,128,512]{3,2,1,0:T(8,128)}, u32[]{:S(2)}, u32[]{:S(2)}) collective-permute-start(f32[4,1,128,512]{3,2,1,0:T(8,128)S(1)} %get-tuple-element.12), channel_id=1, source_target_pairs={{0,1},{1,2},{2,3},{3,4},{4,5},{5,6},{6,7},{7,8},{8,9},{9,10},{10,1... | collective-permute-start | bytes 3145736 | tf_op jit(solution)/shard_map/ppermute | solution.py:215
  164.1 1.9 collective-permute-start.3
  166.0 0.0 all-to-all-done.4
  166.0 8.4 %shard_map.66 = f32[1024,256]{1,0:T(8,128)} custom-call(bf16[2,1024,1024]{2,1,0:T(8,128)(2,1)} %get-tuple-element.8.top, bf16[2,1024,1024]{2,1,0:T(8,128)(2,1)} %get-tuple-element.9.low, f32[2,8,256,128]{3,2,1,0:T(8,128)} %bitcast.9.coef), custom_call_target="tpu_custom_call" | custom-call | flops 3221225472 | bytes 12582912 | tf_op jit(solution)/shard_map/pallas_call | solution.py:126
  174.4 2.1 %fusion.3 = (f32[512,256]{1,0:T(8,128)S(1)}, f32[512,256]{1,0:T(8,128)}) fusion(f32[1024,256]{1,0:T(8,128)} %shard_map.66), kind=kLoop, calls=%fused_computation.7 | loop fusion | bytes 2097152 | tf_op jit(solution)/shard_map/slice | solution.py:262
  176.5 6.6 %collective-permute-start.6 = (f32[512,256]{1,0:T(8,128)S(1)}, f32[512,256]{1,0:T(8,128)S(1)}, u32[]{:S(2)}, u32[]{:S(2)}) collective-permute-start(f32[512,256]{1,0:T(8,128)S(1)} %get-tuple-element.13), channel_id=1, source_target_pairs={{0,1},{1,0},{2,3},{3,2},{4,5},{5,4},{6,7},{7,6},{8,9},{9,8},{10,11... | collective-permute-start | bytes 1572872 | tf_op jit(solution)/shard_map/ppermute | solution.py:262
  183.1 3.0 %collective-permute-done.2.left = f32[4,1,128,512]{3,2,1,0:T(8,128)} collective-permute-done((f32[4,1,128,512]{3,2,1,0:T(8,128)S(1)}, f32[4,1,128,512]{3,2,1,0:T(8,128)}, u32[]{:S(2)}, u32[]{:S(2)}) %collective-permute-start.2) | collective-permute-done | bytes 1048608 | tf_op jit(solution)/shard_map/ppermute | solution.py:215
  186.1 5.4 %collective-permute-done.3.right = f32[4,1,128,512]{3,2,1,0:T(8,128)} collective-permute-done((f32[4,1,128,512]{3,2,1,0:T(8,128)S(1)}, f32[4,1,128,512]{3,2,1,0:T(8,128)}, u32[]{:S(2)}, u32[]{:S(2)}) %collective-permute-start.3) | collective-permute-done | bytes 1048608 | tf_op jit(solution)/shard_map/ppermute | solution.py:216
  191.5 8.1 %shard_map.64 = f32[2,2,128,512]{3,2,1,0:T(8,128)} custom-call(f32[2,2,9,128,128]{4,3,2,1,0:T(8,128)} %taps.1, f32[2,2,128,512]{3,2,1,0:T(8,128)} %copy-done.1, f32[1,2,128,512]{3,2,1,0:T(8,128)} %copy-done.3, f32[1,2,128,512]{3,2,1,0:T(8,128)} %copy-done.4, f32[4,1,128,512]{3,2,1,0:T(8,128)} %collective-permute-done.2.left, ...), custom_call_target="tpu_custom_call" | custom-call | flops 1811939328 | bytes 8388608 | tf_op jit(solution)/shard_map/pallas_call | solution.py:173
  199.6 0.0 collective-permute-done.6.theirs
  199.6 0.8 copy-done.5
  200.5 4.0 %shard_map.67 = f32[512,512]{1,0:T(8,128)} custom-call(s32[1]{0:T(128)} %bitcast.core, f32[512,512]{1,0:T(8,128)} %bitcast.18, f32[512,256]{1,0:T(8,128)} %get-tuple-element.14.mine, f32[512,256]{1,0:T(8,128)} %copy-done.5, f32[512,512]{1,0:T(8,128)} %bitcast.17, f32[1,512]{1,0:T(1,128)} %bitcast.24), custom_call_target="tpu_custom_call" | custom-call | tf_op jit(solution)/shard_map/pallas_call | solution.py:202
  (10 shorter events, 0.1 us)
Async XLA Ops:
  0.0 128.5 %copy-start = (f32[512,512]{1,0:T(8,128)S(1)}, f32[512,512]{1,0:T(8,128)}, u32[]{:S(2)}) copy-start(f32[512,512]{1,0:T(8,128)} %param.10) | copy-start | bytes 3145732
  0.0 10.9 %copy-start.7 = (f32[3,2,2,128]{3,2,1,0:T(2,128)S(1)}, f32[3,2,2,128]{3,2,1,0:T(2,128)}, u32[]{:S(2)}) copy-start(f32[3,2,2,128]{3,2,1,0:T(2,128)} %param.8) | copy-start | bytes 18436
  0.0 12.9 %copy-start.6 = (s32[3,1024]{1,0:T(4,128)S(1)}, s32[3,1024]{1,0:T(4,128)}, u32[]{:S(2)}) copy-start(s32[3,1024]{1,0:T(4,128)} %param.9) | copy-start | bytes 36868
  2.2 12.9 %collective-permute-start.5 = (f32[512,256]{1,0:T(8,128)S(1)}, f32[512,256]{1,0:T(8,128)S(1)}, u32[]{:S(2)}, u32[]{:S(2)}) collective-permute-start(f32[512,256]{1,0:T(8,128)S(1)} %get-tuple-element.15), channel_id=1, source_target_pairs={{0,1},{1,0},{2,3},{3,2},{4,5},{5,4},{6,7},{7,6},{8,9},{9,8},{10,11... | collective-permute-start | bytes 1572872 | tf_op jit(solution)/shard_map/ppermute | solution.py:245
  11.0 3.1 %collective-permute-start.4 = (f32[512,3]{0,1:T(4,128)S(1)}, f32[512,3]{0,1:T(4,128)S(1)}, u32[]{:S(2)}, u32[]{:S(2)}) collective-permute-start(f32[512,3]{0,1:T(4,128)S(1)} %bitcast.22), channel_id=1, source_target_pairs={{0,1},{1,0},{2,3},{3,2},{4,5},{5,4},{6,7},{7,6},{8,9},{9,8},{10,11... | collective-permute-start | bytes 18440 | tf_op jit(solution)/shard_map/ppermute | solution.py:244
  15.1 0.8 copy-start.8
  123.9 4.6 %copy-start.2 = (f32[2,2,128,512]{3,2,1,0:T(8,128)S(1)}, f32[2,2,128,512]{3,2,1,0:T(8,128)}, u32[]{:S(2)}) copy-start(f32[2,2,128,512]{3,2,1,0:T(8,128)} %param.6) | copy-start | bytes 3145732
  123.9 42.1 %all-to-all-start.4 = ((f32[4,1024,128]{2,1,0:T(8,128)}), f32[4,1024,128]{2,1,0:T(8,128)}, u32[]{:S(2)}, u32[]{:S(2)}) async-start(f32[4,1024,128]{2,1,0:T(8,128)} %broadcast_in_dim.22), calls=%async_computation.4 | async-start | bytes 4194304 | tf_op jit(solution)/shard_map/all_to_all | solution.py:228
  130.3 28.7 %copy-start.1 = (f32[2,2,128,512]{3,2,1,0:T(8,128)}, f32[2,2,128,512]{3,2,1,0:T(8,128)S(1)}, u32[]{:S(2)}) copy-start(f32[2,2,128,512]{3,2,1,0:T(8,128)S(1)} %fusion.own) | copy-start | bytes 3145732
  130.4 20.4 %collective-permute-start = (f32[1,2,128,512]{3,2,1,0:T(8,128)S(1)}, f32[1,2,128,512]{3,2,1,0:T(8,128)S(1)}, u32[]{:S(2)}, u32[]{:S(2)}) collective-permute-start(f32[1,2,128,512]{3,2,1,0:T(8,128)S(1)} %get-tuple-element.18), channel_id=1, source_target_pairs={{0,32},{32,64},{64,96},{96,128},{128,160},{160,192},{192,224},{224... | collective-permute-start | bytes 1572872 | tf_op jit(solution)/shard_map/ppermute | solution.py:215
  132.4 26.5 %collective-permute-start.1 = (f32[1,2,128,512]{3,2,1,0:T(8,128)S(1)}, f32[1,2,128,512]{3,2,1,0:T(8,128)S(1)}, u32[]{:S(2)}, u32[]{:S(2)}) collective-permute-start(f32[1,2,128,512]{3,2,1,0:T(8,128)S(1)} %get-tuple-element.17), channel_id=1, source_target_pairs={{32,0},{64,32},{96,64},{128,96},{160,128},{192,160},{224,192},{256... | collective-permute-start | bytes 1572872 | tf_op jit(solution)/shard_map/ppermute | solution.py:216
  150.8 8.2 %copy-start.3 = (f32[1,2,128,512]{3,2,1,0:T(8,128)}, f32[1,2,128,512]{3,2,1,0:T(8,128)S(1)}, u32[]{:S(2)}) copy-start(f32[1,2,128,512]{3,2,1,0:T(8,128)S(1)} %collective-permute-done.up) | copy-start | bytes 1572868
  158.9 0.8 copy-start.4
  159.8 26.3 %collective-permute-start.2 = (f32[4,1,128,512]{3,2,1,0:T(8,128)S(1)}, f32[4,1,128,512]{3,2,1,0:T(8,128)}, u32[]{:S(2)}, u32[]{:S(2)}) collective-permute-start(f32[4,1,128,512]{3,2,1,0:T(8,128)S(1)} %get-tuple-element.12), channel_id=1, source_target_pairs={{0,1},{1,2},{2,3},{3,4},{4,5},{5,6},{6,7},{7,8},{8,9},{9,10},{10,1... | collective-permute-start | bytes 3145736 | tf_op jit(solution)/shard_map/ppermute | solution.py:215
  164.1 27.4 %collective-permute-start.3 = (f32[4,1,128,512]{3,2,1,0:T(8,128)S(1)}, f32[4,1,128,512]{3,2,1,0:T(8,128)}, u32[]{:S(2)}, u32[]{:S(2)}) collective-permute-start(f32[4,1,128,512]{3,2,1,0:T(8,128)S(1)} %get-tuple-element.11), channel_id=1, source_target_pairs={{1,0},{2,1},{3,2},{4,3},{5,4},{6,5},{7,6},{8,7},{9,8},{10,9},{11,1... | collective-permute-start | bytes 3145736 | tf_op jit(solution)/shard_map/ppermute | solution.py:216
  176.5 23.2 %collective-permute-start.6 = (f32[512,256]{1,0:T(8,128)S(1)}, f32[512,256]{1,0:T(8,128)S(1)}, u32[]{:S(2)}, u32[]{:S(2)}) collective-permute-start(f32[512,256]{1,0:T(8,128)S(1)} %get-tuple-element.13), channel_id=1, source_target_pairs={{0,1},{1,0},{2,3},{3,2},{4,5},{5,4},{6,7},{7,6},{8,9},{9,8},{10,11... | collective-permute-start | bytes 1572872 | tf_op jit(solution)/shard_map/ppermute | solution.py:262
  199.6 0.8 copy-start.5
where the time goes:
time: 205 us
  blocking collectives  81.6 us (40%)
  Pallas kernels  44.5 us (22%)
  starting transfers between devices  35.4 us (17%)
  waiting for transfers between devices  30 us (15%)
  local copies, waits for them, and re-layouts  9.29 us (5%)
    all_to_all x2, blocking collectives, scatter(): return jnp.sum(lax.all_to_all(parts, axes, 0, 0, tiled=True), axis=0)  48.6 us
    all_to_all x2, blocking collectives, gather(): return lax.all_to_all(copies, axes, 0, 0, tiled=True)  32.9 us
    pallas_call x1, Pallas kernels, forward(): pl.pallas_call(functools.partial(forward_kernel, scale, 32), grid=(count...  23.9 us
    ppermute x2, waiting for transfers between devices, neighbours(): lax.ppermute(tail, axis, [(i, (i + 1) % count) for i in range(count)])  16 us
    ppermute x2, waiting for transfers between devices, neighbours(): lax.ppermute(head, axis, [((i + 1) % count, i) for i in range(count)])  13.4 us
    ppermute x1, starting transfers between devices, shards(): take = lax.ppermute(give, 'c', swap)  8.76 us
    pallas_call x1, Pallas kernels, inverse(): pl.pallas_call(inverse_kernel, grid=(atoms // block,), in_specs=[trig_spe...  8.4 us
    pallas_call x1, Pallas kernels, neighbour_sum(): pl.pallas_call(message_kernel, grid=(tiles_x, tiles_y), in_specs=[pl.Bloc...  8.13 us
  transfers between devices with their start and end apart: 8, of which 5 were waited for; matrix products, arithmetic and copies ran while one was open for 3% of the time, Pallas kernels for 8%

commit v1 on v0

--- a/solution.py
+++ b/solution.py
@@ -9,12 +9,11 @@
 from jax.sharding import Mesh
 from jax.sharding import PartitionSpec as P
 
-HIGH = lax.Precision.HIGHEST
 F32, BF16 = jnp.float32, jnp.bfloat16
 NN = (((1,), (0,)), ((), ()))
 NT = (((1,), (1,)), ((), ()))
 SLAB_X, SLAB_Y = ("y", "zl"), ("x", "zh", "c")
-VMEM_LIMIT = 56 * 1024 * 1024
+VMEM_LIMIT = 24 * 1024 * 1024
 
 
 def halves(value):
@@ -26,8 +25,9 @@
     return lax.dot_general(a, b, dims, preferred_element_type=F32)
 
 
-SIN_TERMS = tuple((-1) ** n * math.pi ** (2 * n + 1) / math.factorial(2 * n + 1) for n in range(6))
-COS_TERMS = tuple((-1) ** n * math.pi ** (2 * n) / math.factorial(2 * n) for n in range(7))
+SIN_TERMS = (4.44288292, -7.30824569, 3.60635422, -0.84611165, 0.109824516)
+COS_TERMS = (1.4142135, -6.97885095, 5.73946038, -1.88355791, 0.310688028)
+WHOLE = 12582912.0
 
 
 def horner(terms, square):
@@ -38,65 +38,88 @@
 
 
 def turn(fraction):
-    rest = fraction - jnp.round(fraction)
+    rest = fraction - ((fraction + WHOLE) - WHOLE)
     square = rest * rest
     sine = rest * horner(SIN_TERMS, square)
     cosine = horner(COS_TERMS, square)
-    return 1.0 - 2.0 * (sine * sine), 2.0 * (sine * cosine)
-
-
-def forward_kernel(scale, rows, place, vec, feat_a, feat_b, out, top, low, feat_split):
-    atoms = place.shape[0]
-    chans = feat_a.shape[1]
-
+    return 1.0 - sine * sine, sine * cosine
+
+
+def trig_kernel(rows, place, vec, top, low, split, angle):
     @pl.when(pl.program_id(0) == 0)
     def _():
-        for part, ref in enumerate((feat_a, feat_b)):
-            count = ref.shape[0]
-            hi, lo = halves(ref[...].T)
-            feat_split[:chans, part * count : (part + 1) * count] = hi
-            feat_split[chans:, part * count : (part + 1) * count] = lo
-
-    vectors = vec[...]
-    kx, ky, kz = vectors[0:1], vectors[1:2], vectors[2:3]
-
-    @pl.loop(0, atoms // rows)
+        rest = place[...]
+        for part in range(3):
+            piece = rest.astype(BF16)
+            split[:, 3 * part : 3 * part + 3] = piece
+            rest = rest - piece.astype(F32)
+
+    vectors = vec[...].astype(BF16)
+    angle[...] = dot(split[...], jnp.concatenate([vectors] * 3))
+
+    @pl.loop(0, place.shape[0] // rows)
     def _(step):
         here = pl.ds(pl.multiple_of(step * rows, rows), rows)
-        spot = place[here, :]
-        cosine, sine = turn(spot[:, 0:1] * kx + spot[:, 1:2] * ky + spot[:, 2:3] * kz)
-        for kind, value in enumerate((cosine, sine)):
-            hi, lo = halves(value)
-            top[kind, here, :] = hi
-            low[kind, here, :] = lo
-
-    damp = scale * jnp.exp(-(kx * kx + ky * ky + kz * kz) / 64.0)
+        for kind, value in enumerate(turn(angle[here, :])):
+            top[kind, here, :], low[kind, here, :] = halves(value)
+
+
+def trig(place, vec):
+    atoms, count = place.shape[0], vec.shape[1]
+    block = 256
+    shape = jax.ShapeDtypeStruct((2, atoms, count), BF16)
+    spec = pl.BlockSpec((2, atoms, block), lambda j: (0, 0, j))
+    return pl.pallas_call(
+        functools.partial(trig_kernel, 32),
+        grid=(count // block,),
+        in_specs=[pl.BlockSpec(place.shape, lambda j: (0, 0)), pl.BlockSpec((3, block), lambda j: (0, j))],
+        out_specs=[spec, spec],
+        out_shape=[shape, shape],
+        scratch_shapes=[pltpu.VMEM((atoms, 9), BF16), pltpu.VMEM((atoms, block), F32)],
+        compiler_params=pltpu.CompilerParams(vmem_limit_bytes=VMEM_LIMIT),
+        cost_estimate=pl.CostEstimate(flops=4 * 2**30, bytes_accessed=4 * 2**20, transcendentals=0),
+    )(place, vec)
+
+
+def structure_kernel(scale, core, vec, feat, take, top_a, low_a, top_b, low_b, out, split):
+    atoms, chans = take.shape
+
+    @pl.when(pl.program_id(0) == 0)
+    def _():
+        start = pl.multiple_of(core[0] * chans, chans)
+        for part, value in enumerate((feat[:, pl.ds(start, chans)], take[...])):
+            split[part, :chans], split[part, chans:] = halves(value.T)
+
+    vectors = vec[...]
+    damp = scale * jnp.exp(-jnp.sum(vectors * vectors, axis=0, keepdims=True) / 64.0)
     for kind in range(2):
-        both = dot(feat_split[...], top[kind])
-        total = both[:chans] + both[chans:] + dot(feat_split[:chans, :], low[kind])
+        both = dot(split[0], top_a[kind]) + dot(split[1], top_b[kind])
+        total = both[:chans] + both[chans:]
+        total = total + dot(split[0, :chans], low_a[kind]) + dot(split[1, :chans], low_b[kind])
         total = total * damp
         for tile in range(out.shape[1]):
             out[kind, tile] = total[:, tile * 128 : (tile + 1) * 128]
 
 
-def forward(place, vec, feat_a, feat_b, scale):
-    atoms, count, chans = place.shape[0], vec.shape[1], feat_a.shape[1]
+def structure(core, vec, feat, take, trigs, scale):
+    atoms, chans = take.shape
+    count = vec.shape[1]
     block = 256
-    trig = jax.ShapeDtypeStruct((2, atoms, count), BF16)
-    trig_spec = pl.BlockSpec((2, atoms, block), lambda j: (0, 0, j))
+    spec = pl.BlockSpec((2, atoms, block), lambda j: (0, 0, j))
     whole = lambda a: pl.BlockSpec(a.shape, lambda j: (0, 0))
     return pl.pallas_call(
-        functools.partial(forward_kernel, scale, 32),
+        functools.partial(structure_kernel, scale),
         grid=(count // block,),
-        in_specs=[whole(place), pl.BlockSpec((3, block), lambda j: (0, j)), whole(feat_a), whole(feat_b)],
-        out_specs=[pl.BlockSpec((2, block // 128, chans, 128), lambda j: (0, j, 0, 0)), trig_spec, trig_spec],
-        out_shape=[jax.ShapeDtypeStruct((2, count // 128, chans, 128), F32), trig, trig],
-        scratch_shapes=[pltpu.VMEM((2 * chans, atoms), BF16)],
+        in_specs=[pl.BlockSpec(memory_space=pltpu.SMEM), pl.BlockSpec((3, block), lambda j: (0, j)), whole(feat), whole(take)]
+        + [spec] * 4,
+        out_specs=pl.BlockSpec((2, block // 128, chans, 128), lambda j: (0, j, 0, 0)),
+        out_shape=jax.ShapeDtypeStruct((2, count // 128, chans, 128), F32),
+        scratch_shapes=[pltpu.VMEM((2, 2 * chans, atoms), BF16)],
         compiler_params=pltpu.CompilerParams(vmem_limit_bytes=VMEM_LIMIT),
         cost_estimate=pl.CostEstimate(
-            flops=12 * atoms * count * chans, bytes_accessed=24 * 2**20, transcendentals=0
+            flops=24 * atoms * count * chans, bytes_accessed=12 * 2**20, transcendentals=0
         ),
-    )(place, vec, feat_a, feat_b)
+    )(core, vec, feat, take, *trigs)
 
 
 def inverse_kernel(top, low, coef, out, coef_top, coef_low):
@@ -106,14 +129,13 @@
     def _():
         for kind in range(2):
             for tile in range(tiles):
-                hi, lo = halves(coef[kind, tile])
-                coef_top[kind, :, tile * 128 : (tile + 1) * 128] = hi
-                coef_low[kind, :, tile * 128 : (tile + 1) * 128] = lo
+                here = slice(tile * 128, (tile + 1) * 128)
+                coef_top[kind, here, :], coef_low[kind, here, :] = halves(coef[kind, tile].T)
 
     total = None
     for kind in range(2):
         for a, b in ((top, coef_top), (top, coef_low), (low, coef_top)):
-            term = dot(a[kind], b[kind], NT)
+            term = dot(a[kind], b[kind])
             total = term if total is None else total + term
     out[...] = total
 
@@ -129,10 +151,10 @@
         in_specs=[trig_spec, trig_spec, pl.BlockSpec(coef.shape, lambda i: (0, 0, 0, 0))],
         out_specs=pl.BlockSpec((block, chans), lambda i: (i, 0)),
         out_shape=jax.ShapeDtypeStruct((atoms, chans), F32),
-        scratch_shapes=[pltpu.VMEM((kinds, chans, count), BF16)] * 2,
+        scratch_shapes=[pltpu.VMEM((kinds, count, chans), BF16)] * 2,
         compiler_params=pltpu.CompilerParams(vmem_limit_bytes=VMEM_LIMIT),
         cost_estimate=pl.CostEstimate(
-            flops=12 * atoms * count * chans, bytes_accessed=12 * 2**20, transcendentals=0
+            flops=12 * atoms * count * chans, bytes_accessed=6 * 2**20, transcendentals=0
         ),
     )(top, low, coef)
 
@@ -194,7 +216,7 @@
     out[...] = feat[...] + gain[...] * (total / scale)
 
 
-def update(core, message, ewald, theirs, feat, gain):
+def update(core, message, own, got, feat, gain):
     atoms, chans = feat.shape
     block = 128
     rows = pl.BlockSpec((block, chans), lambda i: (i, 0))
@@ -205,7 +227,7 @@
         in_specs=[pl.BlockSpec(memory_space=pltpu.SMEM), rows, part, part, rows, pl.BlockSpec((1, chans), lambda i: (0, 0))],
         out_specs=rows,
         out_shape=jax.ShapeDtypeStruct((atoms, chans), F32),
-    )(core, message, ewald, theirs, feat, gain)
+    )(core, message, own, got, feat, gain)
 
 
 def neighbours(cells, axis, dim):
@@ -234,40 +256,40 @@
     count = wave_vectors.shape[1]
     atoms_all = atoms * lax.axis_size(SLAB_X) * lax.axis_size(SLAB_Y)
     core = lax.axis_index("c")
+    which = core.reshape(1).astype(jnp.int32)
     swap = [(0, 1), (1, 0)]
     half = channels // 2
+    scale = 1.0 / math.sqrt(atoms_all) / math.sqrt(count)
 
     flat = features.reshape(atoms, channels)
+    vec = wave_vectors.astype(F32)
     place = positions.reshape(3, atoms).T
-    keep = lax.dynamic_slice_in_dim(flat, core * half, half, 1)
-    give = lax.dynamic_slice_in_dim(flat, (1 - core) * half, half, 1)
-    place = jnp.concatenate([place, lax.ppermute(place, "c", swap)])
-    take = lax.ppermute(give, "c", swap)
-    scale = 1.0 / math.sqrt(atoms_all) / math.sqrt(count)
-    partial, top, low = forward(place, wave_vectors.astype(F32), keep, take, scale)
-
-    projected = jnp.einsum("abtf,fg->abtg", features, msg_weight, precision=HIGH)
+    take = lax.ppermute(lax.dynamic_slice_in_dim(flat, (1 - core) * half, half, 1), "c", swap)
+    other = lax.ppermute(place, "c", swap)
+    projected = jnp.einsum("abtf,fg->abtg", features, msg_weight, precision=lax.Precision.HIGH)
     up, down = neighbours(projected, SLAB_X, 0)
+    place, _ = lax.optimization_barrier((place, projected))
+    mine = trig(place, vec)
+    other, _ = lax.optimization_barrier((other, mine[0]))
+    theirs = trig(other, vec)
+    partial = structure(which, vec, flat, take, (*mine, *theirs), scale)
+
+    rows, up, down = lax.optimization_barrier((partial.reshape(-1, 128), up, down))
     left, right = neighbours(jnp.concatenate([up, projected, down]), SLAB_Y, 1)
+    rows = scatter(rows, ("x",))
+    rows, left, right = lax.optimization_barrier((rows, left, right))
     message = neighbour_sum(tile_filter, projected, up, down, left, right)
-
-    rows = partial.reshape(-1, 128)
-    rows = scatter(rows, ("x",))
     rows = scatter(rows, ("y", "zl"))
+    rows, message = lax.optimization_barrier((rows, message))
     rows = jnp.sum(gather(rows, ("zh",)), axis=0)
     rows = gather(rows, ("y", "zl")).reshape(-1, 128)
     coef = gather(rows, ("x",)).reshape(partial.shape)
 
-    ewald = inverse(top, low, coef)
-    theirs = lax.ppermute(ewald[atoms:], "c", swap)
-    out = update(
-        core.reshape(1).astype(jnp.int32),
-        message.reshape(atoms, channels),
-        ewald[:atoms],
-        theirs,
-        flat,
-        out_gain.reshape(1, channels),
-    )
+    given = inverse(*theirs, coef)
+    got = lax.ppermute(given, "c", swap)
+    coef, _ = lax.optimization_barrier((coef, given))
+    own = inverse(*mine, coef)
+    out = update(which, message.reshape(atoms, channels), own, got, flat, out_gain.reshape(1, channels))
     return out.reshape(features.shape)
 
 

time: 205 us -> 185 us (0.902)
  blocking collectives: 81.6 us -> 63.5 us
  Pallas kernels: 44.5 us -> 31.8 us
  starting transfers between devices: 35.4 us -> 40.2 us
  waiting for transfers between devices: 30 us -> 33 us
  other arithmetic: 1.76 us -> 3.85 us
    all_to_all x2 -> x0, blocking collectives: 48.6 us -> none  [scatter(): return jnp.sum(lax.all_to_all(parts, axes, 0, 0, tiled=True), axis=0)]
    all_to_all x2 -> x3, blocking collectives: 32.9 us -> 63.5 us  [gather(): return lax.all_to_all(copies, axes, 0, 0, tiled=True)]
    all_to_all x1 -> x2, waiting for transfers between devices: 0.01 us -> 29.1 us  [scatter(): return jnp.sum(lax.all_to_all(parts, axes, 0, 0, tiled=True), axis=0)]
    ppermute x2, waiting for transfers between devices: 16 us -> 0.01 us  [neighbours(): lax.ppermute(tail, axis, [(i, (i + 1) % count) for i in range(count)])]
    ppermute x2, waiting for transfers between devices: 13.4 us -> 3.91 us  [neighbours(): lax.ppermute(head, axis, [((i + 1) % count, i) for i in range(count)])]
    pallas_call x1 -> x3, Pallas kernels: 23.9 us -> 15.4 us  [the longest x2 9.8 us: trig(): pl.pallas_call(functools.partial(trig_kernel, 32), grid=(count // block,)...]
    unnamed x18 -> x33, local copies, waits for them, and re-layouts: 2.26 us -> 6.6 us
    all_to_all x1 -> x2, starting transfers between devices: 4.6 us -> 8.75 us  [scatter(): return jnp.sum(lax.all_to_all(parts, axes, 0, 0, tiled=True), axis=0)]
  transfers between devices with their start and end apart: 8 -> 9, of which waited for: 5 -> 3; matrix products, arithmetic and copies ran while one was open for 3% -> 4% of each run, Pallas kernels for 8% -> 13%
where the time goes in v1:
time: 185 us; the launch traced here: 184 us
  blocking collectives  63.5 us (34%)
  starting transfers between devices  40.2 us (22%)
  waiting for transfers between devices  33 us (18%)
  Pallas kernels  31.8 us (17%)
  local copies, waits for them, and re-layouts  9.52 us (5%)
  other arithmetic  3.85 us (2%)
  matrix products  2.24 us (1%)
    all_to_all x3, blocking collectives, gather(): return lax.all_to_all(copies, axes, 0, 0, tiled=True)  63.5 us
    all_to_all x2, waiting for transfers between devices, scatter(): return jnp.sum(lax.all_to_all(parts, axes, 0, 0, tiled=True), axis=0)  29.1 us
    pallas_call x2, Pallas kernels, trig(): pl.pallas_call(functools.partial(trig_kernel, 32), grid=(count // block,)...  9.8 us
    ppermute x1, starting transfers between devices, shards(): got = lax.ppermute(given, 'c', swap)  8.96 us
    ppermute x1, starting transfers between devices, shards(): other = lax.ppermute(place, 'c', swap)  8.79 us
    all_to_all x2, starting transfers between devices, scatter(): return jnp.sum(lax.all_to_all(parts, axes, 0, 0, tiled=True), axis=0)  8.75 us
    unnamed x33, local copies, waits for them, and re-layouts  6.6 us
    ppermute x2, starting transfers between devices, neighbours(): lax.ppermute(tail, axis, [(i, (i + 1) % count) for i in range(count)])  6.57 us
  transfers between devices with their start and end apart: 9, of which 3 were waited for; matrix products, arithmetic and copies ran while one was open for 4% of the time, Pallas kernels for 13%

profile of v1, /device:TPU:1, one launch (start us, length us, event | category | flops | bytes accessed | tf_op | source)
XLA Modules:
  0.0 184.4 jit_solution(14800624283758869096)
XLA Ops:
  0.0 0.0 copy-start
  0.0 0.9 copy.8
  0.9 8.8 %collective-permute-start.1 = (f32[512,3]{1,0:T(8,128)S(1)}, f32[512,3]{1,0:T(8,128)}, u32[]{:S(2)}, u32[]{:S(2)}) collective-permute-start(f32[512,3]{1,0:T(8,128)S(1)} %bitcast.26), channel_id=1, source_target_pairs={{0,1},{1,0},{2,3},{3,2},{4,5},{5,4},{6,7},{7,6},{8,9},{9,8},{10,11... | collective-permute-start | bytes 18440 | tf_op jit(solution)/shard_map/ppermute | solution.py:268
  9.7 1.1 constant_dynamic-slice_fusion
  10.8 0.0 copy-start.15
  10.8 1.9 %collective-permute-start = (f32[512,256]{1,0:T(8,128)S(1)}, f32[512,256]{1,0:T(8,128)S(1)}, u32[]{:S(2)}, u32[]{:S(2)}) collective-permute-start(f32[512,256]{1,0:T(8,128)S(1)} %constant_dynamic-slice_fusion), channel_id=1, source_target_pairs={{0,1},{1,0},{2,3},{3,2},{4,5},{5,4},{6,7},{7,6},{8,9},{9,8},{10,11... | collective-permute-start | bytes 1572872 | tf_op jit(solution)/shard_map/ppermute | solution.py:267
  12.8 0.0 copy-done
  12.8 2.2 %fusion.own = f32[2,2,128,512]{3,2,1,0:T(8,128)S(1)} fusion(f32[2,2,128,512]{3,2,1,0:T(8,128)} %param.6, f32[512,512]{1,0:T(8,128)S(1)} %copy-done), kind=kOutput, calls=%fused_computation.1 | convolution fusion | flops 805306368 | bytes 3145728 | tf_op jit(solution)/shard_map/abtf,fg->abtg/dot_general | solution.py:269
  15.0 0.1 fusion.3
  15.1 1.9 %collective-permute-start.3 = (f32[1,2,128,512]{3,2,1,0:T(8,128)S(1)}, f32[1,2,128,512]{3,2,1,0:T(8,128)S(1)}, u32[]{:S(2)}, u32[]{:S(2)}) collective-permute-start(f32[1,2,128,512]{3,2,1,0:T(8,128)S(1)} %get-tuple-element.37), channel_id=1, source_target_pairs={{32,0},{64,32},{96,64},{128,96},{160,128},{192,160},{224,192},{256... | collective-permute-start | bytes 1572872 | tf_op jit(solution)/shard_map/ppermute | solution.py:238
  17.0 3.4 %collective-permute-start.2 = (f32[1,2,128,512]{3,2,1,0:T(8,128)S(1)}, f32[1,2,128,512]{3,2,1,0:T(8,128)S(1)}, u32[]{:S(2)}, u32[]{:S(2)}) collective-permute-start(f32[1,2,128,512]{3,2,1,0:T(8,128)S(1)} %get-tuple-element.38), channel_id=1, source_target_pairs={{0,32},{32,64},{64,96},{96,128},{128,160},{160,192},{192,224},{224... | collective-permute-start | bytes 1572872 | tf_op jit(solution)/shard_map/ppermute | solution.py:237
  20.4 4.3 %shard_map.64 = (bf16[2,512,1024]{2,1,0:T(8,128)(2,1)S(1)}, bf16[2,512,1024]{2,1,0:T(8,128)(2,1)S(1)}) custom-call(f32[512,3]{1,0:T(8,128)S(1)} %bitcast.27, f32[3,1024]{1,0:T(4,128)S(1)} %convert_element_type.3.vec), custom_call_target="tpu_custom_call" | custom-call | flops 4294967296 | bytes 4194304 | tf_op jit(solution)/shard_map/pallas_call | solution.py:72
  24.7 0.0 collective-permute-done.1.place
  24.7 0.0 copy-start.1
  24.7 5.5 %shard_map.65 = (bf16[2,512,1024]{2,1,0:T(8,128)(2,1)S(1)}, bf16[2,512,1024]{2,1,0:T(8,128)(2,1)S(1)}) custom-call(f32[512,3]{1,0:T(8,128)} %collective-permute-done.1.place, f32[3,1024]{1,0:T(4,128)S(1)} %convert_element_type.3.vec), custom_call_target="tpu_custom_call" | custom-call | flops 4294967296 | bytes 4194304 | tf_op jit(solution)/shard_map/pallas_call | solution.py:72
  30.3 0.0 copy-start.6
  30.3 0.0 collective-permute-done.take
  30.3 5.6 %shard_map.66 = f32[2,8,256,128]{3,2,1,0:T(8,128)S(1)} custom-call(s32[1]{0:T(128)} %bitcast.core, f32[3,1024]{1,0:T(4,128)S(1)} %convert_element_type.3.vec, f32[512,512]{1,0:T(8,128)S(1)} %bitcast.23, f32[512,256]{1,0:T(8,128)S(1)} %collective-permute-done.take, bf16[2,512,1024]{2,1,0:T(8,128)(2,1)S(1)} %get-tuple-element.21.top_a.top, ...), custom_call_target="tpu_custom_call" | custom-call | flops 3221225472 | bytes 12582912 | tf_op jit(solution)/shard_map/pallas_call | solution.py:110
  36.0 1.3 copy-done.10
  37.3 3.9 %collective-permute-done.3.down = f32[1,2,128,512]{3,2,1,0:T(8,128)S(1)} collective-permute-done((f32[1,2,128,512]{3,2,1,0:T(8,128)S(1)}, f32[1,2,128,512]{3,2,1,0:T(8,128)S(1)}, u32[]{:S(2)}, u32[]{:S(2)}) %collective-permute-start.3) | collective-permute-done | bytes 524320 | tf_op jit(solution)/shard_map/ppermute | solution.py:238
  41.2 0.0 collective-permute-done.2.up
  41.2 4.5 %all-to-all-start = ((f32[4,1024,128]{2,1,0:T(8,128)}), f32[4,1024,128]{2,1,0:T(8,128)}, u32[]{:S(2)}, u32[]{:S(2)}) async-start(f32[4,1024,128]{2,1,0:T(8,128)} %bitcast.24), calls=%async_computation | async-start | bytes 4194304 | tf_op jit(solution)/shard_map/all_to_all | solution.py:245
  45.7 0.2 pad_maximum_fusion
  45.9 1.6 fusion.2
  47.5 3.2 %collective-permute-start.5 = (f32[4,1,128,512]{3,2,1,0:T(8,128)}, f32[4,1,128,512]{3,2,1,0:T(8,128)}, u32[]{:S(2)}, u32[]{:S(2)}) collective-permute-start(f32[4,1,128,512]{3,2,1,0:T(8,128)} %get-tuple-element.35), channel_id=1, source_target_pairs={{1,0},{2,1},{3,2},{4,3},{5,4},{6,5},{7,6},{8,7},{9,8},{10,9},{11,1... | collective-permute-start | bytes 3145736 | tf_op jit(solution)/shard_map/ppermute | solution.py:238
  50.8 3.2 %collective-permute-start.4 = (f32[4,1,128,512]{3,2,1,0:T(8,128)}, f32[4,1,128,512]{3,2,1,0:T(8,128)}, u32[]{:S(2)}, u32[]{:S(2)}) collective-permute-start(f32[4,1,128,512]{3,2,1,0:T(8,128)} %get-tuple-element.36), channel_id=1, source_target_pairs={{0,1},{1,2},{2,3},{3,4},{4,5},{5,6},{6,7},{7,8},{8,9},{9,10},{10,1... | collective-permute-start | bytes 3145736 | tf_op jit(solution)/shard_map/ppermute | solution.py:237
  54.0 26.3 %all-to-all-done = f32[4,1024,128]{2,1,0:T(8,128)} async-done(((f32[4,1024,128]{2,1,0:T(8,128)}), f32[4,1024,128]{2,1,0:T(8,128)}, u32[]{:S(2)}, u32[]{:S(2)}) %all-to-all-start) | async-done | bytes 2097184 | tf_op jit(solution)/shard_map/all_to_all | solution.py:245
  80.3 2.6 %reduce_sum.27 = f32[1024,128]{1,0:T(8,128)} reduce(f32[4,1024,128]{2,1,0:T(8,128)} %all-to-all-done, f32[]{:T(128)} %constant.5.clone.1), dimensions={0}, to_apply=%region_0.0 | reduce | flops 393216 | bytes 2621444 | tf_op jit(solution)/shard_map/reduce_sum | solution.py:245
  82.9 0.0 collective-permute-done.5.right
  82.9 0.0 collective-permute-done.4.left
  82.9 4.2 %all-to-all-start.1 = ((f32[16,64,128]{2,1,0:T(8,128)}), f32[16,64,128]{2,1,0:T(8,128)}, u32[]{:S(2)}, u32[]{:S(2)}) async-start(f32[16,64,128]{2,1,0:T(8,128)} %bitcast.29), calls=%async_computation.1 | async-start | bytes 1048576 | tf_op jit(solution)/shard_map/all_to_all | solution.py:245
  87.1 0.0 copy-start.12
  87.1 1.7 copy-done.12
  88.8 6.5 %shard_map.67 = f32[2,2,128,512]{3,2,1,0:T(8,128)S(1)} custom-call(f32[2,2,9,128,128]{4,3,2,1,0:T(8,128)S(1)} %copy-done.12, f32[2,2,128,512]{3,2,1,0:T(8,128)S(1)} %fusion.own, f32[1,2,128,512]{3,2,1,0:T(8,128)S(1)} %collective-permute-done.2.up, f32[1,2,128,512]{3,2,1,0:T(8,128)S(1)} %collective-permute-done.3.down, ...), custom_call_target="tpu_custom_call" | custom-call | flops 1811939328 | bytes 8388608 | tf_op jit(solution)/shard_map/pallas_call | solution.py:195
  95.3 1.0 copy-done.11
  96.3 2.8 %all-to-all-done.1 = f32[16,64,128]{2,1,0:T(8,128)} async-done(((f32[16,64,128]{2,1,0:T(8,128)}), f32[16,64,128]{2,1,0:T(8,128)}, u32[]{:S(2)}, u32[]{:S(2)}) %all-to-all-start.1) | async-done | bytes 524320 | tf_op jit(solution)/shard_map/all_to_all | solution.py:245
  99.1 1.1 reduce_sum.28
  100.2 16.8 %all_to_all.25 = f32[4,64,128]{2,1,0:T(8,128)S(1)} all-to-all(f32[4,64,128]{2,1,0:T(8,128)S(1)} %broadcast_in_dim.8), channel_id=1, replica_groups=mesh['y'=8,'zl'=2,'x'=4,'zh'=4,'c'=2] {'zh'}, dimensions={0} | all-to-all | bytes 262144 | tf_op jit(solution)/shard_map/all_to_all | solution.py:250
  117.0 15.4 %all_to_all.26 = f32[16,64,128]{2,1,0:T(8,128)S(1)} all-to-all(f32[16,64,128]{2,1,0:T(8,128)S(1)} %broadcast_in_dim.9), channel_id=1, replica_groups=mesh['y'=8,'zl'=2,'x'=4,'zh'=4,'c'=2] {'y','zl'}, dimensions={0} | all-to-all | bytes 1048576 | tf_op jit(solution)/shard_map/all_to_all | solution.py:250
  132.4 0.1 broadcast_in_dim.22
  132.5 31.4 %all_to_all.27 = f32[4,1024,128]{2,1,0:T(8,128)S(1)} all-to-all(f32[4,1024,128]{2,1,0:T(8,128)S(1)} %broadcast_in_dim.22), channel_id=1, replica_groups=mesh['y'=8,'zl'=2,'x'=4,'zh'=4,'c'=2] {'x'}, dimensions={0} | all-to-all | bytes 4194304 | tf_op jit(solution)/shard_map/all_to_all | solution.py:250
  164.0 2.9 %shard_map.68 = f32[512,256]{1,0:T(8,128)S(1)} custom-call(bf16[2,512,1024]{2,1,0:T(8,128)(2,1)S(1)} %copy-done.7, bf16[2,512,1024]{2,1,0:T(8,128)(2,1)S(1)} %copy-done.9, f32[2,8,256,128]{3,2,1,0:T(8,128)S(1)} %bitcast.19), custom_call_target="tpu_custom_call" | custom-call | flops 1610612736 | bytes 6291456 | tf_op jit(solution)/shard_map/pallas_call | solution.py:148
  166.9 9.0 %collective-permute-start.6 = (f32[512,256]{1,0:T(8,128)S(1)}, f32[512,256]{1,0:T(8,128)S(1)}, u32[]{:S(2)}, u32[]{:S(2)}) collective-permute-start(f32[512,256]{1,0:T(8,128)S(1)} %shard_map.68), channel_id=1, source_target_pairs={{0,1},{1,0},{2,3},{3,2},{4,5},{5,4},{6,7},{7,6},{8,9},{9,8},{10,11... | collective-permute-start | bytes 1572872 | tf_op jit(solution)/shard_map/ppermute | solution.py:289
  175.9 2.9 %shard_map.69.mine = f32[512,256]{1,0:T(8,128)S(1)} custom-call(bf16[2,512,1024]{2,1,0:T(8,128)(2,1)S(1)} %copy-done.3, bf16[2,512,1024]{2,1,0:T(8,128)(2,1)S(1)} %copy-done.5, f32[2,8,256,128]{3,2,1,0:T(8,128)S(1)} %bitcast.20), custom_call_target="tpu_custom_call" | custom-call | flops 1610612736 | bytes 6291456 | tf_op jit(solution)/shard_map/pallas_call | solution.py:148
  178.8 0.8 copy-done.13
  179.6 0.0 collective-permute-done.6.theirs
  179.6 0.8 copy-done.14
  180.4 4.0 %shard_map.70 = f32[512,512]{1,0:T(8,128)} custom-call(s32[1]{0:T(128)} %bitcast.core, f32[512,512]{1,0:T(8,128)} %bitcast.25, f32[512,256]{1,0:T(8,128)} %copy-done.13, f32[512,256]{1,0:T(8,128)} %copy-done.14, f32[512,512]{1,0:T(8,128)} %bitcast.22, f32[1,512]{1,0:T(1,128)} %bitcast.30), custom_call_target="tpu_custom_call" | custom-call | tf_op jit(solution)/shard_map/pallas_call | solution.py:224
  (25 shorter events, 0.1 us)
Async XLA Ops:
  0.0 12.8 %copy-start = (f32[512,512]{1,0:T(8,128)S(1)}, f32[512,512]{1,0:T(8,128)}, u32[]{:S(2)}) copy-start(f32[512,512]{1,0:T(8,128)} %param.10) | copy-start | bytes 3145732
  0.9 23.8 %collective-permute-start.1 = (f32[512,3]{1,0:T(8,128)S(1)}, f32[512,3]{1,0:T(8,128)}, u32[]{:S(2)}, u32[]{:S(2)}) collective-permute-start(f32[512,3]{1,0:T(8,128)S(1)} %bitcast.26), channel_id=1, source_target_pairs={{0,1},{1,0},{2,3},{3,2},{4,5},{5,4},{6,7},{7,6},{8,9},{9,8},{10,11... | collective-permute-start | bytes 18440 | tf_op jit(solution)/shard_map/ppermute | solution.py:268
  10.8 9.6 %copy-start.15 = (s32[3,1024]{1,0:T(4,128)S(1)}, s32[3,1024]{1,0:T(4,128)}, u32[]{:S(2)}) copy-start(s32[3,1024]{1,0:T(4,128)} %param.9) | copy-start | bytes 36868
  10.8 19.5 %collective-permute-start = (f32[512,256]{1,0:T(8,128)S(1)}, f32[512,256]{1,0:T(8,128)S(1)}, u32[]{:S(2)}, u32[]{:S(2)}) collective-permute-start(f32[512,256]{1,0:T(8,128)S(1)} %constant_dynamic-slice_fusion), channel_id=1, source_target_pairs={{0,1},{1,0},{2,3},{3,2},{4,5},{5,4},{6,7},{7,6},{8,9},{9,8},{10,11... | collective-permute-start | bytes 1572872 | tf_op jit(solution)/shard_map/ppermute | solution.py:267
  15.1 26.1 %collective-permute-start.3 = (f32[1,2,128,512]{3,2,1,0:T(8,128)S(1)}, f32[1,2,128,512]{3,2,1,0:T(8,128)S(1)}, u32[]{:S(2)}, u32[]{:S(2)}) collective-permute-start(f32[1,2,128,512]{3,2,1,0:T(8,128)S(1)} %get-tuple-element.37), channel_id=1, source_target_pairs={{32,0},{64,32},{96,64},{128,96},{160,128},{192,160},{224,192},{256... | collective-permute-start | bytes 1572872 | tf_op jit(solution)/shard_map/ppermute | solution.py:238
  17.0 24.2 %collective-permute-start.2 = (f32[1,2,128,512]{3,2,1,0:T(8,128)S(1)}, f32[1,2,128,512]{3,2,1,0:T(8,128)S(1)}, u32[]{:S(2)}, u32[]{:S(2)}) collective-permute-start(f32[1,2,128,512]{3,2,1,0:T(8,128)S(1)} %get-tuple-element.38), channel_id=1, source_target_pairs={{0,32},{32,64},{64,96},{96,128},{128,160},{160,192},{192,224},{224... | collective-permute-start | bytes 1572872 | tf_op jit(solution)/shard_map/ppermute | solution.py:237
  24.7 5.6 %copy-start.2 = (bf16[2,512,1024]{2,1,0:T(8,128)(2,1)}, bf16[2,512,1024]{2,1,0:T(8,128)(2,1)S(1)}, u32[]{:S(2)}) copy-start(bf16[2,512,1024]{2,1,0:T(8,128)(2,1)S(1)} %get-tuple-element.21.top_a.top) | copy-start | bytes 6291460
  24.7 5.6 %copy-start.4 = (bf16[2,512,1024]{2,1,0:T(8,128)(2,1)}, bf16[2,512,1024]{2,1,0:T(8,128)(2,1)S(1)}, u32[]{:S(2)}) copy-start(bf16[2,512,1024]{2,1,0:T(8,128)(2,1)S(1)} %get-tuple-element.22.low_a.low) | copy-start | bytes 6291460
  24.7 5.6 %copy-start.1 = (f32[2,2,128,512]{3,2,1,0:T(8,128)S(1)}, f32[2,2,128,512]{3,2,1,0:T(8,128)}, u32[]{:S(2)}) copy-start(f32[2,2,128,512]{3,2,1,0:T(8,128)} %param.6) | copy-start | bytes 3145732
  30.3 5.7 %copy-start.6 = (bf16[2,512,1024]{2,1,0:T(8,128)(2,1)}, bf16[2,512,1024]{2,1,0:T(8,128)(2,1)S(1)}, u32[]{:S(2)}) copy-start(bf16[2,512,1024]{2,1,0:T(8,128)(2,1)S(1)} %get-tuple-element.24.top_b.top) | copy-start | bytes 6291460
  30.3 5.7 %copy-start.8 = (bf16[2,512,1024]{2,1,0:T(8,128)(2,1)}, bf16[2,512,1024]{2,1,0:T(8,128)(2,1)S(1)}, u32[]{:S(2)}) copy-start(bf16[2,512,1024]{2,1,0:T(8,128)(2,1)S(1)} %get-tuple-element.25.low_b.low) | copy-start | bytes 6291460
  36.0 1.3 copy-start.10
  41.2 39.1 %all-to-all-start = ((f32[4,1024,128]{2,1,0:T(8,128)}), f32[4,1024,128]{2,1,0:T(8,128)}, u32[]{:S(2)}, u32[]{:S(2)}) async-start(f32[4,1024,128]{2,1,0:T(8,128)} %bitcast.24), calls=%async_computation | async-start | bytes 4194304 | tf_op jit(solution)/shard_map/all_to_all | solution.py:245
  47.5 35.3 %collective-permute-start.5 = (f32[4,1,128,512]{3,2,1,0:T(8,128)}, f32[4,1,128,512]{3,2,1,0:T(8,128)}, u32[]{:S(2)}, u32[]{:S(2)}) collective-permute-start(f32[4,1,128,512]{3,2,1,0:T(8,128)} %get-tuple-element.35), channel_id=1, source_target_pairs={{1,0},{2,1},{3,2},{4,3},{5,4},{6,5},{7,6},{8,7},{9,8},{10,9},{11,1... | collective-permute-start | bytes 3145736 | tf_op jit(solution)/shard_map/ppermute | solution.py:238
  50.8 32.1 %collective-permute-start.4 = (f32[4,1,128,512]{3,2,1,0:T(8,128)}, f32[4,1,128,512]{3,2,1,0:T(8,128)}, u32[]{:S(2)}, u32[]{:S(2)}) collective-permute-start(f32[4,1,128,512]{3,2,1,0:T(8,128)} %get-tuple-element.36), channel_id=1, source_target_pairs={{0,1},{1,2},{2,3},{3,4},{4,5},{5,6},{6,7},{7,8},{8,9},{9,10},{10,1... | collective-permute-start | bytes 3145736 | tf_op jit(solution)/shard_map/ppermute | solution.py:237
  82.9 16.2 %all-to-all-start.1 = ((f32[16,64,128]{2,1,0:T(8,128)}), f32[16,64,128]{2,1,0:T(8,128)}, u32[]{:S(2)}, u32[]{:S(2)}) async-start(f32[16,64,128]{2,1,0:T(8,128)} %bitcast.29), calls=%async_computation.1 | async-start | bytes 1048576 | tf_op jit(solution)/shard_map/all_to_all | solution.py:245
  87.1 1.7 copy-start.12
  95.3 1.1 copy-start.11
  132.5 31.4 %copy-start.7 = (bf16[2,512,1024]{2,1,0:T(8,128)(2,1)S(1)}, bf16[2,512,1024]{2,1,0:T(8,128)(2,1)}, u32[]{:S(2)}) copy-start(bf16[2,512,1024]{2,1,0:T(8,128)(2,1)} %copy-done.6) | copy-start | bytes 6291460
  132.5 31.4 %copy-start.9 = (bf16[2,512,1024]{2,1,0:T(8,128)(2,1)S(1)}, bf16[2,512,1024]{2,1,0:T(8,128)(2,1)}, u32[]{:S(2)}) copy-start(bf16[2,512,1024]{2,1,0:T(8,128)(2,1)} %copy-done.8) | copy-start | bytes 6291460
  163.9 11.9 %copy-start.3 = (bf16[2,512,1024]{2,1,0:T(8,128)(2,1)S(1)}, bf16[2,512,1024]{2,1,0:T(8,128)(2,1)}, u32[]{:S(2)}) copy-start(bf16[2,512,1024]{2,1,0:T(8,128)(2,1)} %copy-done.2) | copy-start | bytes 6291460
  163.9 11.9 %copy-start.5 = (bf16[2,512,1024]{2,1,0:T(8,128)(2,1)S(1)}, bf16[2,512,1024]{2,1,0:T(8,128)(2,1)}, u32[]{:S(2)}) copy-start(bf16[2,512,1024]{2,1,0:T(8,128)(2,1)} %copy-done.4) | copy-start | bytes 6291460
  166.9 12.7 %collective-permute-start.6 = (f32[512,256]{1,0:T(8,128)S(1)}, f32[512,256]{1,0:T(8,128)S(1)}, u32[]{:S(2)}, u32[]{:S(2)}) collective-permute-start(f32[512,256]{1,0:T(8,128)S(1)} %shard_map.68), channel_id=1, source_target_pairs={{0,1},{1,0},{2,3},{3,2},{4,5},{5,4},{6,7},{7,6},{8,9},{9,8},{10,11... | collective-permute-start | bytes 1572872 | tf_op jit(solution)/shard_map/ppermute | solution.py:289
  178.8 0.8 copy-start.13
  179.6 0.8 copy-start.14

commit v2 on v1

--- a/solution.py
+++ b/solution.py
@@ -227,6 +227,8 @@
         in_specs=[pl.BlockSpec(memory_space=pltpu.SMEM), rows, part, part, rows, pl.BlockSpec((1, chans), lambda i: (0, 0))],
         out_specs=rows,
         out_shape=jax.ShapeDtypeStruct((atoms, chans), F32),
+        compiler_params=pltpu.CompilerParams(vmem_limit_bytes=8 * 1024 * 1024),
+        cost_estimate=pl.CostEstimate(flops=10 * atoms * chans, bytes_accessed=4 * 2**20, transcendentals=0),
     )(core, message, own, got, feat, gain)
 
 
@@ -263,27 +265,28 @@
 
     flat = features.reshape(atoms, channels)
     vec = wave_vectors.astype(F32)
-    place = positions.reshape(3, atoms).T
-    take = lax.ppermute(lax.dynamic_slice_in_dim(flat, (1 - core) * half, half, 1), "c", swap)
-    other = lax.ppermute(place, "c", swap)
     projected = jnp.einsum("abtf,fg->abtg", features, msg_weight, precision=lax.Precision.HIGH)
     up, down = neighbours(projected, SLAB_X, 0)
-    place, _ = lax.optimization_barrier((place, projected))
+    place, give, _ = lax.optimization_barrier((positions, flat, projected))
+    place = place.reshape(3, atoms).T
+    other = lax.ppermute(place, "c", swap)
+    take = lax.ppermute(lax.dynamic_slice_in_dim(give, (1 - core) * half, half, 1), "c", swap)
     mine = trig(place, vec)
     other, _ = lax.optimization_barrier((other, mine[0]))
     theirs = trig(other, vec)
     partial = structure(which, vec, flat, take, (*mine, *theirs), scale)
 
     rows, up, down = lax.optimization_barrier((partial.reshape(-1, 128), up, down))
+    rows = scatter(rows, ("x", "zl"))
+    rows, up, down = lax.optimization_barrier((rows, up, down))
     left, right = neighbours(jnp.concatenate([up, projected, down]), SLAB_Y, 1)
-    rows = scatter(rows, ("x",))
+    rows = scatter(rows, ("y",))
+    rows = jnp.sum(gather(rows, ("zh",)), axis=0)
+    rows = gather(rows, ("y",)).reshape(-1, 128)
     rows, left, right = lax.optimization_barrier((rows, left, right))
     message = neighbour_sum(tile_filter, projected, up, down, left, right)
-    rows = scatter(rows, ("y", "zl"))
-    rows, message = lax.optimization_barrier((rows, message))
-    rows = jnp.sum(gather(rows, ("zh",)), axis=0)
-    rows = gather(rows, ("y", "zl")).reshape(-1, 128)
-    coef = gather(rows, ("x",)).reshape(partial.shape)
+    coef = gather(rows, ("x", "zl")).reshape(partial.shape)
+    coef, message = lax.optimization_barrier((coef, message))
 
     given = inverse(*theirs, coef)
     got = lax.ppermute(given, "c", swap)

time: 185 us -> 183 us (0.989)
  local copies, waits for them, and re-layouts: 9.52 us -> 18.6 us
  waiting for transfers between devices: 33 us -> 24.5 us
  starting transfers between devices: 40.2 us -> 44.3 us
  Pallas kernels: 31.8 us -> 27.9 us
  blocking collectives: 63.5 us -> 61.2 us
    all_to_all x3 -> x1, blocking collectives: 63.5 us -> 32.5 us  [gather(): return lax.all_to_all(copies, axes, 0, 0, tiled=True)]
    all_to_all x2 -> x1, waiting for transfers between devices: 29.1 us -> 0.01 us  [scatter(): return jnp.sum(lax.all_to_all(parts, axes, 0, 0, tiled=True), axis=0)]
    all_to_all x0 -> x1, blocking collectives: none -> 28.8 us  [scatter(): return jnp.sum(lax.all_to_all(parts, axes, 0, 0, tiled=True), axis=0)]
    all_to_all x0 -> x2, waiting for transfers between devices: none -> 19.1 us  [gather(): return lax.all_to_all(copies, axes, 0, 0, tiled=True)]
    all_to_all x0 -> x2, starting transfers between devices: none -> 10.8 us  [gather(): return lax.all_to_all(copies, axes, 0, 0, tiled=True)]
    unnamed x33 -> x58, local copies, waits for them, and re-layouts: 6.6 us -> 14.5 us
    ppermute x1, starting transfers between devices: 8.96 us -> 2.05 us  [shards(): got = lax.ppermute(given, 'c', swap)]
    all_to_all x2 -> x1, starting transfers between devices: 8.75 us -> 5.61 us  [scatter(): return jnp.sum(lax.all_to_all(parts, axes, 0, 0, tiled=True), axis=0)]
  transfers between devices with their start and end apart: 9 -> 10, of which waited for: 3 -> 3; matrix products, arithmetic and copies ran while one was open for 4% -> 1% of each run, Pallas kernels for 13% -> 13%
where the time goes in v2:
time: 183 us; the launch traced here: 182 us
  blocking collectives  61.2 us (33%)
  starting transfers between devices  44.3 us (24%)
  Pallas kernels  27.9 us (15%)
  waiting for transfers between devices  24.5 us (13%)
  local copies, waits for them, and re-layouts  18.6 us (10%)
  other arithmetic  2.73 us (1%)
  matrix products  2.23 us (1%)
    all_to_all x1, blocking collectives, gather(): return lax.all_to_all(copies, axes, 0, 0, tiled=True)  32.5 us
    all_to_all x1, blocking collectives, scatter(): return jnp.sum(lax.all_to_all(parts, axes, 0, 0, tiled=True), axis=0)  28.8 us
    all_to_all x2, waiting for transfers between devices, gather(): return lax.all_to_all(copies, axes, 0, 0, tiled=True)  19.1 us
    unnamed x58, local copies, waits for them, and re-layouts  14.5 us
    all_to_all x2, starting transfers between devices, gather(): return lax.all_to_all(copies, axes, 0, 0, tiled=True)  10.8 us
    pallas_call x2, Pallas kernels, trig(): pl.pallas_call(functools.partial(trig_kernel, 32), grid=(count // block,)...  9.68 us
    ppermute x2, starting transfers between devices, neighbours(): lax.ppermute(tail, axis, [(i, (i + 1) % count) for i in range(count)])  9.07 us
    ppermute x1, starting transfers between devices, shards(): other = lax.ppermute(place, 'c', swap)  8.79 us
  transfers between devices with their start and end apart: 10, of which 3 were waited for; matrix products, arithmetic and copies ran while one was open for 1% of the time, Pallas kernels for 13%

profile of v2, /device:TPU:1, one launch (start us, length us, event | category | flops | bytes accessed | tf_op | source)
XLA Modules:
  0.0 181.9 jit_solution(7207987587377113607)
XLA Ops:
  0.0 1.2 copy-done
  1.2 2.2 %fusion.own = f32[2,2,128,512]{3,2,1,0:T(8,128)S(1)} fusion(f32[2,2,128,512]{3,2,1,0:T(8,128)} %param.6, f32[512,512]{1,0:T(8,128)S(1)} %copy-done), kind=kOutput, calls=%fused_computation.1 | convolution fusion | flops 805306368 | bytes 3145728 | tf_op jit(solution)/shard_map/abtf,fg->abtg/dot_general | solution.py:268
  3.5 0.0 copy-start.1
  3.5 0.0 copy-start.27
  3.5 0.1 copy.8
  3.7 8.8 %collective-permute-start.1 = (f32[512,3]{1,0:T(8,128)S(1)}, f32[512,3]{1,0:T(8,128)}, u32[]{:S(2)}, u32[]{:S(2)}) collective-permute-start(f32[512,3]{1,0:T(8,128)S(1)} %bitcast.26), channel_id=1, source_target_pairs={{0,1},{1,0},{2,3},{3,2},{4,5},{5,4},{6,7},{7,6},{8,9},{9,8},{10,11... | collective-permute-start | bytes 18440 | tf_op jit(solution)/shard_map/ppermute | solution.py:272
  12.5 1.9 %collective-permute-start = (f32[512,256]{1,0:T(8,128)S(1)}, f32[512,256]{1,0:T(8,128)S(1)}, u32[]{:S(2)}, u32[]{:S(2)}) collective-permute-start(f32[512,256]{1,0:T(8,128)S(1)} %constant_dynamic-slice_fusion), channel_id=1, source_target_pairs={{0,1},{1,0},{2,3},{3,2},{4,5},{5,4},{6,7},{7,6},{8,9},{9,8},{10,11... | collective-permute-start | bytes 1572872 | tf_op jit(solution)/shard_map/ppermute | solution.py:273
  14.5 0.1 fusion.3
  14.5 1.9 %collective-permute-start.3 = (f32[1,2,128,512]{3,2,1,0:T(8,128)S(1)}, f32[1,2,128,512]{3,2,1,0:T(8,128)S(1)}, u32[]{:S(2)}, u32[]{:S(2)}) collective-permute-start(f32[1,2,128,512]{3,2,1,0:T(8,128)S(1)} %get-tuple-element.45), channel_id=1, source_target_pairs={{32,0},{64,32},{96,64},{128,96},{160,128},{192,160},{224,192},{256... | collective-permute-start | bytes 1572872 | tf_op jit(solution)/shard_map/ppermute | solution.py:240
  16.5 3.4 %collective-permute-start.2 = (f32[1,2,128,512]{3,2,1,0:T(8,128)S(1)}, f32[1,2,128,512]{3,2,1,0:T(8,128)S(1)}, u32[]{:S(2)}, u32[]{:S(2)}) collective-permute-start(f32[1,2,128,512]{3,2,1,0:T(8,128)S(1)} %get-tuple-element.46), channel_id=1, source_target_pairs={{0,32},{32,64},{64,96},{96,128},{128,160},{160,192},{192,224},{224... | collective-permute-start | bytes 1572872 | tf_op jit(solution)/shard_map/ppermute | solution.py:239
  19.9 4.3 %shard_map.64 = (bf16[2,512,1024]{2,1,0:T(8,128)(2,1)S(1)}, bf16[2,512,1024]{2,1,0:T(8,128)(2,1)S(1)}) custom-call(f32[512,3]{1,0:T(8,128)S(1)} %bitcast.27, f32[3,1024]{1,0:T(4,128)S(1)} %convert_element_type.3.vec), custom_call_target="tpu_custom_call" | custom-call | flops 4294967296 | bytes 4194304 | tf_op jit(solution)/shard_map/pallas_call | solution.py:72
  24.2 5.4 %shard_map.65 = (bf16[2,512,1024]{2,1,0:T(8,128)(2,1)S(1)}, bf16[2,512,1024]{2,1,0:T(8,128)(2,1)S(1)}) custom-call(f32[512,3]{1,0:T(8,128)} %collective-permute-done.1.place, f32[3,1024]{1,0:T(4,128)S(1)} %convert_element_type.3.vec), custom_call_target="tpu_custom_call" | custom-call | flops 4294967296 | bytes 4194304 | tf_op jit(solution)/shard_map/pallas_call | solution.py:72
  29.6 5.6 %shard_map.66 = f32[2,8,256,128]{3,2,1,0:T(8,128)S(1)} custom-call(s32[1]{0:T(128)} %bitcast.core, f32[3,1024]{1,0:T(4,128)S(1)} %convert_element_type.3.vec, f32[512,512]{1,0:T(8,128)S(1)} %bitcast.22, f32[512,256]{1,0:T(8,128)S(1)} %collective-permute-done.take, bf16[2,512,1024]{2,1,0:T(8,128)(2,1)S(1)} %get-tuple-element.26.top_a.top, ...), custom_call_target="tpu_custom_call" | custom-call | flops 3221225472 | bytes 12582912 | tf_op jit(solution)/shard_map/pallas_call | solution.py:110
  35.3 5.4 %collective-permute-done.3.down = f32[1,2,128,512]{3,2,1,0:T(8,128)S(1)} collective-permute-done((f32[1,2,128,512]{3,2,1,0:T(8,128)S(1)}, f32[1,2,128,512]{3,2,1,0:T(8,128)S(1)}, u32[]{:S(2)}, u32[]{:S(2)}) %collective-permute-start.3) | collective-permute-done | bytes 524320 | tf_op jit(solution)/shard_map/ppermute | solution.py:240
  40.7 0.8 copy-done.16
  41.5 0.8 copy-done.19
  42.3 28.8 %all_to_all.25 = f32[8,512,128]{2,1,0:T(8,128)} all-to-all(f32[8,512,128]{2,1,0:T(8,128)S(1)} %bitcast.24), channel_id=1, replica_groups=mesh['y'=8,'zl'=2,'x'=4,'zh'=4,'c'=2] {'x','zl'}, dimensions={0} | all-to-all | bytes 4194304 | tf_op jit(solution)/shard_map/all_to_all | solution.py:247
  71.1 2.5 %reduce_sum.27 = f32[512,128]{1,0:T(8,128)} reduce(f32[8,512,128]{2,1,0:T(8,128)} %all_to_all.25, f32[]{:T(128)} %constant.5.clone.1), dimensions={0}, to_apply=%region_0.0 | reduce | flops 458752 | bytes 2359300 | tf_op jit(solution)/shard_map/reduce_sum | solution.py:247
  73.6 5.6 %all-to-all-start.1 = ((f32[8,64,128]{2,1,0:T(8,128)}), f32[8,64,128]{2,1,0:T(8,128)S(1)}, u32[]{:S(2)}, u32[]{:S(2)}) async-start(f32[8,64,128]{2,1,0:T(8,128)} %bitcast.9), calls=%async_computation.1 | async-start | bytes 524288 | tf_op jit(solution)/shard_map/all_to_all | solution.py:247
  79.2 0.2 pad_maximum_fusion
  79.4 1.6 fusion.2
  81.0 4.1 %collective-permute-start.5 = (f32[4,1,128,512]{3,2,1,0:T(8,128)}, f32[4,1,128,512]{3,2,1,0:T(8,128)S(1)}, u32[]{:S(2)}, u32[]{:S(2)}) collective-permute-start(f32[4,1,128,512]{3,2,1,0:T(8,128)} %get-tuple-element.43), channel_id=1, source_target_pairs={{1,0},{2,1},{3,2},{4,3},{5,4},{6,5},{7,6},{8,7},{9,8},{10,9},{11,1... | collective-permute-start | bytes 3145736 | tf_op jit(solution)/shard_map/ppermute | solution.py:240
  85.1 5.7 %collective-permute-start.4 = (f32[4,1,128,512]{3,2,1,0:T(8,128)}, f32[4,1,128,512]{3,2,1,0:T(8,128)S(1)}, u32[]{:S(2)}, u32[]{:S(2)}) collective-permute-start(f32[4,1,128,512]{3,2,1,0:T(8,128)} %get-tuple-element.44), channel_id=1, source_target_pairs={{0,1},{1,2},{2,3},{3,4},{4,5},{5,6},{6,7},{7,8},{8,9},{9,10},{10,1... | collective-permute-start | bytes 3145736 | tf_op jit(solution)/shard_map/ppermute | solution.py:239
  90.9 32.5 %all_to_all.26 = f32[4,64,128]{2,1,0:T(8,128)S(1)} all-to-all(f32[4,64,128]{2,1,0:T(8,128)S(1)} %broadcast_in_dim.6), channel_id=1, replica_groups=mesh['y'=8,'zl'=2,'x'=4,'zh'=4,'c'=2] {'zh'}, dimensions={0} | all-to-all | bytes 262144 | tf_op jit(solution)/shard_map/all_to_all | solution.py:252
  123.3 0.7 broadcast_in_dim.7
  124.1 6.7 %all-to-all-start.3 = ((f32[8,64,128]{2,1,0:T(8,128)}), f32[8,64,128]{2,1,0:T(8,128)S(1)}, u32[]{:S(2)}, u32[]{:S(2)}) async-start(f32[8,64,128]{2,1,0:T(8,128)} %broadcast_in_dim.7), calls=%async_computation.3 | async-start | bytes 524288 | tf_op jit(solution)/shard_map/all_to_all | solution.py:252
  130.8 9.3 %all-to-all-done.3 = f32[8,64,128]{2,1,0:T(8,128)S(1)} async-done(((f32[8,64,128]{2,1,0:T(8,128)}), f32[8,64,128]{2,1,0:T(8,128)S(1)}, u32[]{:S(2)}, u32[]{:S(2)}) %all-to-all-start.3) | async-done | bytes 262176 | tf_op jit(solution)/shard_map/all_to_all | solution.py:252
  140.1 1.5 broadcast_in_dim.8
  141.7 4.1 %all-to-all-start.4 = ((f32[8,512,128]{2,1,0:T(8,128)}), f32[8,512,128]{2,1,0:T(8,128)S(1)}, u32[]{:S(2)}, u32[]{:S(2)}) async-start(f32[8,512,128]{2,1,0:T(8,128)} %broadcast_in_dim.8), calls=%async_computation.4 | async-start | bytes 4194304 | tf_op jit(solution)/shard_map/all_to_all | solution.py:252
  145.7 1.2 copy-done.2
  147.0 1.7 copy-done.15
  148.6 1.0 copy-done.18
  149.7 1.0 copy-done.21
  150.7 1.2 copy-done.23
  151.9 1.2 copy-done.25
  153.2 4.9 %shard_map.67 = f32[2,2,128,512]{3,2,1,0:T(8,128)S(1)} custom-call(f32[2,2,9,128,128]{4,3,2,1,0:T(8,128)S(1)} %copy-done.15, f32[2,2,128,512]{3,2,1,0:T(8,128)S(1)} %copy-done.2, f32[1,2,128,512]{3,2,1,0:T(8,128)S(1)} %copy-done.21, f32[1,2,128,512]{3,2,1,0:T(8,128)S(1)} %copy-done.18, f32[4,1,128,512]{3,2,1,0:T(8,128)S(1)} %copy-done.25, ...), custom_call_target="tpu_custom_call" | custom-call | flops 1811939328 | bytes 8388608 | tf_op jit(solution)/shard_map/pallas_call | solution.py:195
  158.1 0.0 copy-start.13
  158.1 1.0 copy-done.13
  159.1 9.8 %all-to-all-done.4 = f32[8,512,128]{2,1,0:T(8,128)S(1)} async-done(((f32[8,512,128]{2,1,0:T(8,128)}), f32[8,512,128]{2,1,0:T(8,128)S(1)}, u32[]{:S(2)}, u32[]{:S(2)}) %all-to-all-start.4) | async-done | bytes 2097184 | tf_op jit(solution)/shard_map/all_to_all | solution.py:252
  168.8 1.6 copy-done.10
  170.4 1.6 copy-done.12
  172.0 2.9 %shard_map.68 = f32[512,256]{1,0:T(8,128)S(1)} custom-call(bf16[2,512,1024]{2,1,0:T(8,128)(2,1)S(1)} %copy-done.10, bf16[2,512,1024]{2,1,0:T(8,128)(2,1)S(1)} %copy-done.12, f32[2,8,256,128]{3,2,1,0:T(8,128)S(1)} %bitcast.19), custom_call_target="tpu_custom_call" | custom-call | flops 1610612736 | bytes 6291456 | tf_op jit(solution)/shard_map/pallas_call | solution.py:148
  174.9 0.0 copy-start.4
  174.9 0.0 copy-start.14
  174.9 0.0 copy-start.26
  175.0 2.1 %collective-permute-start.6 = (f32[512,256]{1,0:T(8,128)S(1)}, f32[512,256]{1,0:T(8,128)S(1)}, u32[]{:S(2)}, u32[]{:S(2)}) collective-permute-start(f32[512,256]{1,0:T(8,128)S(1)} %shard_map.68), channel_id=1, source_target_pairs={{0,1},{1,0},{2,3},{3,2},{4,5},{5,4},{6,7},{7,6},{8,9},{9,8},{10,11... | collective-permute-start | bytes 1572872 | tf_op jit(solution)/shard_map/ppermute | solution.py:292
  177.0 2.9 %shard_map.69.mine = f32[512,256]{1,0:T(8,128)S(1)} custom-call(bf16[2,512,1024]{2,1,0:T(8,128)(2,1)S(1)} %copy-done.6, bf16[2,512,1024]{2,1,0:T(8,128)(2,1)S(1)} %copy-done.8, f32[2,8,256,128]{3,2,1,0:T(8,128)S(1)} %bitcast.20), custom_call_target="tpu_custom_call" | custom-call | flops 1610612736 | bytes 6291456 | tf_op jit(solution)/shard_map/pallas_call | solution.py:148
  180.0 1.9 %shard_map.70 = f32[512,512]{1,0:T(8,128)} custom-call(s32[1]{0:T(128)} %bitcast.core, f32[512,512]{1,0:T(8,128)S(1)} %bitcast.25, f32[512,256]{1,0:T(8,128)S(1)} %shard_map.69.mine, f32[512,256]{1,0:T(8,128)S(1)} %collective-permute-done.6.theirs, f32[512,512]{1,0:T(8,128)S(1)} %bitcast.23, f32[1,512]{1,0:T(1,128)S(1)} %bitcast.28), custom_call_target="tpu_custom_call" | custom-call | flops 2621440 | bytes 4194304 | tf_op jit(solution)/shard_map/pallas_call | solution.py:224
  (52 shorter events, 0.2 us)
Async XLA Ops:
  0.0 1.2 copy-start
  0.0 12.5 %copy-start.3 = (f32[2,2,128,512]{3,2,1,0:T(8,128)S(1)}, f32[2,2,128,512]{3,2,1,0:T(8,128)}, u32[]{:S(2)}) copy-start(f32[2,2,128,512]{3,2,1,0:T(8,128)} %param.6) | copy-start | bytes 3145732
  0.0 3.5 %copy-start.28 = (f32[3,2,2,128]{3,2,1,0:T(2,128)S(1)}, f32[3,2,2,128]{3,2,1,0:T(2,128)}, u32[]{:S(2)}) copy-start(f32[3,2,2,128]{3,2,1,0:T(2,128)} %param.8) | copy-start | bytes 18436
  3.5 75.7 %copy-start.1 = (f32[2,2,128,512]{3,2,1,0:T(8,128)}, f32[2,2,128,512]{3,2,1,0:T(8,128)S(1)}, u32[]{:S(2)}) copy-start(f32[2,2,128,512]{3,2,1,0:T(8,128)S(1)} %fusion.own) | copy-start | bytes 3145732
  3.5 16.3 %copy-start.27 = (s32[3,1024]{1,0:T(4,128)S(1)}, s32[3,1024]{1,0:T(4,128)}, u32[]{:S(2)}) copy-start(s32[3,1024]{1,0:T(4,128)} %param.9) | copy-start | bytes 36868
  3.7 20.5 %collective-permute-start.1 = (f32[512,3]{1,0:T(8,128)S(1)}, f32[512,3]{1,0:T(8,128)}, u32[]{:S(2)}, u32[]{:S(2)}) collective-permute-start(f32[512,3]{1,0:T(8,128)S(1)} %bitcast.26), channel_id=1, source_target_pairs={{0,1},{1,0},{2,3},{3,2},{4,5},{5,4},{6,7},{7,6},{8,9},{9,8},{10,11... | collective-permute-start | bytes 18440 | tf_op jit(solution)/shard_map/ppermute | solution.py:272
  12.5 17.1 %collective-permute-start = (f32[512,256]{1,0:T(8,128)S(1)}, f32[512,256]{1,0:T(8,128)S(1)}, u32[]{:S(2)}, u32[]{:S(2)}) collective-permute-start(f32[512,256]{1,0:T(8,128)S(1)} %constant_dynamic-slice_fusion), channel_id=1, source_target_pairs={{0,1},{1,0},{2,3},{3,2},{4,5},{5,4},{6,7},{7,6},{8,9},{9,8},{10,11... | collective-permute-start | bytes 1572872 | tf_op jit(solution)/shard_map/ppermute | solution.py:273
  14.5 26.1 %collective-permute-start.3 = (f32[1,2,128,512]{3,2,1,0:T(8,128)S(1)}, f32[1,2,128,512]{3,2,1,0:T(8,128)S(1)}, u32[]{:S(2)}, u32[]{:S(2)}) collective-permute-start(f32[1,2,128,512]{3,2,1,0:T(8,128)S(1)} %get-tuple-element.45), channel_id=1, source_target_pairs={{32,0},{64,32},{96,64},{128,96},{160,128},{192,160},{224,192},{256... | collective-permute-start | bytes 1572872 | tf_op jit(solution)/shard_map/ppermute | solution.py:240
  16.5 25.0 %collective-permute-start.2 = (f32[1,2,128,512]{3,2,1,0:T(8,128)S(1)}, f32[1,2,128,512]{3,2,1,0:T(8,128)S(1)}, u32[]{:S(2)}, u32[]{:S(2)}) collective-permute-start(f32[1,2,128,512]{3,2,1,0:T(8,128)S(1)} %get-tuple-element.46), channel_id=1, source_target_pairs={{0,32},{32,64},{64,96},{96,128},{128,160},{160,192},{192,224},{224... | collective-permute-start | bytes 1572872 | tf_op jit(solution)/shard_map/ppermute | solution.py:239
  24.1 5.5 %copy-start.5 = (bf16[2,512,1024]{2,1,0:T(8,128)(2,1)}, bf16[2,512,1024]{2,1,0:T(8,128)(2,1)S(1)}, u32[]{:S(2)}) copy-start(bf16[2,512,1024]{2,1,0:T(8,128)(2,1)S(1)} %get-tuple-element.26.top_a.top) | copy-start | bytes 6291460
  24.1 5.5 %copy-start.7 = (bf16[2,512,1024]{2,1,0:T(8,128)(2,1)}, bf16[2,512,1024]{2,1,0:T(8,128)(2,1)S(1)}, u32[]{:S(2)}) copy-start(bf16[2,512,1024]{2,1,0:T(8,128)(2,1)S(1)} %get-tuple-element.27.low_a.low) | copy-start | bytes 6291460
  29.6 5.7 %copy-start.9 = (bf16[2,512,1024]{2,1,0:T(8,128)(2,1)}, bf16[2,512,1024]{2,1,0:T(8,128)(2,1)S(1)}, u32[]{:S(2)}) copy-start(bf16[2,512,1024]{2,1,0:T(8,128)(2,1)S(1)} %get-tuple-element.29.top_b.top) | copy-start | bytes 6291460
  29.6 5.7 %copy-start.11 = (bf16[2,512,1024]{2,1,0:T(8,128)(2,1)}, bf16[2,512,1024]{2,1,0:T(8,128)(2,1)S(1)}, u32[]{:S(2)}) copy-start(bf16[2,512,1024]{2,1,0:T(8,128)(2,1)S(1)} %get-tuple-element.30.low_b.low) | copy-start | bytes 6291460
  40.7 0.8 copy-start.16
  41.5 0.8 copy-start.19
  71.1 8.1 %copy-start.17 = (f32[1,2,128,512]{3,2,1,0:T(8,128)S(1)}, f32[1,2,128,512]{3,2,1,0:T(8,128)}, u32[]{:S(2)}) copy-start(f32[1,2,128,512]{3,2,1,0:T(8,128)} %copy-done.16) | copy-start | bytes 1572868
  71.1 8.1 %copy-start.20 = (f32[1,2,128,512]{3,2,1,0:T(8,128)S(1)}, f32[1,2,128,512]{3,2,1,0:T(8,128)}, u32[]{:S(2)}) copy-start(f32[1,2,128,512]{3,2,1,0:T(8,128)} %copy-done.19) | copy-start | bytes 1572868
  73.6 17.2 %all-to-all-start.1 = ((f32[8,64,128]{2,1,0:T(8,128)}), f32[8,64,128]{2,1,0:T(8,128)S(1)}, u32[]{:S(2)}, u32[]{:S(2)}) async-start(f32[8,64,128]{2,1,0:T(8,128)} %bitcast.9), calls=%async_computation.1 | async-start | bytes 524288 | tf_op jit(solution)/shard_map/all_to_all | solution.py:247
  81.0 49.8 %collective-permute-start.5 = (f32[4,1,128,512]{3,2,1,0:T(8,128)}, f32[4,1,128,512]{3,2,1,0:T(8,128)S(1)}, u32[]{:S(2)}, u32[]{:S(2)}) collective-permute-start(f32[4,1,128,512]{3,2,1,0:T(8,128)} %get-tuple-element.43), channel_id=1, source_target_pairs={{1,0},{2,1},{3,2},{4,3},{5,4},{6,5},{7,6},{8,7},{9,8},{10,9},{11,1... | collective-permute-start | bytes 3145736 | tf_op jit(solution)/shard_map/ppermute | solution.py:240
  85.1 45.7 %collective-permute-start.4 = (f32[4,1,128,512]{3,2,1,0:T(8,128)}, f32[4,1,128,512]{3,2,1,0:T(8,128)S(1)}, u32[]{:S(2)}, u32[]{:S(2)}) collective-permute-start(f32[4,1,128,512]{3,2,1,0:T(8,128)} %get-tuple-element.44), channel_id=1, source_target_pairs={{0,1},{1,2},{2,3},{3,4},{4,5},{5,6},{6,7},{7,8},{8,9},{9,10},{10,1... | collective-permute-start | bytes 3145736 | tf_op jit(solution)/shard_map/ppermute | solution.py:239
  124.1 16.1 %all-to-all-start.3 = ((f32[8,64,128]{2,1,0:T(8,128)}), f32[8,64,128]{2,1,0:T(8,128)S(1)}, u32[]{:S(2)}, u32[]{:S(2)}) async-start(f32[8,64,128]{2,1,0:T(8,128)} %broadcast_in_dim.7), calls=%async_computation.3 | async-start | bytes 524288 | tf_op jit(solution)/shard_map/all_to_all | solution.py:252
  130.8 10.9 %copy-start.22 = (f32[4,1,128,512]{3,2,1,0:T(8,128)}, f32[4,1,128,512]{3,2,1,0:T(8,128)S(1)}, u32[]{:S(2)}) copy-start(f32[4,1,128,512]{3,2,1,0:T(8,128)S(1)} %collective-permute-done.5.right) | copy-start | bytes 3145732
  130.8 10.8 %copy-start.24 = (f32[4,1,128,512]{3,2,1,0:T(8,128)}, f32[4,1,128,512]{3,2,1,0:T(8,128)S(1)}, u32[]{:S(2)}) copy-start(f32[4,1,128,512]{3,2,1,0:T(8,128)S(1)} %collective-permute-done.4.left) | copy-start | bytes 3145732
  141.7 27.2 %all-to-all-start.4 = ((f32[8,512,128]{2,1,0:T(8,128)}), f32[8,512,128]{2,1,0:T(8,128)S(1)}, u32[]{:S(2)}, u32[]{:S(2)}) async-start(f32[8,512,128]{2,1,0:T(8,128)} %broadcast_in_dim.8), calls=%async_computation.4 | async-start | bytes 4194304 | tf_op jit(solution)/shard_map/all_to_all | solution.py:252
  145.7 1.2 copy-start.2
  147.0 1.7 copy-start.15
  148.6 1.0 copy-start.18
  149.7 1.0 copy-start.21
  150.7 1.2 copy-start.23
  151.9 1.2 copy-start.25
  158.1 1.0 copy-start.13
  168.8 1.6 copy-start.10
  170.4 1.6 copy-start.12
  172.0 5.0 %copy-start.6 = (bf16[2,512,1024]{2,1,0:T(8,128)(2,1)S(1)}, bf16[2,512,1024]{2,1,0:T(8,128)(2,1)}, u32[]{:S(2)}) copy-start(bf16[2,512,1024]{2,1,0:T(8,128)(2,1)} %copy-done.5) | copy-start | bytes 6291460
  172.0 5.0 %copy-start.8 = (bf16[2,512,1024]{2,1,0:T(8,128)(2,1)S(1)}, bf16[2,512,1024]{2,1,0:T(8,128)(2,1)}, u32[]{:S(2)}) copy-start(bf16[2,512,1024]{2,1,0:T(8,128)(2,1)} %copy-done.7) | copy-start | bytes 6291460
  174.9 5.0 %copy-start.4 = (f32[2,2,128,512]{3,2,1,0:T(8,128)S(1)}, f32[2,2,128,512]{3,2,1,0:T(8,128)}, u32[]{:S(2)}) copy-start(f32[2,2,128,512]{3,2,1,0:T(8,128)} %param.6) | copy-start | bytes 3145732
  174.9 5.0 %copy-start.14 = (f32[2,2,128,512]{3,2,1,0:T(8,128)S(1)}, f32[2,2,128,512]{3,2,1,0:T(8,128)}, u32[]{:S(2)}) copy-start(f32[2,2,128,512]{3,2,1,0:T(8,128)} %copy-done.13) | copy-start | bytes 3145732
  174.9 5.0 %copy-start.26 = (f32[512]{0:T(512)S(1)}, f32[512]{0:T(512)}, u32[]{:S(2)}) copy-start(f32[512]{0:T(512)} %param.11) | copy-start | bytes 6148
  175.0 5.0 %collective-permute-start.6 = (f32[512,256]{1,0:T(8,128)S(1)}, f32[512,256]{1,0:T(8,128)S(1)}, u32[]{:S(2)}, u32[]{:S(2)}) collective-permute-start(f32[512,256]{1,0:T(8,128)S(1)} %shard_map.68), channel_id=1, source_target_pairs={{0,1},{1,0},{2,3},{3,2},{4,5},{5,4},{6,7},{7,6},{8,9},{9,8},{10,11... | collective-permute-start | bytes 1572872 | tf_op jit(solution)/shard_map/ppermute | solution.py:292

commit v3 on v1

--- a/solution.py
+++ b/solution.py
@@ -13,7 +13,7 @@
 NN = (((1,), (0,)), ((), ()))
 NT = (((1,), (1,)), ((), ()))
 SLAB_X, SLAB_Y = ("y", "zl"), ("x", "zh", "c")
-VMEM_LIMIT = 24 * 1024 * 1024
+VMEM_LIMIT = 16 * 1024 * 1024
 
 
 def halves(value):
@@ -76,7 +76,7 @@
         out_specs=[spec, spec],
         out_shape=[shape, shape],
         scratch_shapes=[pltpu.VMEM((atoms, 9), BF16), pltpu.VMEM((atoms, block), F32)],
-        compiler_params=pltpu.CompilerParams(vmem_limit_bytes=VMEM_LIMIT),
+        compiler_params=pltpu.CompilerParams(vmem_limit_bytes=VMEM_LIMIT // 2),
         cost_estimate=pl.CostEstimate(flops=4 * 2**30, bytes_accessed=4 * 2**20, transcendentals=0),
     )(place, vec)
 
@@ -200,7 +200,7 @@
         out_specs=pl.BlockSpec((1, 1, rows, chans), lambda i, j: (i, j, 0, 0)),
         out_shape=jax.ShapeDtypeStruct(own.shape, F32),
         scratch_shapes=[pltpu.VMEM((tiles_x + 2, tiles_y + 2, rows, chans), BF16)] * 2,
-        compiler_params=pltpu.CompilerParams(vmem_limit_bytes=VMEM_LIMIT),
+        compiler_params=pltpu.CompilerParams(vmem_limit_bytes=VMEM_LIMIT * 5 // 4),
         cost_estimate=pl.CostEstimate(
             flops=6 * tiles_x * tiles_y * 9 * rows * rows * chans, bytes_accessed=8 * 2**20, transcendentals=0
         ),
@@ -227,6 +227,8 @@
         in_specs=[pl.BlockSpec(memory_space=pltpu.SMEM), rows, part, part, rows, pl.BlockSpec((1, chans), lambda i: (0, 0))],
         out_specs=rows,
         out_shape=jax.ShapeDtypeStruct((atoms, chans), F32),
+        compiler_params=pltpu.CompilerParams(vmem_limit_bytes=8 * 1024 * 1024),
+        cost_estimate=pl.CostEstimate(flops=10 * atoms * chans, bytes_accessed=4 * 2**20, transcendentals=0),
     )(core, message, own, got, feat, gain)
 
 
@@ -264,25 +266,25 @@
     flat = features.reshape(atoms, channels)
     vec = wave_vectors.astype(F32)
     place = positions.reshape(3, atoms).T
+    other = lax.ppermute(place, "c", swap)
     take = lax.ppermute(lax.dynamic_slice_in_dim(flat, (1 - core) * half, half, 1), "c", swap)
-    other = lax.ppermute(place, "c", swap)
-    projected = jnp.einsum("abtf,fg->abtg", features, msg_weight, precision=lax.Precision.HIGH)
-    up, down = neighbours(projected, SLAB_X, 0)
-    place, _ = lax.optimization_barrier((place, projected))
     mine = trig(place, vec)
     other, _ = lax.optimization_barrier((other, mine[0]))
     theirs = trig(other, vec)
     partial = structure(which, vec, flat, take, (*mine, *theirs), scale)
 
-    rows, up, down = lax.optimization_barrier((partial.reshape(-1, 128), up, down))
+    rows, cells = lax.optimization_barrier((partial.reshape(-1, 128), features))
+    projected = jnp.einsum("abtf,fg->abtg", cells, msg_weight, precision=lax.Precision.HIGH)
+    up, down = neighbours(projected, SLAB_X, 0)
     left, right = neighbours(jnp.concatenate([up, projected, down]), SLAB_Y, 1)
     rows = scatter(rows, ("x",))
+    rows, up, down = lax.optimization_barrier((rows, up, down))
+    rows = scatter(rows, ("y", "zl"))
     rows, left, right = lax.optimization_barrier((rows, left, right))
     message = neighbour_sum(tile_filter, projected, up, down, left, right)
-    rows = scatter(rows, ("y", "zl"))
-    rows, message = lax.optimization_barrier((rows, message))
     rows = jnp.sum(gather(rows, ("zh",)), axis=0)
     rows = gather(rows, ("y", "zl")).reshape(-1, 128)
+    rows, message = lax.optimization_barrier((rows, message))
     coef = gather(rows, ("x",)).reshape(partial.shape)
 
     given = inverse(*theirs, coef)

time: 185 us -> 184 us (level)
  waiting for transfers between devices: 33 us -> 21.6 us
  blocking collectives: 63.5 us -> 73.8 us
  Pallas kernels: 31.8 us -> 28.3 us
  local copies, waits for them, and re-layouts: 9.52 us -> 11.8 us
    all_to_all x2 -> x1, waiting for transfers between devices: 29.1 us -> 0.01 us  [scatter(): return jnp.sum(lax.all_to_all(parts, axes, 0, 0, tiled=True), axis=0)]
    all_to_all x0 -> x1, blocking collectives: none -> 19.2 us  [scatter(): return jnp.sum(lax.all_to_all(parts, axes, 0, 0, tiled=True), axis=0)]
    ppermute x2, waiting for transfers between devices: 3.91 us -> 20.8 us  [neighbours(): lax.ppermute(head, axis, [((i + 1) % count, i) for i in range(count)])]
    all_to_all x3 -> x2, blocking collectives: 63.5 us -> 54.6 us  [gather(): return lax.all_to_all(copies, axes, 0, 0, tiled=True)]
    all_to_all x0 -> x1, starting transfers between devices: none -> 8.86 us  [gather(): return lax.all_to_all(copies, axes, 0, 0, tiled=True)]
    all_to_all x2 -> x1, starting transfers between devices: 8.75 us -> 4.51 us  [scatter(): return jnp.sum(lax.all_to_all(parts, axes, 0, 0, tiled=True), axis=0)]
    ppermute x1, starting transfers between devices: 8.96 us -> 6.02 us  [shards(): got = lax.ppermute(given, 'c', swap)]
    pallas_call x1, Pallas kernels: 4.05 us -> 1.91 us  [update(): pl.pallas_call(update_kernel, grid=(atoms // block,), in_specs=[pl.BlockS...]
  transfers between devices with their start and end apart: 9 -> 9, of which waited for: 3 -> 2; matrix products, arithmetic and copies ran while one was open for 4% -> 5% of each run, Pallas kernels for 13% -> 10%
where the time goes in v3:
time: 184 us; the launch traced here: 183 us
  blocking collectives  73.8 us (40%)
  starting transfers between devices  41.8 us (23%)
  Pallas kernels  28.3 us (15%)
  waiting for transfers between devices  21.6 us (12%)
  local copies, waits for them, and re-layouts  11.8 us (6%)
  other arithmetic  4.57 us (2%)
    all_to_all x2, blocking collectives, gather(): return lax.all_to_all(copies, axes, 0, 0, tiled=True)  54.6 us
    ppermute x2, waiting for transfers between devices, neighbours(): lax.ppermute(head, axis, [((i + 1) % count, i) for i in range(count)])  20.8 us
    all_to_all x1, blocking collectives, scatter(): return jnp.sum(lax.all_to_all(parts, axes, 0, 0, tiled=True), axis=0)  19.2 us
    all_to_all x1, starting transfers between devices, gather(): return lax.all_to_all(copies, axes, 0, 0, tiled=True)  8.86 us
    ppermute x1, starting transfers between devices, shards(): other = lax.ppermute(place, 'c', swap)  8.79 us
    pallas_call x2, Pallas kernels, trig(): pl.pallas_call(functools.partial(trig_kernel, 32), grid=(count // block,)...  8.5 us
    unnamed x39, local copies, waits for them, and re-layouts  7.03 us
    ppermute x2, starting transfers between devices, neighbours(): lax.ppermute(tail, axis, [(i, (i + 1) % count) for i in range(count)])  6.56 us
  transfers between devices with their start and end apart: 9, of which 2 were waited for; matrix products, arithmetic and copies ran while one was open for 5% of the time, Pallas kernels for 10%

profile of v3, /device:TPU:1, one launch (start us, length us, event | category | flops | bytes accessed | tf_op | source)
XLA Modules:
  0.0 183.3 jit_solution(3694860137012812423)
XLA Ops:
  0.0 0.9 copy.8
  0.9 8.8 %collective-permute-start.1 = (f32[512,3]{1,0:T(8,128)S(1)}, f32[512,3]{1,0:T(8,128)S(1)}, u32[]{:S(2)}, u32[]{:S(2)}) collective-permute-start(f32[512,3]{1,0:T(8,128)S(1)} %bitcast.26), channel_id=1, source_target_pairs={{0,1},{1,0},{2,3},{3,2},{4,5},{5,4},{6,7},{7,6},{8,9},{9,8},{10,11... | collective-permute-start | bytes 18440 | tf_op jit(solution)/shard_map/ppermute | solution.py:269
  9.7 1.1 constant_dynamic-slice_fusion
  10.8 1.9 %collective-permute-start = (f32[512,256]{1,0:T(8,128)S(1)}, f32[512,256]{1,0:T(8,128)S(1)}, u32[]{:S(2)}, u32[]{:S(2)}) collective-permute-start(f32[512,256]{1,0:T(8,128)S(1)} %constant_dynamic-slice_fusion), channel_id=1, source_target_pairs={{0,1},{1,0},{2,3},{3,2},{4,5},{5,4},{6,7},{7,6},{8,9},{9,8},{10,11... | collective-permute-start | bytes 1572872 | tf_op jit(solution)/shard_map/ppermute | solution.py:270
  12.7 0.7 convert_element_type.3.vec
  13.5 4.2 %shard_map.64 = (bf16[2,512,1024]{2,1,0:T(8,128)(2,1)S(1)}, bf16[2,512,1024]{2,1,0:T(8,128)(2,1)S(1)}) custom-call(f32[512,3]{1,0:T(8,128)S(1)} %bitcast.27, f32[3,1024]{1,0:T(4,128)S(1)} %convert_element_type.3.vec), custom_call_target="tpu_custom_call" | custom-call | flops 4294967296 | bytes 4194304 | tf_op jit(solution)/shard_map/pallas_call | solution.py:72
  17.7 0.0 collective-permute-done.1.place
  17.7 0.0 copy-start.1
  17.8 4.3 %shard_map.65 = (bf16[2,512,1024]{2,1,0:T(8,128)(2,1)S(1)}, bf16[2,512,1024]{2,1,0:T(8,128)(2,1)S(1)}) custom-call(f32[512,3]{1,0:T(8,128)S(1)} %collective-permute-done.1.place, f32[3,1024]{1,0:T(4,128)S(1)} %convert_element_type.3.vec), custom_call_target="tpu_custom_call" | custom-call | flops 4294967296 | bytes 4194304 | tf_op jit(solution)/shard_map/pallas_call | solution.py:72
  22.0 0.0 collective-permute-done.take
  22.1 5.6 %shard_map.66 = f32[2,8,256,128]{3,2,1,0:T(8,128)S(1)} custom-call(s32[1]{0:T(128)} %bitcast.core, f32[3,1024]{1,0:T(4,128)S(1)} %convert_element_type.3.vec, f32[512,512]{1,0:T(8,128)S(1)} %bitcast.22, f32[512,256]{1,0:T(8,128)S(1)} %collective-permute-done.take, bf16[2,512,1024]{2,1,0:T(8,128)(2,1)S(1)} %get-tuple-element.21.top_a.top, ...), custom_call_target="tpu_custom_call" | custom-call | flops 3221225472 | bytes 12582912 | tf_op jit(solution)/shard_map/pallas_call | solution.py:110
  27.7 1.3 copy-done.10
  29.1 4.5 %all-to-all-start = ((f32[4,1024,128]{2,1,0:T(8,128)}), f32[4,1024,128]{2,1,0:T(8,128)}, u32[]{:S(2)}, u32[]{:S(2)}) async-start(f32[4,1024,128]{2,1,0:T(8,128)} %bitcast.24), calls=%async_computation | async-start | bytes 4194304 | tf_op jit(solution)/shard_map/all_to_all | solution.py:247
  33.6 1.0 fusion.own
  34.6 0.1 fusion.3
  34.7 1.9 %collective-permute-start.3 = (f32[1,2,128,512]{3,2,1,0:T(8,128)S(1)}, f32[1,2,128,512]{3,2,1,0:T(8,128)S(1)}, u32[]{:S(2)}, u32[]{:S(2)}) collective-permute-start(f32[1,2,128,512]{3,2,1,0:T(8,128)S(1)} %get-tuple-element.39), channel_id=1, source_target_pairs={{32,0},{64,32},{96,64},{128,96},{160,128},{192,160},{224,192},{256... | collective-permute-start | bytes 1572872 | tf_op jit(solution)/shard_map/ppermute | solution.py:240
  36.6 3.4 %collective-permute-start.2 = (f32[1,2,128,512]{3,2,1,0:T(8,128)S(1)}, f32[1,2,128,512]{3,2,1,0:T(8,128)S(1)}, u32[]{:S(2)}, u32[]{:S(2)}) collective-permute-start(f32[1,2,128,512]{3,2,1,0:T(8,128)S(1)} %get-tuple-element.40), channel_id=1, source_target_pairs={{0,32},{32,64},{64,96},{96,128},{128,160},{160,192},{192,224},{224... | collective-permute-start | bytes 1572872 | tf_op jit(solution)/shard_map/ppermute | solution.py:239
  40.0 20.8 %collective-permute-done.3.down = f32[1,2,128,512]{3,2,1,0:T(8,128)S(1)} collective-permute-done((f32[1,2,128,512]{3,2,1,0:T(8,128)S(1)}, f32[1,2,128,512]{3,2,1,0:T(8,128)S(1)}, u32[]{:S(2)}, u32[]{:S(2)}) %collective-permute-start.3) | collective-permute-done | bytes 524320 | tf_op jit(solution)/shard_map/ppermute | solution.py:240
  60.8 0.0 collective-permute-done.2.up
  60.8 0.2 pad_maximum_fusion
  61.0 1.6 fusion.2
  62.6 3.3 %collective-permute-start.5 = (f32[4,1,128,512]{3,2,1,0:T(8,128)}, f32[4,1,128,512]{3,2,1,0:T(8,128)}, u32[]{:S(2)}, u32[]{:S(2)}) collective-permute-start(f32[4,1,128,512]{3,2,1,0:T(8,128)} %get-tuple-element.37), channel_id=1, source_target_pairs={{1,0},{2,1},{3,2},{4,3},{5,4},{6,5},{7,6},{8,7},{9,8},{10,9},{11,1... | collective-permute-start | bytes 3145736 | tf_op jit(solution)/shard_map/ppermute | solution.py:240
  65.9 3.2 %collective-permute-start.4 = (f32[4,1,128,512]{3,2,1,0:T(8,128)}, f32[4,1,128,512]{3,2,1,0:T(8,128)}, u32[]{:S(2)}, u32[]{:S(2)}) collective-permute-start(f32[4,1,128,512]{3,2,1,0:T(8,128)} %get-tuple-element.38), channel_id=1, source_target_pairs={{0,1},{1,2},{2,3},{3,4},{4,5},{5,6},{6,7},{7,8},{8,9},{9,10},{10,1... | collective-permute-start | bytes 3145736 | tf_op jit(solution)/shard_map/ppermute | solution.py:239
  69.1 0.0 all-to-all-done
  69.1 2.6 %reduce_sum.27 = f32[1024,128]{1,0:T(8,128)} reduce(f32[4,1024,128]{2,1,0:T(8,128)} %all-to-all-done, f32[]{:T(128)} %constant.5.clone.1), dimensions={0}, to_apply=%region_0.0 | reduce | flops 393216 | bytes 2621444 | tf_op jit(solution)/shard_map/reduce_sum | solution.py:247
  71.7 19.2 %all_to_all.25 = f32[16,64,128]{2,1,0:T(8,128)} all-to-all(f32[16,64,128]{2,1,0:T(8,128)} %bitcast.29), channel_id=1, replica_groups=mesh['y'=8,'zl'=2,'x'=4,'zh'=4,'c'=2] {'y','zl'}, dimensions={0} | all-to-all | bytes 1048576 | tf_op jit(solution)/shard_map/all_to_all | solution.py:247
  90.8 1.1 reduce_sum.28
  91.9 0.0 collective-permute-done.5.right
  91.9 0.0 collective-permute-done.4.left
  92.0 21.7 %all_to_all.26 = f32[4,64,128]{2,1,0:T(8,128)S(1)} all-to-all(f32[4,64,128]{2,1,0:T(8,128)S(1)} %broadcast_in_dim.6), channel_id=1, replica_groups=mesh['y'=8,'zl'=2,'x'=4,'zh'=4,'c'=2] {'zh'}, dimensions={0} | all-to-all | bytes 262144 | tf_op jit(solution)/shard_map/all_to_all | solution.py:252
  113.7 0.9 broadcast_in_dim.7
  114.5 8.9 %all-to-all-start.3 = ((f32[16,64,128]{2,1,0:T(8,128)}), f32[16,64,128]{2,1,0:T(8,128)}, u32[]{:S(2)}, u32[]{:S(2)}) async-start(f32[16,64,128]{2,1,0:T(8,128)} %broadcast_in_dim.7), calls=%async_computation.3 | async-start | bytes 1048576 | tf_op jit(solution)/shard_map/all_to_all | solution.py:252
  123.4 0.0 copy-start.13
  123.4 1.7 copy-done.13
  125.1 1.0 copy-done.15
  126.1 1.0 copy-done.17
  127.2 6.5 %shard_map.67 = f32[2,2,128,512]{3,2,1,0:T(8,128)S(1)} custom-call(f32[2,2,9,128,128]{4,3,2,1,0:T(8,128)S(1)} %copy-done.13, f32[2,2,128,512]{3,2,1,0:T(8,128)S(1)} %fusion.own, f32[1,2,128,512]{3,2,1,0:T(8,128)S(1)} %copy-done.17, f32[1,2,128,512]{3,2,1,0:T(8,128)S(1)} %copy-done.15, f32[4,1,128,512]{3,2,1,0:T(8,128)} %collective-permute-done.4.left, ...), custom_call_target="tpu_custom_call" | custom-call | flops 1811939328 | bytes 8388608 | tf_op jit(solution)/shard_map/pallas_call | solution.py:195
  133.7 0.0 copy-start.11
  133.7 1.0 copy-done.11
  134.6 0.7 all-to-all-done.3
  135.4 1.2 broadcast_in_dim.8
  136.6 32.9 %all_to_all.27 = f32[4,1024,128]{2,1,0:T(8,128)S(1)} all-to-all(f32[4,1024,128]{2,1,0:T(8,128)S(1)} %broadcast_in_dim.8), channel_id=1, replica_groups=mesh['y'=8,'zl'=2,'x'=4,'zh'=4,'c'=2] {'x'}, dimensions={0} | all-to-all | bytes 4194304 | tf_op jit(solution)/shard_map/all_to_all | solution.py:252
  169.5 2.9 %shard_map.68 = f32[512,256]{1,0:T(8,128)S(1)} custom-call(bf16[2,512,1024]{2,1,0:T(8,128)(2,1)S(1)} %copy-done.7, bf16[2,512,1024]{2,1,0:T(8,128)(2,1)S(1)} %copy-done.9, f32[2,8,256,128]{3,2,1,0:T(8,128)S(1)} %bitcast.19), custom_call_target="tpu_custom_call" | custom-call | flops 1610612736 | bytes 6291456 | tf_op jit(solution)/shard_map/pallas_call | solution.py:148
  172.4 0.0 copy-start.12
  172.4 0.0 copy-start.18
  172.4 6.0 %collective-permute-start.6 = (f32[512,256]{1,0:T(8,128)S(1)}, f32[512,256]{1,0:T(8,128)S(1)}, u32[]{:S(2)}, u32[]{:S(2)}) collective-permute-start(f32[512,256]{1,0:T(8,128)S(1)} %shard_map.68), channel_id=1, source_target_pairs={{0,1},{1,0},{2,3},{3,2},{4,5},{5,4},{6,7},{7,6},{8,9},{9,8},{10,11... | collective-permute-start | bytes 1572872 | tf_op jit(solution)/shard_map/ppermute | solution.py:291
  178.5 2.9 %shard_map.69.mine = f32[512,256]{1,0:T(8,128)S(1)} custom-call(bf16[2,512,1024]{2,1,0:T(8,128)(2,1)S(1)} %copy-done.3, bf16[2,512,1024]{2,1,0:T(8,128)(2,1)S(1)} %copy-done.5, f32[2,8,256,128]{3,2,1,0:T(8,128)S(1)} %bitcast.20), custom_call_target="tpu_custom_call" | custom-call | flops 1610612736 | bytes 6291456 | tf_op jit(solution)/shard_map/pallas_call | solution.py:148
  181.4 1.9 %shard_map.70 = f32[512,512]{1,0:T(8,128)} custom-call(s32[1]{0:T(128)} %bitcast.core, f32[512,512]{1,0:T(8,128)S(1)} %bitcast.25, f32[512,256]{1,0:T(8,128)S(1)} %shard_map.69.mine, f32[512,256]{1,0:T(8,128)S(1)} %collective-permute-done.6.theirs, f32[512,512]{1,0:T(8,128)S(1)} %bitcast.23, f32[1,512]{1,0:T(1,128)S(1)} %bitcast.28), custom_call_target="tpu_custom_call" | custom-call | flops 2621440 | bytes 4194304 | tf_op jit(solution)/shard_map/pallas_call | solution.py:224
  (31 shorter events, 0.1 us)
Async XLA Ops:
  0.0 33.6 %copy-start = (f32[512,512]{1,0:T(8,128)S(1)}, f32[512,512]{1,0:T(8,128)}, u32[]{:S(2)}) copy-start(f32[512,512]{1,0:T(8,128)} %param.10) | copy-start | bytes 3145732
  0.9 16.8 %collective-permute-start.1 = (f32[512,3]{1,0:T(8,128)S(1)}, f32[512,3]{1,0:T(8,128)S(1)}, u32[]{:S(2)}, u32[]{:S(2)}) collective-permute-start(f32[512,3]{1,0:T(8,128)S(1)} %bitcast.26), channel_id=1, source_target_pairs={{0,1},{1,0},{2,3},{3,2},{4,5},{5,4},{6,7},{7,6},{8,9},{9,8},{10,11... | collective-permute-start | bytes 18440 | tf_op jit(solution)/shard_map/ppermute | solution.py:269
  10.8 11.2 %collective-permute-start = (f32[512,256]{1,0:T(8,128)S(1)}, f32[512,256]{1,0:T(8,128)S(1)}, u32[]{:S(2)}, u32[]{:S(2)}) collective-permute-start(f32[512,256]{1,0:T(8,128)S(1)} %constant_dynamic-slice_fusion), channel_id=1, source_target_pairs={{0,1},{1,0},{2,3},{3,2},{4,5},{5,4},{6,7},{7,6},{8,9},{9,8},{10,11... | collective-permute-start | bytes 1572872 | tf_op jit(solution)/shard_map/ppermute | solution.py:270
  17.7 4.3 %copy-start.2 = (bf16[2,512,1024]{2,1,0:T(8,128)(2,1)}, bf16[2,512,1024]{2,1,0:T(8,128)(2,1)S(1)}, u32[]{:S(2)}) copy-start(bf16[2,512,1024]{2,1,0:T(8,128)(2,1)S(1)} %get-tuple-element.21.top_a.top) | copy-start | bytes 6291460
  17.7 4.3 %copy-start.4 = (bf16[2,512,1024]{2,1,0:T(8,128)(2,1)}, bf16[2,512,1024]{2,1,0:T(8,128)(2,1)S(1)}, u32[]{:S(2)}) copy-start(bf16[2,512,1024]{2,1,0:T(8,128)(2,1)S(1)} %get-tuple-element.22.low_a.low) | copy-start | bytes 6291460
  17.7 4.3 %copy-start.1 = (f32[2,2,128,512]{3,2,1,0:T(8,128)S(1)}, f32[2,2,128,512]{3,2,1,0:T(8,128)}, u32[]{:S(2)}) copy-start(f32[2,2,128,512]{3,2,1,0:T(8,128)} %param.6) | copy-start | bytes 3145732
  22.0 5.7 %copy-start.6 = (bf16[2,512,1024]{2,1,0:T(8,128)(2,1)}, bf16[2,512,1024]{2,1,0:T(8,128)(2,1)S(1)}, u32[]{:S(2)}) copy-start(bf16[2,512,1024]{2,1,0:T(8,128)(2,1)S(1)} %get-tuple-element.24.top_b.top) | copy-start | bytes 6291460
  22.0 5.7 %copy-start.8 = (bf16[2,512,1024]{2,1,0:T(8,128)(2,1)}, bf16[2,512,1024]{2,1,0:T(8,128)(2,1)S(1)}, u32[]{:S(2)}) copy-start(bf16[2,512,1024]{2,1,0:T(8,128)(2,1)S(1)} %get-tuple-element.25.low_b.low) | copy-start | bytes 6291460
  27.7 1.3 copy-start.10
  29.1 40.0 %all-to-all-start = ((f32[4,1024,128]{2,1,0:T(8,128)}), f32[4,1024,128]{2,1,0:T(8,128)}, u32[]{:S(2)}, u32[]{:S(2)}) async-start(f32[4,1024,128]{2,1,0:T(8,128)} %bitcast.24), calls=%async_computation | async-start | bytes 4194304 | tf_op jit(solution)/shard_map/all_to_all | solution.py:247
  34.7 26.1 %collective-permute-start.3 = (f32[1,2,128,512]{3,2,1,0:T(8,128)S(1)}, f32[1,2,128,512]{3,2,1,0:T(8,128)S(1)}, u32[]{:S(2)}, u32[]{:S(2)}) collective-permute-start(f32[1,2,128,512]{3,2,1,0:T(8,128)S(1)} %get-tuple-element.39), channel_id=1, source_target_pairs={{32,0},{64,32},{96,64},{128,96},{160,128},{192,160},{224,192},{256... | collective-permute-start | bytes 1572872 | tf_op jit(solution)/shard_map/ppermute | solution.py:240
  36.6 24.2 %collective-permute-start.2 = (f32[1,2,128,512]{3,2,1,0:T(8,128)S(1)}, f32[1,2,128,512]{3,2,1,0:T(8,128)S(1)}, u32[]{:S(2)}, u32[]{:S(2)}) collective-permute-start(f32[1,2,128,512]{3,2,1,0:T(8,128)S(1)} %get-tuple-element.40), channel_id=1, source_target_pairs={{0,32},{32,64},{64,96},{96,128},{128,160},{160,192},{192,224},{224... | collective-permute-start | bytes 1572872 | tf_op jit(solution)/shard_map/ppermute | solution.py:239
  60.8 1.8 copy-start.14
  60.8 1.8 copy-start.16
  62.6 29.3 %collective-permute-start.5 = (f32[4,1,128,512]{3,2,1,0:T(8,128)}, f32[4,1,128,512]{3,2,1,0:T(8,128)}, u32[]{:S(2)}, u32[]{:S(2)}) collective-permute-start(f32[4,1,128,512]{3,2,1,0:T(8,128)} %get-tuple-element.37), channel_id=1, source_target_pairs={{1,0},{2,1},{3,2},{4,3},{5,4},{6,5},{7,6},{8,7},{9,8},{10,9},{11,1... | collective-permute-start | bytes 3145736 | tf_op jit(solution)/shard_map/ppermute | solution.py:240
  65.9 26.0 %collective-permute-start.4 = (f32[4,1,128,512]{3,2,1,0:T(8,128)}, f32[4,1,128,512]{3,2,1,0:T(8,128)}, u32[]{:S(2)}, u32[]{:S(2)}) collective-permute-start(f32[4,1,128,512]{3,2,1,0:T(8,128)} %get-tuple-element.38), channel_id=1, source_target_pairs={{0,1},{1,2},{2,3},{3,4},{4,5},{5,6},{6,7},{7,8},{8,9},{9,10},{10,1... | collective-permute-start | bytes 3145736 | tf_op jit(solution)/shard_map/ppermute | solution.py:239
  114.5 20.8 %all-to-all-start.3 = ((f32[16,64,128]{2,1,0:T(8,128)}), f32[16,64,128]{2,1,0:T(8,128)}, u32[]{:S(2)}, u32[]{:S(2)}) async-start(f32[16,64,128]{2,1,0:T(8,128)} %broadcast_in_dim.7), calls=%async_computation.3 | async-start | bytes 1048576 | tf_op jit(solution)/shard_map/all_to_all | solution.py:252
  123.4 1.7 copy-start.13
  125.1 1.0 copy-start.15
  126.1 1.0 copy-start.17
  133.7 1.0 copy-start.11
  136.5 32.9 %copy-start.7 = (bf16[2,512,1024]{2,1,0:T(8,128)(2,1)S(1)}, bf16[2,512,1024]{2,1,0:T(8,128)(2,1)}, u32[]{:S(2)}) copy-start(bf16[2,512,1024]{2,1,0:T(8,128)(2,1)} %copy-done.6) | copy-start | bytes 6291460
  136.6 32.9 %copy-start.9 = (bf16[2,512,1024]{2,1,0:T(8,128)(2,1)S(1)}, bf16[2,512,1024]{2,1,0:T(8,128)(2,1)}, u32[]{:S(2)}) copy-start(bf16[2,512,1024]{2,1,0:T(8,128)(2,1)} %copy-done.8) | copy-start | bytes 6291460
  169.5 9.0 %copy-start.3 = (bf16[2,512,1024]{2,1,0:T(8,128)(2,1)S(1)}, bf16[2,512,1024]{2,1,0:T(8,128)(2,1)}, u32[]{:S(2)}) copy-start(bf16[2,512,1024]{2,1,0:T(8,128)(2,1)} %copy-done.2) | copy-start | bytes 6291460
  169.5 9.0 %copy-start.5 = (bf16[2,512,1024]{2,1,0:T(8,128)(2,1)S(1)}, bf16[2,512,1024]{2,1,0:T(8,128)(2,1)}, u32[]{:S(2)}) copy-start(bf16[2,512,1024]{2,1,0:T(8,128)(2,1)} %copy-done.4) | copy-start | bytes 6291460
  172.4 9.0 %copy-start.12 = (f32[2,2,128,512]{3,2,1,0:T(8,128)S(1)}, f32[2,2,128,512]{3,2,1,0:T(8,128)}, u32[]{:S(2)}) copy-start(f32[2,2,128,512]{3,2,1,0:T(8,128)} %copy-done.11) | copy-start | bytes 3145732
  172.4 9.0 %copy-start.18 = (f32[512]{0:T(512)S(1)}, f32[512]{0:T(512)}, u32[]{:S(2)}) copy-start(f32[512]{0:T(512)} %param.11) | copy-start | bytes 6148
  172.4 9.0 %collective-permute-start.6 = (f32[512,256]{1,0:T(8,128)S(1)}, f32[512,256]{1,0:T(8,128)S(1)}, u32[]{:S(2)}, u32[]{:S(2)}) collective-permute-start(f32[512,256]{1,0:T(8,128)S(1)} %shard_map.68), channel_id=1, source_target_pairs={{0,1},{1,0},{2,3},{3,2},{4,5},{5,4},{6,7},{7,6},{8,9},{9,8},{10,11... | collective-permute-start | bytes 1572872 | tf_op jit(solution)/shard_map/ppermute | solution.py:291

commit v4 on v3

--- a/solution.py
+++ b/solution.py
@@ -48,16 +48,16 @@
 def trig_kernel(rows, place, vec, top, low, split, angle):
     @pl.when(pl.program_id(0) == 0)
     def _():
-        rest = place[...]
+        rest = place[...].T
         for part in range(3):
             piece = rest.astype(BF16)
             split[:, 3 * part : 3 * part + 3] = piece
             rest = rest - piece.astype(F32)
 
-    vectors = vec[...].astype(BF16)
+    vectors = vec[...].astype(F32).astype(BF16)
     angle[...] = dot(split[...], jnp.concatenate([vectors] * 3))
 
-    @pl.loop(0, place.shape[0] // rows)
+    @pl.loop(0, place.shape[1] // rows)
     def _(step):
         here = pl.ds(pl.multiple_of(step * rows, rows), rows)
         for kind, value in enumerate(turn(angle[here, :])):
@@ -65,18 +65,18 @@
 
 
 def trig(place, vec):
-    atoms, count = place.shape[0], vec.shape[1]
-    block = 256
+    atoms, count = place.shape[1], vec.shape[1]
+    block = count
     shape = jax.ShapeDtypeStruct((2, atoms, count), BF16)
     spec = pl.BlockSpec((2, atoms, block), lambda j: (0, 0, j))
     return pl.pallas_call(
-        functools.partial(trig_kernel, 32),
+        functools.partial(trig_kernel, 16),
         grid=(count // block,),
         in_specs=[pl.BlockSpec(place.shape, lambda j: (0, 0)), pl.BlockSpec((3, block), lambda j: (0, j))],
         out_specs=[spec, spec],
         out_shape=[shape, shape],
         scratch_shapes=[pltpu.VMEM((atoms, 9), BF16), pltpu.VMEM((atoms, block), F32)],
-        compiler_params=pltpu.CompilerParams(vmem_limit_bytes=VMEM_LIMIT // 2),
+        compiler_params=pltpu.CompilerParams(vmem_limit_bytes=VMEM_LIMIT),
         cost_estimate=pl.CostEstimate(flops=4 * 2**30, bytes_accessed=4 * 2**20, transcendentals=0),
     )(place, vec)
 
@@ -90,7 +90,7 @@
         for part, value in enumerate((feat[:, pl.ds(start, chans)], take[...])):
             split[part, :chans], split[part, chans:] = halves(value.T)
 
-    vectors = vec[...]
+    vectors = vec[...].astype(F32)
     damp = scale * jnp.exp(-jnp.sum(vectors * vectors, axis=0, keepdims=True) / 64.0)
     for kind in range(2):
         both = dot(split[0], top_a[kind]) + dot(split[1], top_b[kind])
@@ -264,28 +264,27 @@
     scale = 1.0 / math.sqrt(atoms_all) / math.sqrt(count)
 
     flat = features.reshape(atoms, channels)
-    vec = wave_vectors.astype(F32)
-    place = positions.reshape(3, atoms).T
+    place = positions.reshape(3, atoms)
     other = lax.ppermute(place, "c", swap)
     take = lax.ppermute(lax.dynamic_slice_in_dim(flat, (1 - core) * half, half, 1), "c", swap)
-    mine = trig(place, vec)
+    mine = trig(place, wave_vectors)
     other, _ = lax.optimization_barrier((other, mine[0]))
-    theirs = trig(other, vec)
-    partial = structure(which, vec, flat, take, (*mine, *theirs), scale)
+    theirs = trig(other, wave_vectors)
+    partial = structure(which, wave_vectors, flat, take, (*mine, *theirs), scale)
 
     rows, cells = lax.optimization_barrier((partial.reshape(-1, 128), features))
     projected = jnp.einsum("abtf,fg->abtg", cells, msg_weight, precision=lax.Precision.HIGH)
     up, down = neighbours(projected, SLAB_X, 0)
-    left, right = neighbours(jnp.concatenate([up, projected, down]), SLAB_Y, 1)
     rows = scatter(rows, ("x",))
     rows, up, down = lax.optimization_barrier((rows, up, down))
+    left, right = neighbours(jnp.concatenate([up, projected, down]), SLAB_Y, 1)
     rows = scatter(rows, ("y", "zl"))
+    rows = jnp.sum(gather(rows, ("zh",)), axis=0)
+    rows = gather(rows, ("y", "zl")).reshape(-1, 128)
     rows, left, right = lax.optimization_barrier((rows, left, right))
     message = neighbour_sum(tile_filter, projected, up, down, left, right)
-    rows = jnp.sum(gather(rows, ("zh",)), axis=0)
-    rows = gather(rows, ("y", "zl")).reshape(-1, 128)
-    rows, message = lax.optimization_barrier((rows, message))
     coef = gather(rows, ("x",)).reshape(partial.shape)
+    coef, message = lax.optimization_barrier((coef, message))
 
     given = inverse(*theirs, coef)
     got = lax.ppermute(given, "c", swap)

time: 184 us -> 181 us (0.984)
  blocking collectives: 73.8 us -> 0 us
  waiting for transfers between devices: 21.6 us -> 63.6 us
  starting transfers between devices: 41.8 us -> 61.3 us
  local copies, waits for them, and re-layouts: 11.8 us -> 23.9 us
  Pallas kernels: 28.3 us -> 24.3 us
    all_to_all x3 -> x0, blocking collectives: 73.8 us -> none  [the longest x2 54.6 us: gather(): return lax.all_to_all(copies, axes, 0, 0, tiled=True)]
    all_to_all x1 -> x2, waiting for transfers between devices: 0.01 us -> 32.8 us  [scatter(): return jnp.sum(lax.all_to_all(parts, axes, 0, 0, tiled=True), axis=0)]
    all_to_all x1 -> x3, starting transfers between devices: 8.86 us -> 17.5 us  [gather(): return lax.all_to_all(copies, axes, 0, 0, tiled=True)]
    unnamed x39 -> x56, local copies, waits for them, and re-layouts: 7.03 us -> 13.7 us
    all_to_all x1 -> x3, waiting for transfers between devices: 0.74 us -> 7.37 us  [gather(): return lax.all_to_all(copies, axes, 0, 0, tiled=True)]
    all_to_all x1 -> x2, starting transfers between devices: 4.51 us -> 9.59 us  [scatter(): return jnp.sum(lax.all_to_all(parts, axes, 0, 0, tiled=True), axis=0)]
    ppermute x1, starting transfers between devices: 6.02 us -> 8.97 us  [shards(): got = lax.ppermute(given, 'c', swap)]
    slice x2, local copies, waits for them, and re-layouts: 1.67 us -> 4.21 us  [neighbours(): head = lax.slice_in_dim(cells, 0, 1, axis=dim)]
  transfers between devices with their start and end apart: 9 -> 12, of which waited for: 2 -> 6; matrix products, arithmetic and copies ran while one was open for 5% -> 6% of each run, Pallas kernels for 10% -> 8%
where the time goes in v4:
time: 181 us; the launch traced here: 180 us
  waiting for transfers between devices  63.6 us (35%)
  starting transfers between devices  61.3 us (34%)
  Pallas kernels  24.3 us (13%)
  local copies, waits for them, and re-layouts  23.9 us (13%)
  other arithmetic  5.29 us (3%)
    all_to_all x2, waiting for transfers between devices, scatter(): return jnp.sum(lax.all_to_all(parts, axes, 0, 0, tiled=True), axis=0)  32.8 us
    ppermute x2, waiting for transfers between devices, neighbours(): lax.ppermute(head, axis, [((i + 1) % count, i) for i in range(count)])  21.5 us
    all_to_all x3, starting transfers between devices, gather(): return lax.all_to_all(copies, axes, 0, 0, tiled=True)  17.5 us
    unnamed x56, local copies, waits for them, and re-layouts  13.7 us
    all_to_all x2, starting transfers between devices, scatter(): return jnp.sum(lax.all_to_all(parts, axes, 0, 0, tiled=True), axis=0)  9.59 us
    ppermute x1, starting transfers between devices, shards(): got = lax.ppermute(given, 'c', swap)  8.97 us
    ppermute x1, starting transfers between devices, shards(): other = lax.ppermute(place, 'c', swap)  8.77 us
    ppermute x2, starting transfers between devices, neighbours(): lax.ppermute(tail, axis, [(i, (i + 1) % count) for i in range(count)])  7.81 us
  transfers between devices with their start and end apart: 12, of which 6 were waited for; matrix products, arithmetic and copies ran while one was open for 6% of the time, Pallas kernels for 8%

profile of v4, /device:TPU:1, one launch (start us, length us, event | category | flops | bytes accessed | tf_op | source)
XLA Modules:
  0.0 179.9 jit_solution(18344188638496138230)
XLA Ops:
  0.0 0.8 reshape.38.place
  0.8 8.8 %collective-permute-start.1 = (f32[3,512]{1,0:T(4,128)S(1)}, f32[3,512]{1,0:T(4,128)S(1)}, u32[]{:S(2)}, u32[]{:S(2)}) collective-permute-start(f32[3,512]{1,0:T(4,128)S(1)} %reshape.38.place), channel_id=1, source_target_pairs={{0,1},{1,0},{2,3},{3,2},{4,5},{5,4},{6,7},{7,6},{8,9},{9,8},{10,11... | collective-permute-start | bytes 18440 | tf_op jit(solution)/shard_map/ppermute | solution.py:268
  9.6 1.1 constant_dynamic-slice_fusion
  10.7 1.9 %collective-permute-start = (f32[512,256]{1,0:T(8,128)S(1)}, f32[512,256]{1,0:T(8,128)S(1)}, u32[]{:S(2)}, u32[]{:S(2)}) collective-permute-start(f32[512,256]{1,0:T(8,128)S(1)} %constant_dynamic-slice_fusion), channel_id=1, source_target_pairs={{0,1},{1,0},{2,3},{3,2},{4,5},{5,4},{6,7},{7,6},{8,9},{9,8},{10,11... | collective-permute-start | bytes 1572872 | tf_op jit(solution)/shard_map/ppermute | solution.py:269
  12.6 0.0 copy-start.25
  12.6 0.7 copy-done.25
  13.3 3.0 %shard_map.64 = (bf16[2,512,1024]{2,1,0:T(8,128)(2,1)S(1)}, bf16[2,512,1024]{2,1,0:T(8,128)(2,1)S(1)}) custom-call(f32[3,512]{1,0:T(4,128)S(1)} %reshape.38.place, s32[3,1024]{1,0:T(4,128)S(1)} %copy-done.25), custom_call_target="tpu_custom_call" | custom-call | flops 4294967296 | bytes 4194304 | tf_op jit(solution)/shard_map/pallas_call | solution.py:72
  16.4 3.0 %shard_map.65 = (bf16[2,512,1024]{2,1,0:T(8,128)(2,1)S(1)}, bf16[2,512,1024]{2,1,0:T(8,128)(2,1)S(1)}) custom-call(f32[3,512]{1,0:T(4,128)S(1)} %collective-permute-done.1.place, s32[3,1024]{1,0:T(4,128)S(1)} %copy-done.26), custom_call_target="tpu_custom_call" | custom-call | flops 4294967296 | bytes 4194304 | tf_op jit(solution)/shard_map/pallas_call | solution.py:72
  19.5 5.6 %shard_map.66 = f32[2,8,256,128]{3,2,1,0:T(8,128)S(1)} custom-call(s32[1]{0:T(128)} %bitcast.core, s32[3,1024]{1,0:T(4,128)S(1)} %copy-done.26, f32[512,512]{1,0:T(8,128)S(1)} %bitcast.19, f32[512,256]{1,0:T(8,128)S(1)} %collective-permute-done.take, bf16[2,512,1024]{2,1,0:T(8,128)(2,1)S(1)} %get-tuple-element.21.top_a.top, ...), custom_call_target="tpu_custom_call" | custom-call | flops 3221225472 | bytes 12582912 | tf_op jit(solution)/shard_map/pallas_call | solution.py:110
  25.1 1.4 copy-done.13
  26.5 4.5 %all-to-all-start = ((f32[4,1024,128]{2,1,0:T(8,128)}), f32[4,1024,128]{2,1,0:T(8,128)}, u32[]{:S(2)}, u32[]{:S(2)}) async-start(f32[4,1024,128]{2,1,0:T(8,128)} %bitcast.21), calls=%async_computation | async-start | bytes 4194304 | tf_op jit(solution)/shard_map/all_to_all | solution.py:247
  31.0 1.0 fusion.own
  32.0 1.1 fusion.3
  33.2 1.9 %collective-permute-start.3 = (f32[1,2,128,512]{3,2,1,0:T(8,128)}, f32[1,2,128,512]{3,2,1,0:T(8,128)S(1)}, u32[]{:S(2)}, u32[]{:S(2)}) collective-permute-start(f32[1,2,128,512]{3,2,1,0:T(8,128)} %get-tuple-element.39), channel_id=1, source_target_pairs={{32,0},{64,32},{96,64},{128,96},{160,128},{192,160},{224,192},{256... | collective-permute-start | bytes 1572872 | tf_op jit(solution)/shard_map/ppermute | solution.py:240
  35.1 3.4 %collective-permute-start.2 = (f32[1,2,128,512]{3,2,1,0:T(8,128)}, f32[1,2,128,512]{3,2,1,0:T(8,128)S(1)}, u32[]{:S(2)}, u32[]{:S(2)}) collective-permute-start(f32[1,2,128,512]{3,2,1,0:T(8,128)} %get-tuple-element.40), channel_id=1, source_target_pairs={{0,32},{32,64},{64,96},{96,128},{128,160},{160,192},{192,224},{224... | collective-permute-start | bytes 1572872 | tf_op jit(solution)/shard_map/ppermute | solution.py:239
  38.4 18.6 %all-to-all-done = f32[4,1024,128]{2,1,0:T(8,128)} async-done(((f32[4,1024,128]{2,1,0:T(8,128)}), f32[4,1024,128]{2,1,0:T(8,128)}, u32[]{:S(2)}, u32[]{:S(2)}) %all-to-all-start) | async-done | bytes 2097184 | tf_op jit(solution)/shard_map/all_to_all | solution.py:247
  57.0 2.5 %reduce_sum.27 = f32[1024,128]{1,0:T(8,128)} reduce(f32[4,1024,128]{2,1,0:T(8,128)} %all-to-all-done, f32[]{:T(128)} %constant.5.clone.1), dimensions={0}, to_apply=%region_0.0 | reduce | flops 393216 | bytes 2621444 | tf_op jit(solution)/shard_map/reduce_sum | solution.py:247
  59.6 5.1 %all-to-all-start.1 = ((f32[16,64,128]{2,1,0:T(8,128)}), f32[16,64,128]{2,1,0:T(8,128)}, u32[]{:S(2)}, u32[]{:S(2)}) async-start(f32[16,64,128]{2,1,0:T(8,128)} %bitcast.24), calls=%async_computation.1 | async-start | bytes 1048576 | tf_op jit(solution)/shard_map/all_to_all | solution.py:247
  64.7 1.7 pad_maximum_fusion
  66.3 14.2 %all-to-all-done.1 = f32[16,64,128]{2,1,0:T(8,128)} async-done(((f32[16,64,128]{2,1,0:T(8,128)}), f32[16,64,128]{2,1,0:T(8,128)}, u32[]{:S(2)}, u32[]{:S(2)}) %all-to-all-start.1) | async-done | bytes 524320 | tf_op jit(solution)/shard_map/all_to_all | solution.py:247
  80.6 1.1 reduce_sum.28
  81.6 0.7 broadcast_in_dim.6
  82.3 9.1 %all-to-all-start.2 = ((f32[4,64,128]{2,1,0:T(8,128)}), f32[4,64,128]{2,1,0:T(8,128)S(1)}, u32[]{:S(2)}, u32[]{:S(2)}) async-start(f32[4,64,128]{2,1,0:T(8,128)} %broadcast_in_dim.6), calls=%async_computation.2 | async-start | bytes 262144 | tf_op jit(solution)/shard_map/all_to_all | solution.py:252
  91.4 3.1 %fusion.2 = (f32[4,1,128,512]{3,2,1,0:T(8,128)}, f32[4,1,128,512]{3,2,1,0:T(8,128)}) fusion(f32[4,2,128,512]{3,2,1,0:T(8,128)} %pad_maximum_fusion), kind=kLoop, calls=%fused_computation.4 | loop fusion | bytes 4194304 | tf_op jit(solution)/shard_map/slice | solution.py:237
  94.5 4.8 %collective-permute-start.5 = (f32[4,1,128,512]{3,2,1,0:T(8,128)}, f32[4,1,128,512]{3,2,1,0:T(8,128)S(1)}, u32[]{:S(2)}, u32[]{:S(2)}) collective-permute-start(f32[4,1,128,512]{3,2,1,0:T(8,128)} %get-tuple-element.37), channel_id=1, source_target_pairs={{1,0},{2,1},{3,2},{4,3},{5,4},{6,5},{7,6},{8,7},{9,8},{10,9},{11,1... | collective-permute-start | bytes 3145736 | tf_op jit(solution)/shard_map/ppermute | solution.py:240
  99.3 4.4 %collective-permute-start.4 = (f32[4,1,128,512]{3,2,1,0:T(8,128)}, f32[4,1,128,512]{3,2,1,0:T(8,128)S(1)}, u32[]{:S(2)}, u32[]{:S(2)}) collective-permute-start(f32[4,1,128,512]{3,2,1,0:T(8,128)} %get-tuple-element.38), channel_id=1, source_target_pairs={{0,1},{1,2},{2,3},{3,4},{4,5},{5,6},{6,7},{7,8},{8,9},{9,10},{10,1... | collective-permute-start | bytes 3145736 | tf_op jit(solution)/shard_map/ppermute | solution.py:239
  103.8 0.9 broadcast_in_dim.7
  104.7 4.2 %all-to-all-start.3 = ((f32[16,64,128]{2,1,0:T(8,128)}), f32[16,64,128]{2,1,0:T(8,128)}, u32[]{:S(2)}, u32[]{:S(2)}) async-start(f32[16,64,128]{2,1,0:T(8,128)} %broadcast_in_dim.7), calls=%async_computation.3 | async-start | bytes 1048576 | tf_op jit(solution)/shard_map/all_to_all | solution.py:252
  109.0 21.5 %collective-permute-done.5.right = f32[4,1,128,512]{3,2,1,0:T(8,128)S(1)} collective-permute-done((f32[4,1,128,512]{3,2,1,0:T(8,128)}, f32[4,1,128,512]{3,2,1,0:T(8,128)S(1)}, u32[]{:S(2)}, u32[]{:S(2)}) %collective-permute-start.5) | collective-permute-done | bytes 1048608 | tf_op jit(solution)/shard_map/ppermute | solution.py:240
  130.5 1.9 %collective-permute-done.4.left = f32[4,1,128,512]{3,2,1,0:T(8,128)S(1)} collective-permute-done((f32[4,1,128,512]{3,2,1,0:T(8,128)}, f32[4,1,128,512]{3,2,1,0:T(8,128)S(1)}, u32[]{:S(2)}, u32[]{:S(2)}) %collective-permute-start.4) | collective-permute-done | bytes 1048608 | tf_op jit(solution)/shard_map/ppermute | solution.py:239
  132.4 0.3 all-to-all-done.3
  132.8 2.6 %broadcast_in_dim.8 = f32[4,1024,128]{2,1,0:T(8,128)} broadcast(f32[1024,128]{1,0:T(8,128)} %bitcast.7), dimensions={1,2} | broadcast | bytes 2621440 | tf_op jit(solution)/shard_map/broadcast_in_dim | solution.py:251
  135.4 4.2 %all-to-all-start.4 = ((f32[4,1024,128]{2,1,0:T(8,128)}), f32[4,1024,128]{2,1,0:T(8,128)S(1)}, u32[]{:S(2)}, u32[]{:S(2)}) async-start(f32[4,1024,128]{2,1,0:T(8,128)} %broadcast_in_dim.8), calls=%async_computation.4 | async-start | bytes 4194304 | tf_op jit(solution)/shard_map/all_to_all | solution.py:252
  139.5 1.2 copy-done.2
  140.8 1.7 copy-done.16
  142.4 1.0 copy-done.18
  143.5 1.0 copy-done.20
  144.5 1.2 copy-done.22
  145.7 1.2 copy-done.24
  147.0 4.9 %shard_map.67 = f32[2,2,128,512]{3,2,1,0:T(8,128)S(1)} custom-call(f32[2,2,9,128,128]{4,3,2,1,0:T(8,128)S(1)} %copy-done.16, f32[2,2,128,512]{3,2,1,0:T(8,128)S(1)} %copy-done.2, f32[1,2,128,512]{3,2,1,0:T(8,128)S(1)} %copy-done.20, f32[1,2,128,512]{3,2,1,0:T(8,128)S(1)} %copy-done.18, f32[4,1,128,512]{3,2,1,0:T(8,128)S(1)} %copy-done.24, ...), custom_call_target="tpu_custom_call" | custom-call | flops 1811939328 | bytes 8388608 | tf_op jit(solution)/shard_map/pallas_call | solution.py:195
  151.9 1.0 copy-done.14
  152.9 7.0 %all-to-all-done.4 = f32[4,1024,128]{2,1,0:T(8,128)S(1)} async-done(((f32[4,1024,128]{2,1,0:T(8,128)}), f32[4,1024,128]{2,1,0:T(8,128)S(1)}, u32[]{:S(2)}, u32[]{:S(2)}) %all-to-all-start.4) | async-done | bytes 2097184 | tf_op jit(solution)/shard_map/all_to_all | solution.py:252
  159.9 1.6 copy-done.10
  161.5 1.6 copy-done.12
  163.1 2.9 %shard_map.68 = f32[512,256]{1,0:T(8,128)S(1)} custom-call(bf16[2,512,1024]{2,1,0:T(8,128)(2,1)S(1)} %copy-done.10, bf16[2,512,1024]{2,1,0:T(8,128)(2,1)S(1)} %copy-done.12, f32[2,8,256,128]{3,2,1,0:T(8,128)S(1)} %bitcast.16), custom_call_target="tpu_custom_call" | custom-call | flops 1610612736 | bytes 6291456 | tf_op jit(solution)/shard_map/pallas_call | solution.py:148
  166.0 9.0 %collective-permute-start.6 = (f32[512,256]{1,0:T(8,128)S(1)}, f32[512,256]{1,0:T(8,128)S(1)}, u32[]{:S(2)}, u32[]{:S(2)}) collective-permute-start(f32[512,256]{1,0:T(8,128)S(1)} %shard_map.68), channel_id=1, source_target_pairs={{0,1},{1,0},{2,3},{3,2},{4,5},{5,4},{6,7},{7,6},{8,9},{9,8},{10,11... | collective-permute-start | bytes 1572872 | tf_op jit(solution)/shard_map/ppermute | solution.py:290
  175.0 2.9 %shard_map.69.mine = f32[512,256]{1,0:T(8,128)S(1)} custom-call(bf16[2,512,1024]{2,1,0:T(8,128)(2,1)S(1)} %copy-done.6, bf16[2,512,1024]{2,1,0:T(8,128)(2,1)S(1)} %copy-done.8, f32[2,8,256,128]{3,2,1,0:T(8,128)S(1)} %bitcast.17), custom_call_target="tpu_custom_call" | custom-call | flops 1610612736 | bytes 6291456 | tf_op jit(solution)/shard_map/pallas_call | solution.py:148
  178.0 1.9 %shard_map.70 = f32[512,512]{1,0:T(8,128)} custom-call(s32[1]{0:T(128)} %bitcast.core, f32[512,512]{1,0:T(8,128)S(1)} %bitcast.22, f32[512,256]{1,0:T(8,128)S(1)} %shard_map.69.mine, f32[512,256]{1,0:T(8,128)S(1)} %collective-permute-done.6.theirs, f32[512,512]{1,0:T(8,128)S(1)} %bitcast.20, f32[1,512]{1,0:T(1,128)S(1)} %bitcast.23), custom_call_target="tpu_custom_call" | custom-call | flops 2621440 | bytes 4194304 | tf_op jit(solution)/shard_map/pallas_call | solution.py:224
  (51 shorter events, 0.1 us)
Async XLA Ops:
  0.0 31.0 %copy-start = (f32[512,512]{1,0:T(8,128)S(1)}, f32[512,512]{1,0:T(8,128)}, u32[]{:S(2)}) copy-start(f32[512,512]{1,0:T(8,128)} %param.10) | copy-start | bytes 3145732
  0.8 15.6 %collective-permute-start.1 = (f32[3,512]{1,0:T(4,128)S(1)}, f32[3,512]{1,0:T(4,128)S(1)}, u32[]{:S(2)}, u32[]{:S(2)}) collective-permute-start(f32[3,512]{1,0:T(4,128)S(1)} %reshape.38.place), channel_id=1, source_target_pairs={{0,1},{1,0},{2,3},{3,2},{4,5},{5,4},{6,7},{7,6},{8,9},{9,8},{10,11... | collective-permute-start | bytes 18440 | tf_op jit(solution)/shard_map/ppermute | solution.py:268
  10.7 8.8 %collective-permute-start = (f32[512,256]{1,0:T(8,128)S(1)}, f32[512,256]{1,0:T(8,128)S(1)}, u32[]{:S(2)}, u32[]{:S(2)}) collective-permute-start(f32[512,256]{1,0:T(8,128)S(1)} %constant_dynamic-slice_fusion), channel_id=1, source_target_pairs={{0,1},{1,0},{2,3},{3,2},{4,5},{5,4},{6,7},{7,6},{8,9},{9,8},{10,11... | collective-permute-start | bytes 1572872 | tf_op jit(solution)/shard_map/ppermute | solution.py:269
  12.6 0.7 copy-start.25
  13.3 3.0 %copy-start.26 = (s32[3,1024]{1,0:T(4,128)S(1)}, s32[3,1024]{1,0:T(4,128)}, u32[]{:S(2)}) copy-start(s32[3,1024]{1,0:T(4,128)} %vec.5) | copy-start | bytes 36868
  16.3 3.1 %copy-start.5 = (bf16[2,512,1024]{2,1,0:T(8,128)(2,1)}, bf16[2,512,1024]{2,1,0:T(8,128)(2,1)S(1)}, u32[]{:S(2)}) copy-start(bf16[2,512,1024]{2,1,0:T(8,128)(2,1)S(1)} %get-tuple-element.21.top_a.top) | copy-start | bytes 6291460
  16.3 3.1 %copy-start.7 = (bf16[2,512,1024]{2,1,0:T(8,128)(2,1)}, bf16[2,512,1024]{2,1,0:T(8,128)(2,1)S(1)}, u32[]{:S(2)}) copy-start(bf16[2,512,1024]{2,1,0:T(8,128)(2,1)S(1)} %get-tuple-element.22.low_a.low) | copy-start | bytes 6291460
  16.4 3.1 %copy-start.3 = (f32[2,2,128,512]{3,2,1,0:T(8,128)S(1)}, f32[2,2,128,512]{3,2,1,0:T(8,128)}, u32[]{:S(2)}) copy-start(f32[2,2,128,512]{3,2,1,0:T(8,128)} %param.6) | copy-start | bytes 3145732
  19.4 5.7 %copy-start.9 = (bf16[2,512,1024]{2,1,0:T(8,128)(2,1)}, bf16[2,512,1024]{2,1,0:T(8,128)(2,1)S(1)}, u32[]{:S(2)}) copy-start(bf16[2,512,1024]{2,1,0:T(8,128)(2,1)S(1)} %get-tuple-element.24.top_b.top) | copy-start | bytes 6291460
  19.4 5.7 %copy-start.11 = (bf16[2,512,1024]{2,1,0:T(8,128)(2,1)}, bf16[2,512,1024]{2,1,0:T(8,128)(2,1)S(1)}, u32[]{:S(2)}) copy-start(bf16[2,512,1024]{2,1,0:T(8,128)(2,1)S(1)} %get-tuple-element.25.low_b.low) | copy-start | bytes 6291460
  25.1 1.4 copy-start.13
  26.5 30.5 %all-to-all-start = ((f32[4,1024,128]{2,1,0:T(8,128)}), f32[4,1024,128]{2,1,0:T(8,128)}, u32[]{:S(2)}, u32[]{:S(2)}) async-start(f32[4,1024,128]{2,1,0:T(8,128)} %bitcast.21), calls=%async_computation | async-start | bytes 4194304 | tf_op jit(solution)/shard_map/all_to_all | solution.py:247
  32.0 32.6 %copy-start.1 = (f32[2,2,128,512]{3,2,1,0:T(8,128)}, f32[2,2,128,512]{3,2,1,0:T(8,128)S(1)}, u32[]{:S(2)}) copy-start(f32[2,2,128,512]{3,2,1,0:T(8,128)S(1)} %fusion.own) | copy-start | bytes 3145732
  33.2 26.4 %collective-permute-start.3 = (f32[1,2,128,512]{3,2,1,0:T(8,128)}, f32[1,2,128,512]{3,2,1,0:T(8,128)S(1)}, u32[]{:S(2)}, u32[]{:S(2)}) collective-permute-start(f32[1,2,128,512]{3,2,1,0:T(8,128)} %get-tuple-element.39), channel_id=1, source_target_pairs={{32,0},{64,32},{96,64},{128,96},{160,128},{192,160},{224,192},{256... | collective-permute-start | bytes 1572872 | tf_op jit(solution)/shard_map/ppermute | solution.py:240
  35.1 24.5 %collective-permute-start.2 = (f32[1,2,128,512]{3,2,1,0:T(8,128)}, f32[1,2,128,512]{3,2,1,0:T(8,128)S(1)}, u32[]{:S(2)}, u32[]{:S(2)}) collective-permute-start(f32[1,2,128,512]{3,2,1,0:T(8,128)} %get-tuple-element.40), channel_id=1, source_target_pairs={{0,32},{32,64},{64,96},{96,128},{128,160},{160,192},{192,224},{224... | collective-permute-start | bytes 1572872 | tf_op jit(solution)/shard_map/ppermute | solution.py:239
  59.5 6.8 %copy-start.17 = (f32[1,2,128,512]{3,2,1,0:T(8,128)}, f32[1,2,128,512]{3,2,1,0:T(8,128)S(1)}, u32[]{:S(2)}) copy-start(f32[1,2,128,512]{3,2,1,0:T(8,128)S(1)} %collective-permute-done.3.down) | copy-start | bytes 1572868
  59.5 6.8 %copy-start.19 = (f32[1,2,128,512]{3,2,1,0:T(8,128)}, f32[1,2,128,512]{3,2,1,0:T(8,128)S(1)}, u32[]{:S(2)}) copy-start(f32[1,2,128,512]{3,2,1,0:T(8,128)S(1)} %collective-permute-done.2.up) | copy-start | bytes 1572868
  59.6 21.0 %all-to-all-start.1 = ((f32[16,64,128]{2,1,0:T(8,128)}), f32[16,64,128]{2,1,0:T(8,128)}, u32[]{:S(2)}, u32[]{:S(2)}) async-start(f32[16,64,128]{2,1,0:T(8,128)} %bitcast.24), calls=%async_computation.1 | async-start | bytes 1048576 | tf_op jit(solution)/shard_map/all_to_all | solution.py:247
  82.3 21.5 %all-to-all-start.2 = ((f32[4,64,128]{2,1,0:T(8,128)}), f32[4,64,128]{2,1,0:T(8,128)S(1)}, u32[]{:S(2)}, u32[]{:S(2)}) async-start(f32[4,64,128]{2,1,0:T(8,128)} %broadcast_in_dim.6), calls=%async_computation.2 | async-start | bytes 262144 | tf_op jit(solution)/shard_map/all_to_all | solution.py:252
  94.5 36.0 %collective-permute-start.5 = (f32[4,1,128,512]{3,2,1,0:T(8,128)}, f32[4,1,128,512]{3,2,1,0:T(8,128)S(1)}, u32[]{:S(2)}, u32[]{:S(2)}) collective-permute-start(f32[4,1,128,512]{3,2,1,0:T(8,128)} %get-tuple-element.37), channel_id=1, source_target_pairs={{1,0},{2,1},{3,2},{4,3},{5,4},{6,5},{7,6},{8,7},{9,8},{10,9},{11,1... | collective-permute-start | bytes 3145736 | tf_op jit(solution)/shard_map/ppermute | solution.py:240
  99.3 33.1 %collective-permute-start.4 = (f32[4,1,128,512]{3,2,1,0:T(8,128)}, f32[4,1,128,512]{3,2,1,0:T(8,128)S(1)}, u32[]{:S(2)}, u32[]{:S(2)}) collective-permute-start(f32[4,1,128,512]{3,2,1,0:T(8,128)} %get-tuple-element.38), channel_id=1, source_target_pairs={{0,1},{1,2},{2,3},{3,4},{4,5},{5,6},{6,7},{7,8},{8,9},{9,10},{10,1... | collective-permute-start | bytes 3145736 | tf_op jit(solution)/shard_map/ppermute | solution.py:239
  104.7 28.1 %all-to-all-start.3 = ((f32[16,64,128]{2,1,0:T(8,128)}), f32[16,64,128]{2,1,0:T(8,128)}, u32[]{:S(2)}, u32[]{:S(2)}) async-start(f32[16,64,128]{2,1,0:T(8,128)} %broadcast_in_dim.7), calls=%async_computation.3 | async-start | bytes 1048576 | tf_op jit(solution)/shard_map/all_to_all | solution.py:252
  130.5 4.8 %copy-start.21 = (f32[4,1,128,512]{3,2,1,0:T(8,128)}, f32[4,1,128,512]{3,2,1,0:T(8,128)S(1)}, u32[]{:S(2)}) copy-start(f32[4,1,128,512]{3,2,1,0:T(8,128)S(1)} %collective-permute-done.5.right) | copy-start | bytes 3145732
  132.4 2.9 %copy-start.23 = (f32[4,1,128,512]{3,2,1,0:T(8,128)}, f32[4,1,128,512]{3,2,1,0:T(8,128)S(1)}, u32[]{:S(2)}) copy-start(f32[4,1,128,512]{3,2,1,0:T(8,128)S(1)} %collective-permute-done.4.left) | copy-start | bytes 3145732
  135.4 24.5 %all-to-all-start.4 = ((f32[4,1024,128]{2,1,0:T(8,128)}), f32[4,1024,128]{2,1,0:T(8,128)S(1)}, u32[]{:S(2)}, u32[]{:S(2)}) async-start(f32[4,1024,128]{2,1,0:T(8,128)} %broadcast_in_dim.8), calls=%async_computation.4 | async-start | bytes 4194304 | tf_op jit(solution)/shard_map/all_to_all | solution.py:252
  139.5 1.2 copy-start.2
  140.8 1.7 copy-start.16
  142.4 1.0 copy-start.18
  143.5 1.0 copy-start.20
  144.5 1.2 copy-start.22
  145.7 1.2 copy-start.24
  151.9 1.0 copy-start.14
  159.9 1.6 copy-start.10
  161.5 1.6 copy-start.12
  163.1 11.9 %copy-start.6 = (bf16[2,512,1024]{2,1,0:T(8,128)(2,1)S(1)}, bf16[2,512,1024]{2,1,0:T(8,128)(2,1)}, u32[]{:S(2)}) copy-start(bf16[2,512,1024]{2,1,0:T(8,128)(2,1)} %copy-done.5) | copy-start | bytes 6291460
  163.1 11.9 %copy-start.8 = (bf16[2,512,1024]{2,1,0:T(8,128)(2,1)S(1)}, bf16[2,512,1024]{2,1,0:T(8,128)(2,1)}, u32[]{:S(2)}) copy-start(bf16[2,512,1024]{2,1,0:T(8,128)(2,1)} %copy-done.7) | copy-start | bytes 6291460
  166.0 12.0 %copy-start.4 = (f32[2,2,128,512]{3,2,1,0:T(8,128)S(1)}, f32[2,2,128,512]{3,2,1,0:T(8,128)}, u32[]{:S(2)}) copy-start(f32[2,2,128,512]{3,2,1,0:T(8,128)} %param.6) | copy-start | bytes 3145732
  166.0 12.0 %copy-start.15 = (f32[2,2,128,512]{3,2,1,0:T(8,128)S(1)}, f32[2,2,128,512]{3,2,1,0:T(8,128)}, u32[]{:S(2)}) copy-start(f32[2,2,128,512]{3,2,1,0:T(8,128)} %copy-done.14) | copy-start | bytes 3145732
  166.0 12.0 %copy-start.27 = (f32[512]{0:T(512)S(1)}, f32[512]{0:T(512)}, u32[]{:S(2)}) copy-start(f32[512]{0:T(512)} %param.11) | copy-start | bytes 6148
  166.0 11.9 %collective-permute-start.6 = (f32[512,256]{1,0:T(8,128)S(1)}, f32[512,256]{1,0:T(8,128)S(1)}, u32[]{:S(2)}, u32[]{:S(2)}) collective-permute-start(f32[512,256]{1,0:T(8,128)S(1)} %shard_map.68), channel_id=1, source_target_pairs={{0,1},{1,0},{2,3},{3,2},{4,5},{5,4},{6,7},{7,6},{8,9},{9,8},{10,11... | collective-permute-start | bytes 1572872 | tf_op jit(solution)/shard_map/ppermute | solution.py:290

commit v5 on v4

--- a/solution.py
+++ b/solution.py
@@ -123,14 +123,21 @@
 
 
 def inverse_kernel(top, low, coef, out, coef_top, coef_low):
-    tiles = coef.shape[1]
+    span_x, span_z, span_y, piece, lanes = coef.shape
+    tiles, chans = coef_top.shape[1] // lanes, coef_top.shape[2]
+    per_tile = chans // piece
+    per_x = span_z * span_y
 
     @pl.when(pl.program_id(0) == 0)
     def _():
-        for kind in range(2):
-            for tile in range(tiles):
-                here = slice(tile * 128, (tile + 1) * 128)
-                coef_top[kind, here, :], coef_low[kind, here, :] = halves(coef[kind, tile].T)
+        for tile in range(2 * tiles):
+            parts = []
+            for number in range(tile * per_tile, (tile + 1) * per_tile):
+                here = number % per_x
+                parts.append(coef[number // per_x, here % span_z, here // span_z])
+            here = slice(tile % tiles * lanes, (tile % tiles + 1) * lanes)
+            kind = tile // tiles
+            coef_top[kind, here, :], coef_low[kind, here, :] = halves(jnp.concatenate(parts).T)
 
     total = None
     for kind in range(2):
@@ -140,15 +147,14 @@
     out[...] = total
 
 
-def inverse(top, low, coef):
+def inverse(top, low, coef, chans):
     kinds, atoms, count = top.shape
-    chans = coef.shape[2]
     block = 256
     trig_spec = pl.BlockSpec((kinds, block, count), lambda i: (0, i, 0))
     return pl.pallas_call(
         inverse_kernel,
         grid=(atoms // block,),
-        in_specs=[trig_spec, trig_spec, pl.BlockSpec(coef.shape, lambda i: (0, 0, 0, 0))],
+        in_specs=[trig_spec, trig_spec, pl.BlockSpec(coef.shape, lambda i: (0, 0, 0, 0, 0))],
         out_specs=pl.BlockSpec((block, chans), lambda i: (i, 0)),
         out_shape=jax.ShapeDtypeStruct((atoms, chans), F32),
         scratch_shapes=[pltpu.VMEM((kinds, count, chans), BF16)] * 2,
@@ -280,16 +286,17 @@
     left, right = neighbours(jnp.concatenate([up, projected, down]), SLAB_Y, 1)
     rows = scatter(rows, ("y", "zl"))
     rows = jnp.sum(gather(rows, ("zh",)), axis=0)
-    rows = gather(rows, ("y", "zl")).reshape(-1, 128)
     rows, left, right = lax.optimization_barrier((rows, left, right))
+    rows = gather(rows, ("y",)).reshape(-1, 128)
     message = neighbour_sum(tile_filter, projected, up, down, left, right)
-    coef = gather(rows, ("x",)).reshape(partial.shape)
+    coef = gather(rows, ("x", "zl"))
+    coef = coef.reshape(lax.axis_size("x"), lax.axis_size("zl"), lax.axis_size("y"), -1, 128)
     coef, message = lax.optimization_barrier((coef, message))
 
-    given = inverse(*theirs, coef)
+    given = inverse(*theirs, coef, half)
     got = lax.ppermute(given, "c", swap)
     coef, _ = lax.optimization_barrier((coef, given))
-    own = inverse(*mine, coef)
+    own = inverse(*mine, coef, half)
     out = update(which, message.reshape(atoms, channels), own, got, flat, out_gain.reshape(1, channels))
     return out.reshape(features.shape)
 

time: 181 us -> 177 us (0.978)
  blocking collectives: 0 us -> 42.6 us
  waiting for transfers between devices: 63.6 us -> 38.8 us
  starting transfers between devices: 61.3 us -> 44.7 us
  local copies, waits for them, and re-layouts: 23.9 us -> 19.9 us
    all_to_all x0 -> x2, blocking collectives: none -> 42.6 us  [gather(): return lax.all_to_all(copies, axes, 0, 0, tiled=True)]
    ppermute x2, waiting for transfers between devices: 21.5 us -> 0.01 us  [neighbours(): lax.ppermute(head, axis, [((i + 1) % count, i) for i in range(count)])]
    all_to_all x3 -> x1, starting transfers between devices: 17.5 us -> 7.62 us  [gather(): return lax.all_to_all(copies, axes, 0, 0, tiled=True)]
    all_to_all x2, waiting for transfers between devices: 32.8 us -> 25.3 us  [scatter(): return jnp.sum(lax.all_to_all(parts, axes, 0, 0, tiled=True), axis=0)]
    all_to_all x3 -> x1, waiting for transfers between devices: 7.37 us -> 13.5 us  [gather(): return lax.all_to_all(copies, axes, 0, 0, tiled=True)]
    ppermute x1, starting transfers between devices: 8.97 us -> 3.11 us  [shards(): got = lax.ppermute(given, 'c', swap)]
    broadcast_in_dim x3, local copies, waits for them, and re-layouts: 4.12 us -> 1.55 us  [gather(): copies = jnp.broadcast_to(value[None], (lax.axis_size(axes),) + value.shape)]
    ppermute x2, starting transfers between devices: 6.76 us -> 4.57 us  [neighbours(): lax.ppermute(head, axis, [((i + 1) % count, i) for i in range(count)])]
  transfers between devices with their start and end apart: 12 -> 10, of which waited for: 6 -> 3; matrix products, arithmetic and copies ran while one was open for 6% -> 5% of each run, Pallas kernels for 8% -> 8%
where the time goes in v5:
time: 177 us; the launch traced here: 176 us
  starting transfers between devices  44.7 us (25%)
  blocking collectives  42.6 us (24%)
  waiting for transfers between devices  38.8 us (22%)
  Pallas kernels  24.3 us (14%)
  local copies, waits for them, and re-layouts  19.9 us (11%)
  other arithmetic  3.85 us (2%)
    all_to_all x2, blocking collectives, gather(): return lax.all_to_all(copies, axes, 0, 0, tiled=True)  42.6 us
    all_to_all x2, waiting for transfers between devices, scatter(): return jnp.sum(lax.all_to_all(parts, axes, 0, 0, tiled=True), axis=0)  25.3 us
    unnamed x56, local copies, waits for them, and re-layouts  13.7 us
    all_to_all x1, waiting for transfers between devices, gather(): return lax.all_to_all(copies, axes, 0, 0, tiled=True)  13.5 us
    all_to_all x2, starting transfers between devices, scatter(): return jnp.sum(lax.all_to_all(parts, axes, 0, 0, tiled=True), axis=0)  9.59 us
    ppermute x2, starting transfers between devices, neighbours(): lax.ppermute(tail, axis, [(i, (i + 1) % count) for i in range(count)])  9.07 us
    ppermute x1, starting transfers between devices, shards(): other = lax.ppermute(place, 'c', swap)  8.77 us
    all_to_all x1, starting transfers between devices, gather(): return lax.all_to_all(copies, axes, 0, 0, tiled=True)  7.62 us
  transfers between devices with their start and end apart: 10, of which 3 were waited for; matrix products, arithmetic and copies ran while one was open for 5% of the time, Pallas kernels for 8%

profile of v5, /device:TPU:1, one launch (start us, length us, event | category | flops | bytes accessed | tf_op | source)
XLA Modules:
  0.0 175.6 jit_solution(3011309440821611668)
XLA Ops:
  0.0 0.8 reshape.35.place
  0.8 8.8 %collective-permute-start.1 = (f32[3,512]{1,0:T(4,128)S(1)}, f32[3,512]{1,0:T(4,128)S(1)}, u32[]{:S(2)}, u32[]{:S(2)}) collective-permute-start(f32[3,512]{1,0:T(4,128)S(1)} %reshape.35.place), channel_id=1, source_target_pairs={{0,1},{1,0},{2,3},{3,2},{4,5},{5,4},{6,7},{7,6},{8,9},{9,8},{10,11... | collective-permute-start | bytes 18440 | tf_op jit(solution)/shard_map/ppermute | solution.py:274
  9.6 1.1 constant_dynamic-slice_fusion
  10.7 1.9 %collective-permute-start = (f32[512,256]{1,0:T(8,128)S(1)}, f32[512,256]{1,0:T(8,128)S(1)}, u32[]{:S(2)}, u32[]{:S(2)}) collective-permute-start(f32[512,256]{1,0:T(8,128)S(1)} %constant_dynamic-slice_fusion), channel_id=1, source_target_pairs={{0,1},{1,0},{2,3},{3,2},{4,5},{5,4},{6,7},{7,6},{8,9},{9,8},{10,11... | collective-permute-start | bytes 1572872 | tf_op jit(solution)/shard_map/ppermute | solution.py:275
  12.6 0.0 copy-start.25
  12.6 0.7 copy-done.25
  13.3 3.0 %shard_map.64 = (bf16[2,512,1024]{2,1,0:T(8,128)(2,1)S(1)}, bf16[2,512,1024]{2,1,0:T(8,128)(2,1)S(1)}) custom-call(f32[3,512]{1,0:T(4,128)S(1)} %reshape.35.place, s32[3,1024]{1,0:T(4,128)S(1)} %copy-done.25), custom_call_target="tpu_custom_call" | custom-call | flops 4294967296 | bytes 4194304 | tf_op jit(solution)/shard_map/pallas_call | solution.py:72
  16.4 0.0 copy-start.3
  16.4 3.0 %shard_map.65 = (bf16[2,512,1024]{2,1,0:T(8,128)(2,1)S(1)}, bf16[2,512,1024]{2,1,0:T(8,128)(2,1)S(1)}) custom-call(f32[3,512]{1,0:T(4,128)S(1)} %collective-permute-done.1.place, s32[3,1024]{1,0:T(4,128)S(1)} %copy-done.26), custom_call_target="tpu_custom_call" | custom-call | flops 4294967296 | bytes 4194304 | tf_op jit(solution)/shard_map/pallas_call | solution.py:72
  19.5 5.6 %shard_map.66 = f32[2,8,256,128]{3,2,1,0:T(8,128)S(1)} custom-call(s32[1]{0:T(128)} %bitcast.core, s32[3,1024]{1,0:T(4,128)S(1)} %copy-done.26, f32[512,512]{1,0:T(8,128)S(1)} %bitcast.19, f32[512,256]{1,0:T(8,128)S(1)} %collective-permute-done.take, bf16[2,512,1024]{2,1,0:T(8,128)(2,1)S(1)} %get-tuple-element.21.top_a.top, ...), custom_call_target="tpu_custom_call" | custom-call | flops 3221225472 | bytes 12582912 | tf_op jit(solution)/shard_map/pallas_call | solution.py:110
  25.1 1.4 copy-done.13
  26.5 4.5 %all-to-all-start = ((f32[4,1024,128]{2,1,0:T(8,128)}), f32[4,1024,128]{2,1,0:T(8,128)}, u32[]{:S(2)}, u32[]{:S(2)}) async-start(f32[4,1024,128]{2,1,0:T(8,128)} %bitcast.21), calls=%async_computation | async-start | bytes 4194304 | tf_op jit(solution)/shard_map/all_to_all | solution.py:253
  31.0 1.0 fusion.own
  32.0 0.0 copy-start.1
  32.0 1.2 fusion.3
  33.2 1.9 %collective-permute-start.3 = (f32[1,2,128,512]{3,2,1,0:T(8,128)}, f32[1,2,128,512]{3,2,1,0:T(8,128)S(1)}, u32[]{:S(2)}, u32[]{:S(2)}) collective-permute-start(f32[1,2,128,512]{3,2,1,0:T(8,128)} %get-tuple-element.39), channel_id=1, source_target_pairs={{32,0},{64,32},{96,64},{128,96},{160,128},{192,160},{224,192},{256... | collective-permute-start | bytes 1572872 | tf_op jit(solution)/shard_map/ppermute | solution.py:246
  35.1 3.4 %collective-permute-start.2 = (f32[1,2,128,512]{3,2,1,0:T(8,128)}, f32[1,2,128,512]{3,2,1,0:T(8,128)S(1)}, u32[]{:S(2)}, u32[]{:S(2)}) collective-permute-start(f32[1,2,128,512]{3,2,1,0:T(8,128)} %get-tuple-element.40), channel_id=1, source_target_pairs={{0,32},{32,64},{64,96},{96,128},{128,160},{160,192},{192,224},{224... | collective-permute-start | bytes 1572872 | tf_op jit(solution)/shard_map/ppermute | solution.py:245
  38.4 18.5 %all-to-all-done = f32[4,1024,128]{2,1,0:T(8,128)} async-done(((f32[4,1024,128]{2,1,0:T(8,128)}), f32[4,1024,128]{2,1,0:T(8,128)}, u32[]{:S(2)}, u32[]{:S(2)}) %all-to-all-start) | async-done | bytes 2097184 | tf_op jit(solution)/shard_map/all_to_all | solution.py:253
  57.0 2.6 %reduce_sum.27 = f32[1024,128]{1,0:T(8,128)} reduce(f32[4,1024,128]{2,1,0:T(8,128)} %all-to-all-done, f32[]{:T(128)} %constant.5.clone.1), dimensions={0}, to_apply=%region_0.0 | reduce | flops 393216 | bytes 2621444 | tf_op jit(solution)/shard_map/reduce_sum | solution.py:253
  59.5 5.1 %all-to-all-start.1 = ((f32[16,64,128]{2,1,0:T(8,128)}), f32[16,64,128]{2,1,0:T(8,128)}, u32[]{:S(2)}, u32[]{:S(2)}) async-start(f32[16,64,128]{2,1,0:T(8,128)} %bitcast.24), calls=%async_computation.1 | async-start | bytes 1048576 | tf_op jit(solution)/shard_map/all_to_all | solution.py:253
  64.7 0.2 pad_maximum_fusion
  64.9 1.6 fusion.2
  66.5 2.7 %collective-permute-start.5 = (f32[4,1,128,512]{3,2,1,0:T(8,128)}, f32[4,1,128,512]{3,2,1,0:T(8,128)S(1)}, u32[]{:S(2)}, u32[]{:S(2)}) collective-permute-start(f32[4,1,128,512]{3,2,1,0:T(8,128)} %get-tuple-element.37), channel_id=1, source_target_pairs={{1,0},{2,1},{3,2},{4,3},{5,4},{6,5},{7,6},{8,7},{9,8},{10,9},{11,1... | collective-permute-start | bytes 3145736 | tf_op jit(solution)/shard_map/ppermute | solution.py:246
  69.2 5.7 %collective-permute-start.4 = (f32[4,1,128,512]{3,2,1,0:T(8,128)}, f32[4,1,128,512]{3,2,1,0:T(8,128)S(1)}, u32[]{:S(2)}, u32[]{:S(2)}) collective-permute-start(f32[4,1,128,512]{3,2,1,0:T(8,128)} %get-tuple-element.38), channel_id=1, source_target_pairs={{0,1},{1,2},{2,3},{3,4},{4,5},{5,6},{6,7},{7,8},{8,9},{9,10},{10,1... | collective-permute-start | bytes 3145736 | tf_op jit(solution)/shard_map/ppermute | solution.py:245
  74.9 6.7 %all-to-all-done.1 = f32[16,64,128]{2,1,0:T(8,128)} async-done(((f32[16,64,128]{2,1,0:T(8,128)}), f32[16,64,128]{2,1,0:T(8,128)}, u32[]{:S(2)}, u32[]{:S(2)}) %all-to-all-start.1) | async-done | bytes 524320 | tf_op jit(solution)/shard_map/all_to_all | solution.py:253
  81.7 1.1 reduce_sum.28
  82.8 28.2 %all_to_all.25 = f32[4,64,128]{2,1,0:T(8,128)S(1)} all-to-all(f32[4,64,128]{2,1,0:T(8,128)S(1)} %broadcast_in_dim.8), channel_id=1, replica_groups=mesh['y'=8,'zl'=2,'x'=4,'zh'=4,'c'=2] {'zh'}, dimensions={0} | all-to-all | bytes 262144 | tf_op jit(solution)/shard_map/all_to_all | solution.py:258
  111.0 14.4 %all_to_all.26 = f32[8,64,128]{2,1,0:T(8,128)S(1)} all-to-all(f32[8,64,128]{2,1,0:T(8,128)S(1)} %broadcast_in_dim.9), channel_id=1, replica_groups=mesh['y'=8,'zl'=2,'x'=4,'zh'=4,'c'=2] {'y'}, dimensions={0} | all-to-all | bytes 524288 | tf_op jit(solution)/shard_map/all_to_all | solution.py:258
  125.5 1.5 broadcast_in_dim.22
  127.0 7.6 %all-to-all-start.4 = ((f32[8,512,128]{2,1,0:T(8,128)}), f32[8,512,128]{2,1,0:T(8,128)S(1)}, u32[]{:S(2)}, u32[]{:S(2)}) async-start(f32[8,512,128]{2,1,0:T(8,128)} %broadcast_in_dim.22), calls=%async_computation.4 | async-start | bytes 4194304 | tf_op jit(solution)/shard_map/all_to_all | solution.py:258
  134.6 1.2 copy-done.2
  135.8 1.7 copy-done.16
  137.5 1.0 copy-done.18
  138.6 1.0 copy-done.20
  139.6 1.2 copy-done.22
  140.8 1.2 copy-done.24
  142.0 4.9 %shard_map.67 = f32[2,2,128,512]{3,2,1,0:T(8,128)S(1)} custom-call(f32[2,2,9,128,128]{4,3,2,1,0:T(8,128)S(1)} %copy-done.16, f32[2,2,128,512]{3,2,1,0:T(8,128)S(1)} %copy-done.2, f32[1,2,128,512]{3,2,1,0:T(8,128)S(1)} %copy-done.20, f32[1,2,128,512]{3,2,1,0:T(8,128)S(1)} %copy-done.18, f32[4,1,128,512]{3,2,1,0:T(8,128)S(1)} %copy-done.24, ...), custom_call_target="tpu_custom_call" | custom-call | flops 1811939328 | bytes 8388608 | tf_op jit(solution)/shard_map/pallas_call | solution.py:201
  147.0 0.0 copy-start.14
  147.0 1.0 copy-done.14
  148.0 13.5 %all-to-all-done.4 = f32[8,512,128]{2,1,0:T(8,128)S(1)} async-done(((f32[8,512,128]{2,1,0:T(8,128)}), f32[8,512,128]{2,1,0:T(8,128)S(1)}, u32[]{:S(2)}, u32[]{:S(2)}) %all-to-all-start.4) | async-done | bytes 2097184 | tf_op jit(solution)/shard_map/all_to_all | solution.py:258
  161.5 1.6 copy-done.10
  163.1 1.6 copy-done.12
  164.7 2.9 %shard_map.68 = f32[512,256]{1,0:T(8,128)S(1)} custom-call(bf16[2,512,1024]{2,1,0:T(8,128)(2,1)S(1)} %copy-done.10, bf16[2,512,1024]{2,1,0:T(8,128)(2,1)S(1)} %copy-done.12, f32[4,2,8,64,128]{4,3,2,1,0:T(8,128)S(1)} %bitcast.16), custom_call_target="tpu_custom_call" | custom-call | flops 1610612736 | bytes 6291456 | tf_op jit(solution)/shard_map/pallas_call | solution.py:154
  167.6 0.0 copy-start.15
  167.6 0.0 copy-start.27
  167.6 3.1 %collective-permute-start.6 = (f32[512,256]{1,0:T(8,128)S(1)}, f32[512,256]{1,0:T(8,128)S(1)}, u32[]{:S(2)}, u32[]{:S(2)}) collective-permute-start(f32[512,256]{1,0:T(8,128)S(1)} %shard_map.68), channel_id=1, source_target_pairs={{0,1},{1,0},{2,3},{3,2},{4,5},{5,4},{6,7},{7,6},{8,9},{9,8},{10,11... | collective-permute-start | bytes 1572872 | tf_op jit(solution)/shard_map/ppermute | solution.py:297
  170.7 2.9 %shard_map.69.mine = f32[512,256]{1,0:T(8,128)S(1)} custom-call(bf16[2,512,1024]{2,1,0:T(8,128)(2,1)S(1)} %copy-done.6, bf16[2,512,1024]{2,1,0:T(8,128)(2,1)S(1)} %copy-done.8, f32[4,2,8,64,128]{4,3,2,1,0:T(8,128)S(1)} %bitcast.17), custom_call_target="tpu_custom_call" | custom-call | flops 1610612736 | bytes 6291456 | tf_op jit(solution)/shard_map/pallas_call | solution.py:154
  173.7 1.9 %shard_map.70 = f32[512,512]{1,0:T(8,128)} custom-call(s32[1]{0:T(128)} %bitcast.core, f32[512,512]{1,0:T(8,128)S(1)} %bitcast.22, f32[512,256]{1,0:T(8,128)S(1)} %shard_map.69.mine, f32[512,256]{1,0:T(8,128)S(1)} %collective-permute-done.6.theirs, f32[512,512]{1,0:T(8,128)S(1)} %bitcast.20, f32[1,512]{1,0:T(1,128)S(1)} %bitcast.23), custom_call_target="tpu_custom_call" | custom-call | flops 2621440 | bytes 4194304 | tf_op jit(solution)/shard_map/pallas_call | solution.py:230
  (49 shorter events, 0.1 us)
Async XLA Ops:
  0.0 31.0 %copy-start = (f32[512,512]{1,0:T(8,128)S(1)}, f32[512,512]{1,0:T(8,128)}, u32[]{:S(2)}) copy-start(f32[512,512]{1,0:T(8,128)} %param.10) | copy-start | bytes 3145732
  0.8 15.6 %collective-permute-start.1 = (f32[3,512]{1,0:T(4,128)S(1)}, f32[3,512]{1,0:T(4,128)S(1)}, u32[]{:S(2)}, u32[]{:S(2)}) collective-permute-start(f32[3,512]{1,0:T(4,128)S(1)} %reshape.35.place), channel_id=1, source_target_pairs={{0,1},{1,0},{2,3},{3,2},{4,5},{5,4},{6,7},{7,6},{8,9},{9,8},{10,11... | collective-permute-start | bytes 18440 | tf_op jit(solution)/shard_map/ppermute | solution.py:274
  10.7 8.8 %collective-permute-start = (f32[512,256]{1,0:T(8,128)S(1)}, f32[512,256]{1,0:T(8,128)S(1)}, u32[]{:S(2)}, u32[]{:S(2)}) collective-permute-start(f32[512,256]{1,0:T(8,128)S(1)} %constant_dynamic-slice_fusion), channel_id=1, source_target_pairs={{0,1},{1,0},{2,3},{3,2},{4,5},{5,4},{6,7},{7,6},{8,9},{9,8},{10,11... | collective-permute-start | bytes 1572872 | tf_op jit(solution)/shard_map/ppermute | solution.py:275
  12.6 0.7 copy-start.25
  13.3 3.0 %copy-start.26 = (s32[3,1024]{1,0:T(4,128)S(1)}, s32[3,1024]{1,0:T(4,128)}, u32[]{:S(2)}) copy-start(s32[3,1024]{1,0:T(4,128)} %vec.5) | copy-start | bytes 36868
  16.3 3.1 %copy-start.5 = (bf16[2,512,1024]{2,1,0:T(8,128)(2,1)}, bf16[2,512,1024]{2,1,0:T(8,128)(2,1)S(1)}, u32[]{:S(2)}) copy-start(bf16[2,512,1024]{2,1,0:T(8,128)(2,1)S(1)} %get-tuple-element.21.top_a.top) | copy-start | bytes 6291460
  16.3 3.1 %copy-start.7 = (bf16[2,512,1024]{2,1,0:T(8,128)(2,1)}, bf16[2,512,1024]{2,1,0:T(8,128)(2,1)S(1)}, u32[]{:S(2)}) copy-start(bf16[2,512,1024]{2,1,0:T(8,128)(2,1)S(1)} %get-tuple-element.22.low_a.low) | copy-start | bytes 6291460
  16.4 3.1 %copy-start.3 = (f32[2,2,128,512]{3,2,1,0:T(8,128)S(1)}, f32[2,2,128,512]{3,2,1,0:T(8,128)}, u32[]{:S(2)}) copy-start(f32[2,2,128,512]{3,2,1,0:T(8,128)} %param.6) | copy-start | bytes 3145732
  19.4 5.7 %copy-start.9 = (bf16[2,512,1024]{2,1,0:T(8,128)(2,1)}, bf16[2,512,1024]{2,1,0:T(8,128)(2,1)S(1)}, u32[]{:S(2)}) copy-start(bf16[2,512,1024]{2,1,0:T(8,128)(2,1)S(1)} %get-tuple-element.24.top_b.top) | copy-start | bytes 6291460
  19.4 5.7 %copy-start.11 = (bf16[2,512,1024]{2,1,0:T(8,128)(2,1)}, bf16[2,512,1024]{2,1,0:T(8,128)(2,1)S(1)}, u32[]{:S(2)}) copy-start(bf16[2,512,1024]{2,1,0:T(8,128)(2,1)S(1)} %get-tuple-element.25.low_b.low) | copy-start | bytes 6291460
  25.1 1.4 copy-start.13
  26.5 30.5 %all-to-all-start = ((f32[4,1024,128]{2,1,0:T(8,128)}), f32[4,1024,128]{2,1,0:T(8,128)}, u32[]{:S(2)}, u32[]{:S(2)}) async-start(f32[4,1024,128]{2,1,0:T(8,128)} %bitcast.21), calls=%async_computation | async-start | bytes 4194304 | tf_op jit(solution)/shard_map/all_to_all | solution.py:253
  32.0 32.7 %copy-start.1 = (f32[2,2,128,512]{3,2,1,0:T(8,128)}, f32[2,2,128,512]{3,2,1,0:T(8,128)S(1)}, u32[]{:S(2)}) copy-start(f32[2,2,128,512]{3,2,1,0:T(8,128)S(1)} %fusion.own) | copy-start | bytes 3145732
  33.2 26.4 %collective-permute-start.3 = (f32[1,2,128,512]{3,2,1,0:T(8,128)}, f32[1,2,128,512]{3,2,1,0:T(8,128)S(1)}, u32[]{:S(2)}, u32[]{:S(2)}) collective-permute-start(f32[1,2,128,512]{3,2,1,0:T(8,128)} %get-tuple-element.39), channel_id=1, source_target_pairs={{32,0},{64,32},{96,64},{128,96},{160,128},{192,160},{224,192},{256... | collective-permute-start | bytes 1572872 | tf_op jit(solution)/shard_map/ppermute | solution.py:246
  35.1 24.5 %collective-permute-start.2 = (f32[1,2,128,512]{3,2,1,0:T(8,128)}, f32[1,2,128,512]{3,2,1,0:T(8,128)S(1)}, u32[]{:S(2)}, u32[]{:S(2)}) collective-permute-start(f32[1,2,128,512]{3,2,1,0:T(8,128)} %get-tuple-element.40), channel_id=1, source_target_pairs={{0,32},{32,64},{64,96},{96,128},{128,160},{160,192},{192,224},{224... | collective-permute-start | bytes 1572872 | tf_op jit(solution)/shard_map/ppermute | solution.py:245
  59.5 5.3 %copy-start.17 = (f32[1,2,128,512]{3,2,1,0:T(8,128)}, f32[1,2,128,512]{3,2,1,0:T(8,128)S(1)}, u32[]{:S(2)}) copy-start(f32[1,2,128,512]{3,2,1,0:T(8,128)S(1)} %collective-permute-done.3.down) | copy-start | bytes 1572868
  59.5 5.4 %copy-start.19 = (f32[1,2,128,512]{3,2,1,0:T(8,128)}, f32[1,2,128,512]{3,2,1,0:T(8,128)S(1)}, u32[]{:S(2)}) copy-start(f32[1,2,128,512]{3,2,1,0:T(8,128)S(1)} %collective-permute-done.2.up) | copy-start | bytes 1572868
  59.5 22.1 %all-to-all-start.1 = ((f32[16,64,128]{2,1,0:T(8,128)}), f32[16,64,128]{2,1,0:T(8,128)}, u32[]{:S(2)}, u32[]{:S(2)}) async-start(f32[16,64,128]{2,1,0:T(8,128)} %bitcast.24), calls=%async_computation.1 | async-start | bytes 1048576 | tf_op jit(solution)/shard_map/all_to_all | solution.py:253
  66.5 44.4 %collective-permute-start.5 = (f32[4,1,128,512]{3,2,1,0:T(8,128)}, f32[4,1,128,512]{3,2,1,0:T(8,128)S(1)}, u32[]{:S(2)}, u32[]{:S(2)}) collective-permute-start(f32[4,1,128,512]{3,2,1,0:T(8,128)} %get-tuple-element.37), channel_id=1, source_target_pairs={{1,0},{2,1},{3,2},{4,3},{5,4},{6,5},{7,6},{8,7},{9,8},{10,9},{11,1... | collective-permute-start | bytes 3145736 | tf_op jit(solution)/shard_map/ppermute | solution.py:246
  69.2 41.8 %collective-permute-start.4 = (f32[4,1,128,512]{3,2,1,0:T(8,128)}, f32[4,1,128,512]{3,2,1,0:T(8,128)S(1)}, u32[]{:S(2)}, u32[]{:S(2)}) collective-permute-start(f32[4,1,128,512]{3,2,1,0:T(8,128)} %get-tuple-element.38), channel_id=1, source_target_pairs={{0,1},{1,2},{2,3},{3,4},{4,5},{5,6},{6,7},{7,8},{8,9},{9,10},{10,1... | collective-permute-start | bytes 3145736 | tf_op jit(solution)/shard_map/ppermute | solution.py:245
  111.0 16.0 %copy-start.21 = (f32[4,1,128,512]{3,2,1,0:T(8,128)}, f32[4,1,128,512]{3,2,1,0:T(8,128)S(1)}, u32[]{:S(2)}) copy-start(f32[4,1,128,512]{3,2,1,0:T(8,128)S(1)} %collective-permute-done.5.right) | copy-start | bytes 3145732
  111.0 16.0 %copy-start.23 = (f32[4,1,128,512]{3,2,1,0:T(8,128)}, f32[4,1,128,512]{3,2,1,0:T(8,128)S(1)}, u32[]{:S(2)}) copy-start(f32[4,1,128,512]{3,2,1,0:T(8,128)S(1)} %collective-permute-done.4.left) | copy-start | bytes 3145732
  127.0 34.5 %all-to-all-start.4 = ((f32[8,512,128]{2,1,0:T(8,128)}), f32[8,512,128]{2,1,0:T(8,128)S(1)}, u32[]{:S(2)}, u32[]{:S(2)}) async-start(f32[8,512,128]{2,1,0:T(8,128)} %broadcast_in_dim.22), calls=%async_computation.4 | async-start | bytes 4194304 | tf_op jit(solution)/shard_map/all_to_all | solution.py:258
  134.6 1.2 copy-start.2
  135.8 1.7 copy-start.16
  137.5 1.0 copy-start.18
  138.6 1.0 copy-start.20
  139.6 1.2 copy-start.22
  140.8 1.2 copy-start.24
  147.0 1.0 copy-start.14
  161.5 1.6 copy-start.10
  163.1 1.6 copy-start.12
  164.7 6.1 %copy-start.6 = (bf16[2,512,1024]{2,1,0:T(8,128)(2,1)S(1)}, bf16[2,512,1024]{2,1,0:T(8,128)(2,1)}, u32[]{:S(2)}) copy-start(bf16[2,512,1024]{2,1,0:T(8,128)(2,1)} %copy-done.5) | copy-start | bytes 6291460
  164.7 6.1 %copy-start.8 = (bf16[2,512,1024]{2,1,0:T(8,128)(2,1)S(1)}, bf16[2,512,1024]{2,1,0:T(8,128)(2,1)}, u32[]{:S(2)}) copy-start(bf16[2,512,1024]{2,1,0:T(8,128)(2,1)} %copy-done.7) | copy-start | bytes 6291460
  167.6 6.1 %copy-start.4 = (f32[2,2,128,512]{3,2,1,0:T(8,128)S(1)}, f32[2,2,128,512]{3,2,1,0:T(8,128)}, u32[]{:S(2)}) copy-start(f32[2,2,128,512]{3,2,1,0:T(8,128)} %param.6) | copy-start | bytes 3145732
  167.6 6.1 %copy-start.15 = (f32[2,2,128,512]{3,2,1,0:T(8,128)S(1)}, f32[2,2,128,512]{3,2,1,0:T(8,128)}, u32[]{:S(2)}) copy-start(f32[2,2,128,512]{3,2,1,0:T(8,128)} %copy-done.14) | copy-start | bytes 3145732
  167.6 6.1 %copy-start.27 = (f32[512]{0:T(512)S(1)}, f32[512]{0:T(512)}, u32[]{:S(2)}) copy-start(f32[512]{0:T(512)} %param.11) | copy-start | bytes 6148
  167.6 6.1 %collective-permute-start.6 = (f32[512,256]{1,0:T(8,128)S(1)}, f32[512,256]{1,0:T(8,128)S(1)}, u32[]{:S(2)}, u32[]{:S(2)}) collective-permute-start(f32[512,256]{1,0:T(8,128)S(1)} %shard_map.68), channel_id=1, source_target_pairs={{0,1},{1,0},{2,3},{3,2},{4,5},{5,4},{6,7},{7,6},{8,9},{9,8},{10,11... | collective-permute-start | bytes 1572872 | tf_op jit(solution)/shard_map/ppermute | solution.py:297

commit v6 on v5

--- a/solution.py
+++ b/solution.py
@@ -281,12 +281,13 @@
     rows, cells = lax.optimization_barrier((partial.reshape(-1, 128), features))
     projected = jnp.einsum("abtf,fg->abtg", cells, msg_weight, precision=lax.Precision.HIGH)
     up, down = neighbours(projected, SLAB_X, 0)
+    left, right = neighbours(jnp.concatenate([up, projected, down]), SLAB_Y, 1)
     rows = scatter(rows, ("x",))
     rows, up, down = lax.optimization_barrier((rows, up, down))
-    left, right = neighbours(jnp.concatenate([up, projected, down]), SLAB_Y, 1)
     rows = scatter(rows, ("y", "zl"))
+    rows, right = lax.optimization_barrier((rows, right))
     rows = jnp.sum(gather(rows, ("zh",)), axis=0)
-    rows, left, right = lax.optimization_barrier((rows, left, right))
+    rows, left = lax.optimization_barrier((rows, left))
     rows = gather(rows, ("y",)).reshape(-1, 128)
     message = neighbour_sum(tile_filter, projected, up, down, left, right)
     coef = gather(rows, ("x", "zl"))

time: 177 us -> 180 us (1.017)
  waiting for transfers between devices: 38.8 us -> 42.3 us
    ppermute x2, waiting for transfers between devices: 0.01 us -> 23.6 us  [neighbours(): lax.ppermute(head, axis, [((i + 1) % count, i) for i in range(count)])]
    all_to_all x2, waiting for transfers between devices: 25.3 us -> 6.36 us  [scatter(): return jnp.sum(lax.all_to_all(parts, axes, 0, 0, tiled=True), axis=0)]
    slice x2 -> x1, local copies, waits for them, and re-layouts: 2.79 us -> 0.07 us  [neighbours(): head = lax.slice_in_dim(cells, 0, 1, axis=dim)]
  transfers between devices with their start and end apart: 10 -> 10, of which waited for: 3 -> 4; matrix products, arithmetic and copies ran while one was open for 5% -> 4% of each run, Pallas kernels for 8% -> 8%
where the time goes in v6:
time: 180 us; the launch traced here: 179 us
  starting transfers between devices  44.4 us (25%)
  blocking collectives  43.5 us (24%)
  waiting for transfers between devices  42.3 us (24%)
  Pallas kernels  24.3 us (14%)
  local copies, waits for them, and re-layouts  19.6 us (11%)
  other arithmetic  3.82 us (2%)
    all_to_all x2, blocking collectives, gather(): return lax.all_to_all(copies, axes, 0, 0, tiled=True)  43.5 us
    ppermute x2, waiting for transfers between devices, neighbours(): lax.ppermute(head, axis, [((i + 1) % count, i) for i in range(count)])  23.6 us
    unnamed x56, local copies, waits for them, and re-layouts  14.5 us
    all_to_all x1, waiting for transfers between devices, gather(): return lax.all_to_all(copies, axes, 0, 0, tiled=True)  12.3 us
    ppermute x2, starting transfers between devices, neighbours(): lax.ppermute(tail, axis, [(i, (i + 1) % count) for i in range(count)])  9.21 us
    ppermute x1, starting transfers between devices, shards(): other = lax.ppermute(place, 'c', swap)  8.77 us
    all_to_all x2, starting transfers between devices, scatter(): return jnp.sum(lax.all_to_all(parts, axes, 0, 0, tiled=True), axis=0)  8.73 us
    all_to_all x2, waiting for transfers between devices, scatter(): return jnp.sum(lax.all_to_all(parts, axes, 0, 0, tiled=True), axis=0)  6.36 us
  transfers between devices with their start and end apart: 10, of which 4 were waited for; matrix products, arithmetic and copies ran while one was open for 4% of the time, Pallas kernels for 8%

profile of v6, /device:TPU:1, one launch (start us, length us, event | category | flops | bytes accessed | tf_op | source)
XLA Modules:
  0.0 179.3 jit_solution(14854244354475830931)
XLA Ops:
  0.0 0.8 reshape.35.place
  0.8 8.8 %collective-permute-start.1 = (f32[3,512]{1,0:T(4,128)S(1)}, f32[3,512]{1,0:T(4,128)S(1)}, u32[]{:S(2)}, u32[]{:S(2)}) collective-permute-start(f32[3,512]{1,0:T(4,128)S(1)} %reshape.35.place), channel_id=1, source_target_pairs={{0,1},{1,0},{2,3},{3,2},{4,5},{5,4},{6,7},{7,6},{8,9},{9,8},{10,11... | collective-permute-start | bytes 18440 | tf_op jit(solution)/shard_map/ppermute | solution.py:274
  9.6 1.1 constant_dynamic-slice_fusion
  10.7 1.9 %collective-permute-start = (f32[512,256]{1,0:T(8,128)S(1)}, f32[512,256]{1,0:T(8,128)S(1)}, u32[]{:S(2)}, u32[]{:S(2)}) collective-permute-start(f32[512,256]{1,0:T(8,128)S(1)} %constant_dynamic-slice_fusion), channel_id=1, source_target_pairs={{0,1},{1,0},{2,3},{3,2},{4,5},{5,4},{6,7},{7,6},{8,9},{9,8},{10,11... | collective-permute-start | bytes 1572872 | tf_op jit(solution)/shard_map/ppermute | solution.py:275
  12.6 0.0 copy-start.25
  12.6 0.7 copy-done.25
  13.3 3.0 %shard_map.64 = (bf16[2,512,1024]{2,1,0:T(8,128)(2,1)S(1)}, bf16[2,512,1024]{2,1,0:T(8,128)(2,1)S(1)}) custom-call(f32[3,512]{1,0:T(4,128)S(1)} %reshape.35.place, s32[3,1024]{1,0:T(4,128)S(1)} %copy-done.25), custom_call_target="tpu_custom_call" | custom-call | flops 4294967296 | bytes 4194304 | tf_op jit(solution)/shard_map/pallas_call | solution.py:72
  16.4 0.0 copy-start.3
  16.4 3.0 %shard_map.65 = (bf16[2,512,1024]{2,1,0:T(8,128)(2,1)S(1)}, bf16[2,512,1024]{2,1,0:T(8,128)(2,1)S(1)}) custom-call(f32[3,512]{1,0:T(4,128)S(1)} %collective-permute-done.1.place, s32[3,1024]{1,0:T(4,128)S(1)} %copy-done.26), custom_call_target="tpu_custom_call" | custom-call | flops 4294967296 | bytes 4194304 | tf_op jit(solution)/shard_map/pallas_call | solution.py:72
  19.5 5.6 %shard_map.66 = f32[2,8,256,128]{3,2,1,0:T(8,128)S(1)} custom-call(s32[1]{0:T(128)} %bitcast.core, s32[3,1024]{1,0:T(4,128)S(1)} %copy-done.26, f32[512,512]{1,0:T(8,128)S(1)} %bitcast.19, f32[512,256]{1,0:T(8,128)S(1)} %collective-permute-done.take, bf16[2,512,1024]{2,1,0:T(8,128)(2,1)S(1)} %get-tuple-element.22.top_a.top, ...), custom_call_target="tpu_custom_call" | custom-call | flops 3221225472 | bytes 12582912 | tf_op jit(solution)/shard_map/pallas_call | solution.py:110
  25.1 1.4 copy-done.13
  26.5 4.5 %all-to-all-start = ((f32[4,1024,128]{2,1,0:T(8,128)}), f32[4,1024,128]{2,1,0:T(8,128)}, u32[]{:S(2)}, u32[]{:S(2)}) async-start(f32[4,1024,128]{2,1,0:T(8,128)} %bitcast.21), calls=%async_computation | async-start | bytes 4194304 | tf_op jit(solution)/shard_map/all_to_all | solution.py:253
  31.0 1.0 fusion.own
  32.0 0.1 fusion.3
  32.1 1.9 %collective-permute-start.3 = (f32[1,2,128,512]{3,2,1,0:T(8,128)S(1)}, f32[1,2,128,512]{3,2,1,0:T(8,128)S(1)}, u32[]{:S(2)}, u32[]{:S(2)}) collective-permute-start(f32[1,2,128,512]{3,2,1,0:T(8,128)S(1)} %get-tuple-element.41), channel_id=1, source_target_pairs={{32,0},{64,32},{96,64},{128,96},{160,128},{192,160},{224,192},{256... | collective-permute-start | bytes 1572872 | tf_op jit(solution)/shard_map/ppermute | solution.py:246
  34.0 3.4 %collective-permute-start.2 = (f32[1,2,128,512]{3,2,1,0:T(8,128)S(1)}, f32[1,2,128,512]{3,2,1,0:T(8,128)S(1)}, u32[]{:S(2)}, u32[]{:S(2)}) collective-permute-start(f32[1,2,128,512]{3,2,1,0:T(8,128)S(1)} %get-tuple-element.42), channel_id=1, source_target_pairs={{0,32},{32,64},{64,96},{96,128},{128,160},{160,192},{192,224},{224... | collective-permute-start | bytes 1572872 | tf_op jit(solution)/shard_map/ppermute | solution.py:245
  37.4 20.8 %collective-permute-done.3.down = f32[1,2,128,512]{3,2,1,0:T(8,128)S(1)} collective-permute-done((f32[1,2,128,512]{3,2,1,0:T(8,128)S(1)}, f32[1,2,128,512]{3,2,1,0:T(8,128)S(1)}, u32[]{:S(2)}, u32[]{:S(2)}) %collective-permute-start.3) | collective-permute-done | bytes 524320 | tf_op jit(solution)/shard_map/ppermute | solution.py:246
  58.2 0.2 pad_maximum_fusion
  58.4 0.6 copy-done.17
  59.0 0.2 copy-done.19
  59.2 1.6 fusion.2
  60.8 3.2 %collective-permute-start.4 = (f32[4,1,128,512]{3,2,1,0:T(8,128)}, f32[4,1,128,512]{3,2,1,0:T(8,128)S(1)}, u32[]{:S(2)}, u32[]{:S(2)}) collective-permute-start(f32[4,1,128,512]{3,2,1,0:T(8,128)} %get-tuple-element.40), channel_id=1, source_target_pairs={{1,0},{2,1},{3,2},{4,3},{5,4},{6,5},{7,6},{8,7},{9,8},{10,9},{11,1... | collective-permute-start | bytes 3145736 | tf_op jit(solution)/shard_map/ppermute | solution.py:246
  64.1 2.6 %reduce_sum.27 = f32[1024,128]{1,0:T(8,128)} reduce(f32[4,1024,128]{2,1,0:T(8,128)} %all-to-all-done, f32[]{:T(128)} %constant.5.clone.1), dimensions={0}, to_apply=%region_0.0 | reduce | flops 393216 | bytes 2621444 | tf_op jit(solution)/shard_map/reduce_sum | solution.py:253
  66.6 4.2 %all-to-all-start.1 = ((f32[16,64,128]{2,1,0:T(8,128)}), f32[16,64,128]{2,1,0:T(8,128)}, u32[]{:S(2)}, u32[]{:S(2)}) async-start(f32[16,64,128]{2,1,0:T(8,128)} %bitcast.6), calls=%async_computation.1 | async-start | bytes 1048576 | tf_op jit(solution)/shard_map/all_to_all | solution.py:253
  70.9 5.8 %collective-permute-start.5 = (f32[4,1,128,512]{3,2,1,0:T(8,128)}, f32[4,1,128,512]{3,2,1,0:T(8,128)S(1)}, u32[]{:S(2)}, u32[]{:S(2)}) collective-permute-start(f32[4,1,128,512]{3,2,1,0:T(8,128)} %get-tuple-element.39), channel_id=1, source_target_pairs={{0,1},{1,2},{2,3},{3,4},{4,5},{5,6},{6,7},{7,8},{8,9},{9,10},{10,1... | collective-permute-start | bytes 3145736 | tf_op jit(solution)/shard_map/ppermute | solution.py:245
  76.7 6.4 %all-to-all-done.1 = f32[16,64,128]{2,1,0:T(8,128)} async-done(((f32[16,64,128]{2,1,0:T(8,128)}), f32[16,64,128]{2,1,0:T(8,128)}, u32[]{:S(2)}, u32[]{:S(2)}) %all-to-all-start.1) | async-done | bytes 524320 | tf_op jit(solution)/shard_map/all_to_all | solution.py:253
  83.1 1.1 reduce_sum.28
  84.2 2.8 %collective-permute-done.4.right = f32[4,1,128,512]{3,2,1,0:T(8,128)S(1)} collective-permute-done((f32[4,1,128,512]{3,2,1,0:T(8,128)}, f32[4,1,128,512]{3,2,1,0:T(8,128)S(1)}, u32[]{:S(2)}, u32[]{:S(2)}) %collective-permute-start.4) | collective-permute-done | bytes 1048608 | tf_op jit(solution)/shard_map/ppermute | solution.py:246
  86.9 28.4 %all_to_all.25 = f32[4,64,128]{2,1,0:T(8,128)S(1)} all-to-all(f32[4,64,128]{2,1,0:T(8,128)S(1)} %broadcast_in_dim.8), channel_id=1, replica_groups=mesh['y'=8,'zl'=2,'x'=4,'zh'=4,'c'=2] {'zh'}, dimensions={0} | all-to-all | bytes 262144 | tf_op jit(solution)/shard_map/all_to_all | solution.py:258
  115.4 15.1 %all_to_all.26 = f32[8,64,128]{2,1,0:T(8,128)S(1)} all-to-all(f32[8,64,128]{2,1,0:T(8,128)S(1)} %broadcast_in_dim.9), channel_id=1, replica_groups=mesh['y'=8,'zl'=2,'x'=4,'zh'=4,'c'=2] {'y'}, dimensions={0} | all-to-all | bytes 524288 | tf_op jit(solution)/shard_map/all_to_all | solution.py:258
  130.5 1.5 broadcast_in_dim.22
  132.0 6.2 %all-to-all-start.4 = ((f32[8,512,128]{2,1,0:T(8,128)}), f32[8,512,128]{2,1,0:T(8,128)S(1)}, u32[]{:S(2)}, u32[]{:S(2)}) async-start(f32[8,512,128]{2,1,0:T(8,128)} %broadcast_in_dim.22), calls=%async_computation.4 | async-start | bytes 4194304 | tf_op jit(solution)/shard_map/all_to_all | solution.py:258
  138.3 1.2 copy-done.2
  139.5 1.7 copy-done.16
  141.2 1.0 copy-done.18
  142.2 1.0 copy-done.20
  143.2 1.2 copy-done.22
  144.5 1.2 copy-done.24
  145.7 4.9 %shard_map.67 = f32[2,2,128,512]{3,2,1,0:T(8,128)S(1)} custom-call(f32[2,2,9,128,128]{4,3,2,1,0:T(8,128)S(1)} %copy-done.16, f32[2,2,128,512]{3,2,1,0:T(8,128)S(1)} %copy-done.2, f32[1,2,128,512]{3,2,1,0:T(8,128)S(1)} %copy-done.20, f32[1,2,128,512]{3,2,1,0:T(8,128)S(1)} %copy-done.18, f32[4,1,128,512]{3,2,1,0:T(8,128)S(1)} %copy-done.24, ...), custom_call_target="tpu_custom_call" | custom-call | flops 1811939328 | bytes 8388608 | tf_op jit(solution)/shard_map/pallas_call | solution.py:201
  150.6 0.0 copy-start.14
  150.6 1.0 copy-done.14
  151.6 12.3 %all-to-all-done.4 = f32[8,512,128]{2,1,0:T(8,128)S(1)} async-done(((f32[8,512,128]{2,1,0:T(8,128)}), f32[8,512,128]{2,1,0:T(8,128)S(1)}, u32[]{:S(2)}, u32[]{:S(2)}) %all-to-all-start.4) | async-done | bytes 2097184 | tf_op jit(solution)/shard_map/all_to_all | solution.py:258
  163.9 1.6 copy-done.10
  165.5 1.6 copy-done.12
  167.1 2.9 %shard_map.68 = f32[512,256]{1,0:T(8,128)S(1)} custom-call(bf16[2,512,1024]{2,1,0:T(8,128)(2,1)S(1)} %copy-done.10, bf16[2,512,1024]{2,1,0:T(8,128)(2,1)S(1)} %copy-done.12, f32[4,2,8,64,128]{4,3,2,1,0:T(8,128)S(1)} %bitcast.16), custom_call_target="tpu_custom_call" | custom-call | flops 1610612736 | bytes 6291456 | tf_op jit(solution)/shard_map/pallas_call | solution.py:154
  170.0 4.3 %collective-permute-start.6 = (f32[512,256]{1,0:T(8,128)S(1)}, f32[512,256]{1,0:T(8,128)S(1)}, u32[]{:S(2)}, u32[]{:S(2)}) collective-permute-start(f32[512,256]{1,0:T(8,128)S(1)} %shard_map.68), channel_id=1, source_target_pairs={{0,1},{1,0},{2,3},{3,2},{4,5},{5,4},{6,7},{7,6},{8,9},{9,8},{10,11... | collective-permute-start | bytes 1572872 | tf_op jit(solution)/shard_map/ppermute | solution.py:298
  174.4 2.9 %shard_map.69.mine = f32[512,256]{1,0:T(8,128)S(1)} custom-call(bf16[2,512,1024]{2,1,0:T(8,128)(2,1)S(1)} %copy-done.6, bf16[2,512,1024]{2,1,0:T(8,128)(2,1)S(1)} %copy-done.8, f32[4,2,8,64,128]{4,3,2,1,0:T(8,128)S(1)} %bitcast.17), custom_call_target="tpu_custom_call" | custom-call | flops 1610612736 | bytes 6291456 | tf_op jit(solution)/shard_map/pallas_call | solution.py:154
  177.3 1.9 %shard_map.70 = f32[512,512]{1,0:T(8,128)} custom-call(s32[1]{0:T(128)} %bitcast.core, f32[512,512]{1,0:T(8,128)S(1)} %bitcast.22, f32[512,256]{1,0:T(8,128)S(1)} %shard_map.69.mine, f32[512,256]{1,0:T(8,128)S(1)} %collective-permute-done.6.theirs, f32[512,512]{1,0:T(8,128)S(1)} %bitcast.20, f32[1,512]{1,0:T(1,128)S(1)} %bitcast.23), custom_call_target="tpu_custom_call" | custom-call | flops 2621440 | bytes 4194304 | tf_op jit(solution)/shard_map/pallas_call | solution.py:230
  (49 shorter events, 0.1 us)
Async XLA Ops:
  0.0 31.0 %copy-start = (f32[512,512]{1,0:T(8,128)S(1)}, f32[512,512]{1,0:T(8,128)}, u32[]{:S(2)}) copy-start(f32[512,512]{1,0:T(8,128)} %param.10) | copy-start | bytes 3145732
  0.8 15.6 %collective-permute-start.1 = (f32[3,512]{1,0:T(4,128)S(1)}, f32[3,512]{1,0:T(4,128)S(1)}, u32[]{:S(2)}, u32[]{:S(2)}) collective-permute-start(f32[3,512]{1,0:T(4,128)S(1)} %reshape.35.place), channel_id=1, source_target_pairs={{0,1},{1,0},{2,3},{3,2},{4,5},{5,4},{6,7},{7,6},{8,9},{9,8},{10,11... | collective-permute-start | bytes 18440 | tf_op jit(solution)/shard_map/ppermute | solution.py:274
  10.7 8.8 %collective-permute-start = (f32[512,256]{1,0:T(8,128)S(1)}, f32[512,256]{1,0:T(8,128)S(1)}, u32[]{:S(2)}, u32[]{:S(2)}) collective-permute-start(f32[512,256]{1,0:T(8,128)S(1)} %constant_dynamic-slice_fusion), channel_id=1, source_target_pairs={{0,1},{1,0},{2,3},{3,2},{4,5},{5,4},{6,7},{7,6},{8,9},{9,8},{10,11... | collective-permute-start | bytes 1572872 | tf_op jit(solution)/shard_map/ppermute | solution.py:275
  12.6 0.7 copy-start.25
  13.3 3.0 %copy-start.26 = (s32[3,1024]{1,0:T(4,128)S(1)}, s32[3,1024]{1,0:T(4,128)}, u32[]{:S(2)}) copy-start(s32[3,1024]{1,0:T(4,128)} %vec.5) | copy-start | bytes 36868
  16.3 3.1 %copy-start.5 = (bf16[2,512,1024]{2,1,0:T(8,128)(2,1)}, bf16[2,512,1024]{2,1,0:T(8,128)(2,1)S(1)}, u32[]{:S(2)}) copy-start(bf16[2,512,1024]{2,1,0:T(8,128)(2,1)S(1)} %get-tuple-element.22.top_a.top) | copy-start | bytes 6291460
  16.3 3.1 %copy-start.7 = (bf16[2,512,1024]{2,1,0:T(8,128)(2,1)}, bf16[2,512,1024]{2,1,0:T(8,128)(2,1)S(1)}, u32[]{:S(2)}) copy-start(bf16[2,512,1024]{2,1,0:T(8,128)(2,1)S(1)} %get-tuple-element.23.low_a.low) | copy-start | bytes 6291460
  16.4 3.1 %copy-start.3 = (f32[2,2,128,512]{3,2,1,0:T(8,128)S(1)}, f32[2,2,128,512]{3,2,1,0:T(8,128)}, u32[]{:S(2)}) copy-start(f32[2,2,128,512]{3,2,1,0:T(8,128)} %param.6) | copy-start | bytes 3145732
  19.4 5.7 %copy-start.9 = (bf16[2,512,1024]{2,1,0:T(8,128)(2,1)}, bf16[2,512,1024]{2,1,0:T(8,128)(2,1)S(1)}, u32[]{:S(2)}) copy-start(bf16[2,512,1024]{2,1,0:T(8,128)(2,1)S(1)} %get-tuple-element.25.top_b.top) | copy-start | bytes 6291460
  19.4 5.7 %copy-start.11 = (bf16[2,512,1024]{2,1,0:T(8,128)(2,1)}, bf16[2,512,1024]{2,1,0:T(8,128)(2,1)S(1)}, u32[]{:S(2)}) copy-start(bf16[2,512,1024]{2,1,0:T(8,128)(2,1)S(1)} %get-tuple-element.26.low_b.low) | copy-start | bytes 6291460
  25.1 1.4 copy-start.13
  26.5 37.6 %all-to-all-start = ((f32[4,1024,128]{2,1,0:T(8,128)}), f32[4,1024,128]{2,1,0:T(8,128)}, u32[]{:S(2)}, u32[]{:S(2)}) async-start(f32[4,1024,128]{2,1,0:T(8,128)} %bitcast.21), calls=%async_computation | async-start | bytes 4194304 | tf_op jit(solution)/shard_map/all_to_all | solution.py:253
  32.0 26.4 %copy-start.1 = (f32[2,2,128,512]{3,2,1,0:T(8,128)}, f32[2,2,128,512]{3,2,1,0:T(8,128)S(1)}, u32[]{:S(2)}) copy-start(f32[2,2,128,512]{3,2,1,0:T(8,128)S(1)} %fusion.own) | copy-start | bytes 3145732
  32.1 26.1 %collective-permute-start.3 = (f32[1,2,128,512]{3,2,1,0:T(8,128)S(1)}, f32[1,2,128,512]{3,2,1,0:T(8,128)S(1)}, u32[]{:S(2)}, u32[]{:S(2)}) collective-permute-start(f32[1,2,128,512]{3,2,1,0:T(8,128)S(1)} %get-tuple-element.41), channel_id=1, source_target_pairs={{32,0},{64,32},{96,64},{128,96},{160,128},{192,160},{224,192},{256... | collective-permute-start | bytes 1572872 | tf_op jit(solution)/shard_map/ppermute | solution.py:246
  34.0 24.2 %collective-permute-start.2 = (f32[1,2,128,512]{3,2,1,0:T(8,128)S(1)}, f32[1,2,128,512]{3,2,1,0:T(8,128)S(1)}, u32[]{:S(2)}, u32[]{:S(2)}) collective-permute-start(f32[1,2,128,512]{3,2,1,0:T(8,128)S(1)} %get-tuple-element.42), channel_id=1, source_target_pairs={{0,32},{32,64},{64,96},{96,128},{128,160},{160,192},{192,224},{224... | collective-permute-start | bytes 1572872 | tf_op jit(solution)/shard_map/ppermute | solution.py:245
  58.2 0.8 copy-start.17
  58.2 1.0 copy-start.19
  60.8 26.1 %collective-permute-start.4 = (f32[4,1,128,512]{3,2,1,0:T(8,128)}, f32[4,1,128,512]{3,2,1,0:T(8,128)S(1)}, u32[]{:S(2)}, u32[]{:S(2)}) collective-permute-start(f32[4,1,128,512]{3,2,1,0:T(8,128)} %get-tuple-element.40), channel_id=1, source_target_pairs={{1,0},{2,1},{3,2},{4,3},{5,4},{6,5},{7,6},{8,7},{9,8},{10,9},{11,1... | collective-permute-start | bytes 3145736 | tf_op jit(solution)/shard_map/ppermute | solution.py:246
  66.6 16.5 %all-to-all-start.1 = ((f32[16,64,128]{2,1,0:T(8,128)}), f32[16,64,128]{2,1,0:T(8,128)}, u32[]{:S(2)}, u32[]{:S(2)}) async-start(f32[16,64,128]{2,1,0:T(8,128)} %bitcast.6), calls=%async_computation.1 | async-start | bytes 1048576 | tf_op jit(solution)/shard_map/all_to_all | solution.py:253
  70.9 44.5 %collective-permute-start.5 = (f32[4,1,128,512]{3,2,1,0:T(8,128)}, f32[4,1,128,512]{3,2,1,0:T(8,128)S(1)}, u32[]{:S(2)}, u32[]{:S(2)}) collective-permute-start(f32[4,1,128,512]{3,2,1,0:T(8,128)} %get-tuple-element.39), channel_id=1, source_target_pairs={{0,1},{1,2},{2,3},{3,4},{4,5},{5,6},{6,7},{7,8},{8,9},{9,10},{10,1... | collective-permute-start | bytes 3145736 | tf_op jit(solution)/shard_map/ppermute | solution.py:245
  86.9 45.1 %copy-start.21 = (f32[4,1,128,512]{3,2,1,0:T(8,128)}, f32[4,1,128,512]{3,2,1,0:T(8,128)S(1)}, u32[]{:S(2)}) copy-start(f32[4,1,128,512]{3,2,1,0:T(8,128)S(1)} %collective-permute-done.4.right) | copy-start | bytes 3145732
  115.4 16.7 %copy-start.23 = (f32[4,1,128,512]{3,2,1,0:T(8,128)}, f32[4,1,128,512]{3,2,1,0:T(8,128)S(1)}, u32[]{:S(2)}) copy-start(f32[4,1,128,512]{3,2,1,0:T(8,128)S(1)} %collective-permute-done.5.left) | copy-start | bytes 3145732
  132.0 31.8 %all-to-all-start.4 = ((f32[8,512,128]{2,1,0:T(8,128)}), f32[8,512,128]{2,1,0:T(8,128)S(1)}, u32[]{:S(2)}, u32[]{:S(2)}) async-start(f32[8,512,128]{2,1,0:T(8,128)} %broadcast_in_dim.22), calls=%async_computation.4 | async-start | bytes 4194304 | tf_op jit(solution)/shard_map/all_to_all | solution.py:258
  138.3 1.2 copy-start.2
  139.5 1.7 copy-start.16
  141.2 1.0 copy-start.18
  142.2 1.0 copy-start.20
  143.2 1.2 copy-start.22
  144.5 1.2 copy-start.24
  150.6 1.0 copy-start.14
  163.9 1.6 copy-start.10
  165.5 1.6 copy-start.12
  167.1 7.3 %copy-start.6 = (bf16[2,512,1024]{2,1,0:T(8,128)(2,1)S(1)}, bf16[2,512,1024]{2,1,0:T(8,128)(2,1)}, u32[]{:S(2)}) copy-start(bf16[2,512,1024]{2,1,0:T(8,128)(2,1)} %copy-done.5) | copy-start | bytes 6291460
  167.1 7.3 %copy-start.8 = (bf16[2,512,1024]{2,1,0:T(8,128)(2,1)S(1)}, bf16[2,512,1024]{2,1,0:T(8,128)(2,1)}, u32[]{:S(2)}) copy-start(bf16[2,512,1024]{2,1,0:T(8,128)(2,1)} %copy-done.7) | copy-start | bytes 6291460
  170.0 7.3 %copy-start.4 = (f32[2,2,128,512]{3,2,1,0:T(8,128)S(1)}, f32[2,2,128,512]{3,2,1,0:T(8,128)}, u32[]{:S(2)}) copy-start(f32[2,2,128,512]{3,2,1,0:T(8,128)} %param.6) | copy-start | bytes 3145732
  170.0 7.3 %copy-start.15 = (f32[2,2,128,512]{3,2,1,0:T(8,128)S(1)}, f32[2,2,128,512]{3,2,1,0:T(8,128)}, u32[]{:S(2)}) copy-start(f32[2,2,128,512]{3,2,1,0:T(8,128)} %copy-done.14) | copy-start | bytes 3145732
  170.0 7.3 %copy-start.27 = (f32[512]{0:T(512)S(1)}, f32[512]{0:T(512)}, u32[]{:S(2)}) copy-start(f32[512]{0:T(512)} %param.11) | copy-start | bytes 6148
  170.0 7.3 %collective-permute-start.6 = (f32[512,256]{1,0:T(8,128)S(1)}, f32[512,256]{1,0:T(8,128)S(1)}, u32[]{:S(2)}, u32[]{:S(2)}) collective-permute-start(f32[512,256]{1,0:T(8,128)S(1)} %shard_map.68), channel_id=1, source_target_pairs={{0,1},{1,0},{2,3},{3,2},{4,5},{5,4},{6,7},{7,6},{8,9},{9,8},{10,11... | collective-permute-start | bytes 1572872 | tf_op jit(solution)/shard_map/ppermute | solution.py:298
